TPU v7x, 512 devices: a whole 4x8x8 slice. The times are simulated.
512 devices in a mesh: gx: 16 (over y, core), gy: 32 (over z, x).
Axes of the slice: x: 4, y: 8, z: 8, core: 2. Of those that a mesh axis runs over, the one named last changes fastest.
Arguments:
- species: float32 [9, 128, 256, 128], P(None, 'gx', 'gy'), may hold values from -4 to 4
- flow_fields: float32 [5, 128, 256, 128], P(None, 'gx', 'gy'), may hold values from -5 to 5
- classes: int32 [128, 256], P('gx', 'gy'), may hold values from 1 to 4, as said below
- diffusivity: float32 [14], replicated, may hold values from 0.2 to 0.6
- left_form: float32 [19, 9], replicated, may hold values from -2 to 2
- right_form: float32 [19, 9], replicated, may hold values from -2 to 2
- stoich: float32 [19, 9], replicated, may hold values from -1.25 to 1.25
- heat_release: float32 [19], replicated, may hold values from -3 to 3
- arrhenius_prefactor: float32 [19], replicated, may hold values from 0.4 to 4
- arrhenius_energy: float32 [19], replicated, may hold values from 0.5 to 2
- newton_matrix: float32 [10, 10], replicated, may hold values from -0.5 to 1.5
Outputs:
- species_out: float32 [9, 128, 256, 128], P(None, 'gx', 'gy')
- flow_out: float32 [5, 128, 256, 128], P(None, 'gx', 'gy')
Inputs may be any that keep to these rules, and one draw needn't show every extreme that they name: `classes`: 1 where a column takes one substep, 2 to 4 otherwise. Among the columns of one device at most 32 have a class over 1, and some device has exactly that many; two devices with the same gx index whose gy indices differ by half the gy axis hold at most 40 such columns together, and some pair has exactly that many.
All inputs are finite; a program needn't handle non-finite values.
Results may differ from a plain program's by a relative error of at most 0.0003.
Values sent between devices are 32-bit elements; how exact they have to be, the bound alone decides.
No kernel may reach another device: no remote copies, remote signals or barrier semaphores. Data moves between devices by JAX's collectives and lax.ppermute only.
A program may use at most 64 MiB of HBM per device.

v0:
```python
import functools

import jax
import jax.numpy as jnp
import numpy as np
from jax import lax
from jax.experimental import pallas as pl
from jax.experimental.pallas import tpu as pltpu
from jax.sharding import Mesh
from jax.sharding import PartitionSpec as P

GX = ("y", "c")
GY = ("z", "x")
MODES = ("y", "c", "z")

NSPEC = 9
NREAC = 19
NS = NSPEC + 1
NF = 14
NX = 128
NY = 256
NZ = 128
CX = 8
CY = 8
COLS = CX * CY
CAP = COLS // 2
CHUNK = 16
DT = 0.25
PRECISE = lax.Precision.HIGHEST
F32 = jnp.float32
VMEM = pl.BlockSpec(memory_space=pltpu.VMEM)
SMEM = pl.BlockSpec(memory_space=pltpu.SMEM)
LIMIT = 32 * 1024 * 1024


def basis(n):
    j = np.arange(n)
    h = n // 2
    f = np.zeros((n, n))
    k = np.zeros(n)
    f[0] = 1.0 / np.sqrt(n)
    f[h] = (-1.0) ** j / np.sqrt(n)
    for m in range(1, h):
        f[m] = np.sqrt(2.0 / n) * np.cos(2 * np.pi * (m * j % n) / n)
        f[h + m] = np.sqrt(2.0 / n) * np.sin(2 * np.pi * (m * j % n) / n)
        k[m] = k[h + m] = 2 * np.pi * m / n
    d = np.zeros((n, n))
    for m in range(1, h):
        d[m] = k[m] * f[h + m]
        d[h + m] = -k[m] * f[m]
    return f, d, k


def dot(a, b, dims=((1,), (0,))):
    return lax.dot_general(a, b, (dims, ((), ())), precision=PRECISE, preferred_element_type=F32)


def rates(z, left, right, msa, energy):
    acc = None
    for j in range(NREAC):
        a = left[j, 0] * z[0]
        b = right[j, 0] * z[0]
        for s in range(1, NSPEC):
            a = a + left[j, s] * z[s]
            b = b + right[j, s] * z[s]
        r = jnp.tanh(a) * jnp.tanh(b)
        r = r + r * jnp.tanh(energy[j] * z[NSPEC])
        term = [msa[i, j] * r for i in range(NS)]
        acc = term if acc is None else [p + q for p, q in zip(acc, term)]
    return acc


def substep(load, store, h, left, right, msa, energy, newton):
    z0 = [load(i) for i in range(NS)]
    acc = rates(z0, left, right, msa, energy)
    z = tuple(z0[i] + h * acc[i] for i in range(NS))

    def again(_, z):
        acc = rates(z, left, right, msa, energy)
        d = [z[i] - load(i) for i in range(NS)]
        out = []
        for i in range(NS):
            m = newton[i, 0] * d[0]
            for j in range(1, NS):
                m = m + newton[i, j] * d[j]
            out.append(z[i] + (h * acc[i] - m))
        return tuple(out)

    z = lax.fori_loop(0, 2, again, z)
    for i in range(NS):
        store(i, z[i])


def react_kernel(
    species,
    flow,
    xlo,
    xhi,
    ylo,
    yhi,
    classes,
    diff,
    left,
    right,
    msa,
    energy,
    newton,
    fz,
    dz,
    species_out,
    flow_mid,
    spectra,
    state,
    temp0,
    hcol,
    buf,
):
    ysub = lax.broadcasted_iota(jnp.int32, (CY, NZ), 0)
    half = [0.5 * flow[c] for c in (1, 2, 3)]

    def transport(f, field, coef):
        ahead_x = jnp.concatenate([field[1:], xhi[f][None]], axis=0)
        behind_x = jnp.concatenate([xlo[f][None], field[:-1]], axis=0)
        up = pltpu.roll(field, CY - 1, 1)
        down = pltpu.roll(field, 1, 1)
        ahead_y = jnp.stack([jnp.where(ysub == CY - 1, yhi[f, x : x + 1, :], up[x]) for x in range(CX)])
        behind_y = jnp.stack([jnp.where(ysub == 0, ylo[f, x : x + 1, :], down[x]) for x in range(CX)])
        ahead_z = pltpu.roll(field, NZ - 1, 2)
        behind_z = pltpu.roll(field, 1, 2)
        lap = (ahead_x + behind_x) + (ahead_y + behind_y) + (ahead_z + behind_z) - 6.0 * field
        adv = (
            half[0] * (ahead_x - behind_x)
            + half[1] * (ahead_y - behind_y)
            + half[2] * (ahead_z - behind_z)
        )
        return field + DT * (coef * lap - adv)

    for f in range(NF):
        field = species[f] if f < NSPEC else flow[f - NSPEC]
        moved = transport(f, field, diff[f])
        if f < NSPEC:
            state[:, f * NZ : (f + 1) * NZ] = moved.reshape(COLS, NZ)
        elif f == NF - 1:
            state[:, NSPEC * NZ :] = moved.reshape(COLS, NZ)
            temp0[...] = moved.reshape(COLS, NZ)
        else:
            flow_mid[f - NSPEC] = moved

    cls = classes[...].astype(F32)
    col = lax.broadcasted_iota(jnp.int32, (COLS, CX), 0)
    lane = lax.broadcasted_iota(jnp.int32, (COLS, CX), 1)
    pick_x = (col // CY == lane).astype(F32)
    pick_y = (col % CY == lane).astype(F32)
    class_col = jnp.sum(dot(pick_x, cls) * pick_y, axis=1, keepdims=True)
    rows = dot(cls, pick_y, ((1,), (1,)))
    row_x = lax.broadcasted_iota(jnp.int32, (CX, COLS), 0)
    row_c = lax.broadcasted_iota(jnp.int32, (CX, COLS), 1)
    class_row = jnp.sum(jnp.where(row_c // CY == row_x, rows, 0.0), axis=0, keepdims=True)
    hcol[...] = jnp.broadcast_to(DT / class_col, (COLS, NZ))
    ii = lax.broadcasted_iota(jnp.int32, (COLS, COLS), 0).astype(F32)
    jj = lax.broadcasted_iota(jnp.int32, (COLS, COLS), 1).astype(F32)
    key_col = class_col * COLS - ii
    key_row = class_row * COLS - jj
    rank_row = jnp.sum((key_col > key_row).astype(F32), axis=0, keepdims=True)
    rank_col = jnp.sum((key_row > key_col).astype(F32), axis=1, keepdims=True)
    place = lax.broadcasted_iota(jnp.int32, (CAP, COLS), 0).astype(F32)
    gather = (place == rank_row).astype(F32)
    place_t = lax.broadcasted_iota(jnp.int32, (COLS, CAP), 1).astype(F32)
    scatter = (place_t == rank_col).astype(F32)
    counts = [jnp.sum((class_row > float(s)).astype(jnp.int32)) for s in (1, 2, 3)]

    def first(g, _):
        rows16 = pl.ds(pl.multiple_of(g * CHUNK, CHUNK), CHUNK)

        def load(i):
            return state[rows16, i * NZ : (i + 1) * NZ]

        def store(i, value):
            state[rows16, i * NZ : (i + 1) * NZ] = value

        substep(load, store, hcol[rows16, :], left, right, msa, energy, newton)
        return 0

    lax.fori_loop(0, COLS // CHUNK, first, 0)

    buf[...] = dot(gather, state[...])
    class_sorted = jnp.sum(gather * class_row, axis=1, keepdims=True)
    hcol[0:CAP, :] = jnp.broadcast_to(DT / class_sorted, (CAP, NZ))

    def extra(g, _):
        start = g * CHUNK
        rows16 = pl.ds(pl.multiple_of(start, CHUNK), CHUNK)
        more = sum((c > start).astype(jnp.int32) for c in counts)

        def again(s, _):
            h = hcol[rows16, :]
            active = h < DT / (s + 1.5)

            def load(i):
                return buf[rows16, i * NZ : (i + 1) * NZ]

            def store(i, value):
                buf[rows16, i * NZ : (i + 1) * NZ] = jnp.where(active, value, load(i))

            substep(load, store, h, left, right, msa, energy, newton)
            return 0

        lax.fori_loop(0, more, again, 0)
        return 0

    lax.fori_loop(0, CAP // CHUNK, extra, 0)

    spread = dot(scatter, buf[...])
    chosen = rank_col < CAP - 0.5
    final = [
        jnp.where(chosen, spread[:, i * NZ : (i + 1) * NZ], state[:, i * NZ : (i + 1) * NZ])
        for i in range(NS)
    ]
    for i in range(NSPEC):
        species_out[i] = final[i].reshape(CX, CY, NZ)
    flow_mid[4] = final[NSPEC].reshape(CX, CY, NZ)
    source = (final[NSPEC] - temp0[...]) * (1.0 / DT)
    nt = ((1,), (1,))
    horizontal = flow_mid[1:3].reshape(2 * COLS, NZ)
    spectra[:, 0, :] = dot(fz[...], horizontal, nt)
    vertical = flow_mid[3].reshape(COLS, NZ)
    third = dot(dz[...], vertical, nt) - dot(fz[...], source, nt)
    spectra[:, 1, :] = jnp.concatenate([third, jnp.zeros_like(third)], axis=1)


def swap_blocks(v):
    rows, lanes = v.shape
    r = lax.broadcasted_iota(jnp.int32, v.shape, 0)
    k = lax.broadcasted_iota(jnp.int32, v.shape, 1) // 8
    for b in (1, 2, 4):
        low_r, low_k = (r & b) == 0, (k & b) == 0
        from_above = pltpu.roll(pltpu.roll(v, b, 0), lanes - 8 * b, 1)
        from_below = pltpu.roll(pltpu.roll(v, rows - b, 0), 8 * b, 1)
        v = jnp.where(low_r == low_k, v, jnp.where(low_r, from_below, from_above))
    return v


def stream_kernel(got, fx, dx, out):
    a = swap_blocks(got[:, 0, :])
    w = swap_blocks(got[:, 1, :])
    u = a[:, :COLS]
    h = dot(dx[...], u) + dot(fx[...], w[:, :COLS])
    y = dot(fx[...], a[:, COLS:])
    both = jnp.concatenate([h, y], axis=1)
    for i in range(4):
        out[i] = both


def solve_kernel(place, kz2, got, forth, back, kx2, ky2, fxt, dxt, out):
    full = dot(got[0], forth[0])
    for i in range(1, 4):
        full = full + dot(got[i], forth[i])
    k2 = kx2[...] + ky2[...] + kz2[place[0]]
    q = full / jnp.where(k2 > 0, k2, 1.0)
    lines = dot(q, back[place[1]])
    first = dot(fxt[...], lines)
    second = dot(dxt[...], lines)
    out[:, 0, :] = swap_blocks(first)
    out[:, 1, :] = swap_blocks(second)


def finish_kernel(got, mid, fz, dz, out):
    tn = ((0,), (0,))
    first = got[:, 0, :]
    second = got[:, 1, :]
    a = dot(second, fz[...], tn)[:COLS]
    b = dot(first[:, COLS:], fz[...], tn)
    c = dot(first[:, :COLS], dz[...], tn)
    out[0] = mid[0]
    out[1] = mid[1] + a.reshape(CX, CY, NZ)
    out[2] = mid[2] + b.reshape(CX, CY, NZ)
    out[3] = mid[3] - c.reshape(CX, CY, NZ)
    out[4] = mid[4]


def call(kernel, out_shapes, specs, scratch=(), flops=0, nbytes=0):
    out = [jax.ShapeDtypeStruct(s, F32) for s in out_shapes]
    return pl.pallas_call(
        kernel,
        out_shape=out if len(out) > 1 else out[0],
        in_specs=specs,
        out_specs=[VMEM] * len(out) if len(out) > 1 else VMEM,
        scratch_shapes=list(scratch),
        compiler_params=pltpu.CompilerParams(vmem_limit_bytes=LIMIT),
    )


def ring(axes, n, step):
    return functools.partial(
        lax.ppermute, axis_name=axes, perm=[(i, (i + step) % n) for i in range(n)]
    )


def shards(
    species,
    flow,
    classes,
    diffusivity,
    left,
    right,
    stoich,
    heat,
    prefactor,
    energy,
    newton,
):
    fields = lambda *at: jnp.concatenate([species[at], flow[at]], axis=0)
    every = slice(None)
    n_gx, n_gy = NX // CX, NY // CY
    ylo = ring(GY, n_gy, 1)(fields(every, every, CY - 1))
    yhi = ring(GY, n_gy, -1)(fields(every, every, 0))
    xlo = ring(GX, n_gx, 1)(fields(every, CX - 1))
    xhi = ring(GX, n_gx, -1)(fields(every, 0))

    both = jnp.concatenate([stoich, heat[:, None]], axis=1)
    msa = jnp.einsum("ij,rj->ir", newton, both, precision=PRECISE) * (0.5 * prefactor)[None, :]

    fz, dz, kz = basis(NZ)
    fy, dy, ky = basis(NY)
    fx, dx, kx = basis(NX)
    f32 = lambda v: np.ascontiguousarray(v, np.float32)
    y_of = ((np.arange(8)[None, :, None] * 4 + np.arange(4)[:, None, None]) * CY + np.arange(CY)).reshape(4, COLS)
    forth = np.stack([np.concatenate([fy[:, y].T, dy[:, y].T], axis=0) for y in y_of])
    back = np.stack([np.concatenate([fy[:, y], -dy[:, y]], axis=1) for y in y_of])

    species_out, mid, spectra = call(
        react_kernel,
        [(NSPEC, CX, CY, NZ), (5, CX, CY, NZ), (NZ, 2, 2 * COLS)],
        [VMEM] * 7 + [SMEM] * 6 + [VMEM] * 2,
        [
            pltpu.VMEM((COLS, NS * NZ), F32),
            pltpu.VMEM((COLS, NZ), F32),
            pltpu.VMEM((COLS, NZ), F32),
            pltpu.VMEM((CAP, NS * NZ), F32),
        ],
    )(
        species,
        flow,
        xlo,
        xhi,
        ylo,
        yhi,
        classes,
        diffusivity,
        left,
        right,
        msa,
        0.5 * energy,
        newton,
        f32(fz),
        f32(dz),
    )
    got = lax.all_to_all(spectra, MODES, 0, 0, tiled=True)
    lines = call(stream_kernel, [(4, NX, 2 * COLS)], [VMEM] * 3)(got, f32(fx), f32(dx))
    lines = lax.all_to_all(lines, "x", 0, 0, tiled=True)
    place = jnp.stack([lax.axis_index(MODES), lax.axis_index("x")]).astype(jnp.int32)
    grads = call(solve_kernel, [(NX, 2, 2 * COLS)], [SMEM] * 2 + [VMEM] * 7)(
        place,
        f32(kz * kz),
        lines,
        f32(forth),
        f32(back),
        f32(kx * kx)[:, None],
        f32(ky * ky)[None, :],
        f32(fx.T),
        f32(-dx.T),
    )
    got = lax.all_to_all(grads, MODES, 0, 0, tiled=True)
    flow_out = call(finish_kernel, [(5, CX, CY, NZ)], [VMEM] * 4)(got, mid, f32(fz), f32(dz))
    return (species_out, flow_out)


def solution(mesh):
    finer = Mesh(mesh.devices.reshape(8, 2, 8, 4), GX + GY)
    return jax.shard_map(
        shards,
        mesh=finer,
        in_specs=(P(None, GX, GY, None), P(None, GX, GY, None), P(GX, GY)) + (P(),) * 8,
        out_specs=(P(None, GX, GY, None), P(None, GX, GY, None)),
        check_vma=False,
    )
```

profile of v0, /device:TPU:1, one launch (start us, length us, event | category | flops | bytes accessed | tf_op | source)
XLA Modules:
  0.0 95.8 jit_solution(13208473333401449688)
XLA Ops:
  0.6 0.0 copy-start
  0.6 0.8 slice_bitcast_fusion.2
  1.4 0.8 slice_bitcast_fusion
  2.3 2.7 %collective-permute-start = (f32[14,8,128]{2,1,0:T(8,128)S(1)}, f32[14,8,128]{2,1,0:T(8,128)S(1)}, u32[]{:S(2)}, u32[]{:S(2)}) collective-permute-start(f32[14,8,128]{2,1,0:T(8,128)S(1)} %pad_maximum_fusion), channel_id=1, source_target_pairs={{0,32},{32,64},{64,96},{96,128},{128,160},{160,192},{192,224},{224... | collective-permute-start | bytes 172040 | tf_op jit(solution)/shard_map/ppermute | solution.py:317
  5.0 4.2 %collective-permute-start.1 = (f32[14,8,128]{2,1,0:T(8,128)S(1)}, f32[14,8,128]{2,1,0:T(8,128)S(1)}, u32[]{:S(2)}, u32[]{:S(2)}) collective-permute-start(f32[14,8,128]{2,1,0:T(8,128)S(1)} %pad_maximum_fusion.1), channel_id=1, source_target_pairs={{0,480},{32,0},{64,32},{96,64},{128,96},{160,128},{192,160},{224,1... | collective-permute-start | bytes 172040 | tf_op jit(solution)/shard_map/ppermute | solution.py:318
  9.2 0.0 copy-done.5
  9.2 0.0 copy-done
  9.3 0.0 copy-start.18
  9.3 0.0 copy-start.9
  9.3 0.0 copy-start.14
  9.3 0.0 copy-start.17
  9.4 1.9 %collective-permute-start.2 = (f32[14,8,128]{2,1,0:T(8,128)S(1)}, f32[14,8,128]{2,1,0:T(8,128)S(1)}, u32[]{:S(2)}, u32[]{:S(2)}) collective-permute-start(f32[14,8,128]{2,1,0:T(8,128)S(1)} %pad_maximum_fusion.2), channel_id=1, source_target_pairs={{0,1},{1,2},{2,3},{3,4},{4,5},{5,6},{6,7},{7,8},{8,9},{9,10},{10,1... | collective-permute-start | bytes 172040 | tf_op jit(solution)/shard_map/ppermute | solution.py:315
  11.3 0.0 copy-start.1
  11.3 0.0 copy-start.2
  11.3 8.8 %collective-permute-start.3 = (f32[14,8,128]{2,1,0:T(8,128)S(1)}, f32[14,8,128]{2,1,0:T(8,128)S(1)}, u32[]{:S(2)}, u32[]{:S(2)}) collective-permute-start(f32[14,8,128]{2,1,0:T(8,128)S(1)} %pad_maximum_fusion.3), channel_id=1, source_target_pairs={{0,31},{1,0},{2,1},{3,2},{4,3},{5,4},{6,5},{7,6},{8,7},{9,8},{10,9... | collective-permute-start | bytes 172040 | tf_op jit(solution)/shard_map/ppermute | solution.py:316
  20.1 0.0 copy-done.18
  20.1 0.0 copy-done.9
  20.2 0.0 copy-done.14
  20.2 0.0 copy-done.17
  20.2 0.0 copy-start.19
  20.2 0.0 copy-start.15
  20.2 0.1 fusion.msa
  20.3 0.5 copy-done.19
  20.8 0.1 copy-done.15
  20.9 0.1 copy.34.left
  21.0 0.6 copy-done.16
  21.6 0.1 copy.35.right
  21.7 0.0 collective-permute-done.xlo
  21.7 0.0 collective-permute-done.1.xhi
  21.7 0.0 collective-permute-done.2.ylo
  21.7 0.0 collective-permute-done.3.yhi
  21.7 0.0 copy-done.1
  21.7 0.0 copy-done.2
  21.7 0.5 copy-done.10
  22.3 0.0 copy-done.13
  22.3 12.5 %shard_map.239 = (f32[9,8,8,128]{3,2,1,0:T(8,128)}, f32[5,8,8,128]{3,2,1,0:T(8,128)S(1)}, f32[128,2,128]{2,1,0:T(2,128)S(1)}) custom-call(f32[9,8,8,128]{3,2,1,0:T(8,128)S(1)} %copy-done, f32[5,8,8,128]{3,2,1,0:T(8,128)S(1)} %copy-done.5, f32[14,8,128]{2,1,0:T(8,128)S(1)} %collective-permute-done.xlo, f32[14,8,128]{2,1,0:T(8,128)S(1)} %collective-permute-done.1.xhi, ...), custom_call_target="tpu_custom_call" | custom-call | tf_op jit(solution)/shard_map/pallas_call | solution.py:331
  34.8 28.2 %all_to_all.15.got = f32[128,2,128]{2,1,0:T(2,128)S(1)} all-to-all(f32[128,2,128]{2,1,0:T(2,128)S(1)} %get-tuple-element.6), channel_id=1, replica_groups=mesh['y'=8,'c'=2,'z'=8,'x'=4] {'y','c','z'}, dimensions={0} | all-to-all | bytes 262144 | tf_op jit(solution)/shard_map/all_to_all | solution.py:358
  63.0 1.4 %shard_map.240 = f32[4,128,128]{2,1,0:T(8,128)} custom-call(f32[128,2,128]{2,1,0:T(2,128)S(1)} %all_to_all.15.got, f32[128,128]{1,0:T(8,128)S(1)} %copy-done.2, f32[128,128]{1,0:T(8,128)S(1)} %copy-done.1), custom_call_target="tpu_custom_call" | custom-call | tf_op jit(solution)/shard_map/pallas_call | solution.py:359
  64.4 3.4 %all-to-all-start.1 = ((f32[4,128,128]{2,1,0:T(8,128)}), f32[4,128,128]{2,1,0:T(8,128)S(1)}, u32[]{:S(2)}, u32[]{:S(2)}) async-start(f32[4,128,128]{2,1,0:T(8,128)} %shard_map.240), calls=%async_computation.1 | async-start | bytes 524288 | tf_op jit(solution)/shard_map/all_to_all | solution.py:360
  67.8 0.0 copy-start.11
  67.8 0.0 copy-start.12
  67.8 0.1 pad_add_fusion.place
  67.9 6.0 %all-to-all-done.1.got = f32[4,128,128]{2,1,0:T(8,128)S(1)} async-done(((f32[4,128,128]{2,1,0:T(8,128)}), f32[4,128,128]{2,1,0:T(8,128)S(1)}, u32[]{:S(2)}, u32[]{:S(2)}) %all-to-all-start.1) | async-done | bytes 262176 | tf_op jit(solution)/shard_map/all_to_all | solution.py:360
  73.9 0.0 copy-done.6
  73.9 0.0 copy-done.7
  74.0 2.2 %shard_map.241 = f32[128,2,128]{2,1,0:T(2,128)S(1)} custom-call(s32[2]{0:T(128)S(1)} %pad_add_fusion.place, f32[128]{0:T(128)S(1)} %copy-done.12, f32[4,128,128]{2,1,0:T(8,128)S(1)} %all-to-all-done.1.got, f32[4,128,256]{2,1,0:T(8,128)S(1)} %copy-done.4, f32[4,256,128]{2,1,0:T(8,128)S(1)} %copy-done.3, f32[128,1]{1,0:T(8,128)S(1)} %copy-done.8, ...), custom_call_target="tpu_custom_call" | custom-call | tf_op jit(solution)/shard_map/pallas_call | solution.py:362
  76.2 18.6 %all_to_all.16.got = f32[128,2,128]{2,1,0:T(2,128)S(1)} all-to-all(f32[128,2,128]{2,1,0:T(2,128)S(1)} %shard_map.241), channel_id=1, replica_groups=mesh['y'=8,'c'=2,'z'=8,'x'=4] {'y','c','z'}, dimensions={0} | all-to-all | bytes 262144 | tf_op jit(solution)/shard_map/all_to_all | solution.py:373
  94.8 1.1 %shard_map.242 = f32[5,8,8,128]{3,2,1,0:T(8,128)} custom-call(f32[128,2,128]{2,1,0:T(2,128)S(1)} %all_to_all.16.got, f32[5,8,8,128]{3,2,1,0:T(8,128)S(1)} %get-tuple-element.7.mid, f32[128,128]{1,0:T(8,128)S(1)} %copy-done.2, f32[128,128]{1,0:T(8,128)S(1)} %copy-done.1), custom_call_target="tpu_custom_call" | custom-call | tf_op jit(solution)/shard_map/pallas_call | solution.py:374
  (22 shorter events, 0.1 us)
Async XLA Ops:
  0.6 8.6 %copy-start = (f32[9,8,8,128]{3,2,1,0:T(8,128)S(1)}, f32[9,8,8,128]{3,2,1,0:T(8,128)}, u32[]{:S(2)}) copy-start(f32[9,8,8,128]{3,2,1,0:T(8,128)} %species.1) | copy-start | bytes 884740
  1.4 7.8 %copy-start.5 = (f32[5,8,8,128]{3,2,1,0:T(8,128)S(1)}, f32[5,8,8,128]{3,2,1,0:T(8,128)}, u32[]{:S(2)}) copy-start(f32[5,8,8,128]{3,2,1,0:T(8,128)} %flow.1) | copy-start | bytes 491524
  2.3 19.4 %collective-permute-start = (f32[14,8,128]{2,1,0:T(8,128)S(1)}, f32[14,8,128]{2,1,0:T(8,128)S(1)}, u32[]{:S(2)}, u32[]{:S(2)}) collective-permute-start(f32[14,8,128]{2,1,0:T(8,128)S(1)} %pad_maximum_fusion), channel_id=1, source_target_pairs={{0,32},{32,64},{64,96},{96,128},{128,160},{160,192},{192,224},{224... | collective-permute-start | bytes 172040 | tf_op jit(solution)/shard_map/ppermute | solution.py:317
  5.0 16.7 %collective-permute-start.1 = (f32[14,8,128]{2,1,0:T(8,128)S(1)}, f32[14,8,128]{2,1,0:T(8,128)S(1)}, u32[]{:S(2)}, u32[]{:S(2)}) collective-permute-start(f32[14,8,128]{2,1,0:T(8,128)S(1)} %pad_maximum_fusion.1), channel_id=1, source_target_pairs={{0,480},{32,0},{64,32},{96,64},{128,96},{160,128},{192,160},{224,1... | collective-permute-start | bytes 172040 | tf_op jit(solution)/shard_map/ppermute | solution.py:318
  9.3 10.8 %copy-start.18 = (f32[19]{0:T(128)S(1)}, f32[19]{0:T(128)}, u32[]{:S(2)}) copy-start(f32[19]{0:T(128)} %param.32) | copy-start | bytes 232
  9.3 10.8 %copy-start.9 = (f32[10,10]{1,0:T(8,128)S(1)}, f32[10,10]{1,0:T(8,128)}, u32[]{:S(2)}) copy-start(f32[10,10]{1,0:T(8,128)} %newton.1) | copy-start | bytes 1204
  9.3 10.8 %copy-start.14 = (f32[19,9]{0,1:T(8,128)S(1)}, f32[19,9]{0,1:T(8,128)}, u32[]{:S(2)}) copy-start(f32[19,9]{0,1:T(8,128)} %param.30) | copy-start | bytes 2056
  9.3 10.8 %copy-start.17 = (f32[19]{0:T(128)S(1)}, f32[19]{0:T(128)}, u32[]{:S(2)}) copy-start(f32[19]{0:T(128)} %param.31) | copy-start | bytes 232
  9.4 12.3 %collective-permute-start.2 = (f32[14,8,128]{2,1,0:T(8,128)S(1)}, f32[14,8,128]{2,1,0:T(8,128)S(1)}, u32[]{:S(2)}, u32[]{:S(2)}) collective-permute-start(f32[14,8,128]{2,1,0:T(8,128)S(1)} %pad_maximum_fusion.2), channel_id=1, source_target_pairs={{0,1},{1,2},{2,3},{3,4},{4,5},{5,6},{6,7},{7,8},{8,9},{9,10},{10,1... | collective-permute-start | bytes 172040 | tf_op jit(solution)/shard_map/ppermute | solution.py:315
  11.3 10.4 %copy-start.1 = (f32[128,128]{1,0:T(8,128)S(1)}, f32[128,128]{1,0:T(8,128)}, u32[]{:S(2)}) copy-start(f32[128,128]{1,0:T(8,128)} %constant.44.clone.dz.dx) | copy-start | bytes 196612
  11.3 10.4 %copy-start.2 = (f32[128,128]{1,0:T(8,128)S(1)}, f32[128,128]{1,0:T(8,128)}, u32[]{:S(2)}) copy-start(f32[128,128]{1,0:T(8,128)} %constant.43.clone.fz.fx) | copy-start | bytes 196612
  11.3 10.4 %collective-permute-start.3 = (f32[14,8,128]{2,1,0:T(8,128)S(1)}, f32[14,8,128]{2,1,0:T(8,128)S(1)}, u32[]{:S(2)}, u32[]{:S(2)}) collective-permute-start(f32[14,8,128]{2,1,0:T(8,128)S(1)} %pad_maximum_fusion.3), channel_id=1, source_target_pairs={{0,31},{1,0},{2,1},{3,2},{4,3},{5,4},{6,5},{7,6},{8,7},{9,8},{10,9... | collective-permute-start | bytes 172040 | tf_op jit(solution)/shard_map/ppermute | solution.py:316
  20.2 0.7 copy-start.19
  20.2 0.7 copy-start.15
  20.9 0.7 copy-start.16
  21.6 0.7 copy-start.10
  21.6 0.7 copy-start.13
  34.8 39.2 %copy-start.6 = (f32[128,128]{1,0:T(8,128)S(1)}, f32[128,128]{1,0:T(8,128)}, u32[]{:S(2)}) copy-start(f32[128,128]{1,0:T(8,128)} %constant.51.clone.dxt) | copy-start | bytes 196612
  34.8 39.2 %copy-start.7 = (f32[128,128]{1,0:T(8,128)S(1)}, f32[128,128]{1,0:T(8,128)}, u32[]{:S(2)}) copy-start(f32[128,128]{1,0:T(8,128)} %constant.50.clone.fxt) | copy-start | bytes 196612
  34.8 39.2 %copy-start.8 = (f32[128,1]{1,0:T(8,128)S(1)}, f32[128,1]{1,0:T(8,128)}, u32[]{:S(2)}) copy-start(f32[128,1]{1,0:T(8,128)} %constant.48.clone.kx2) | copy-start | bytes 1540
  63.0 11.0 %copy-start.3 = (f32[4,256,128]{2,1,0:T(8,128)S(1)}, f32[4,256,128]{2,1,0:T(8,128)}, u32[]{:S(2)}) copy-start(f32[4,256,128]{2,1,0:T(8,128)} %constant.47.clone.back) | copy-start | bytes 1572868
  63.0 11.0 %copy-start.4 = (f32[4,128,256]{2,1,0:T(8,128)S(1)}, f32[4,128,256]{2,1,0:T(8,128)}, u32[]{:S(2)}) copy-start(f32[4,128,256]{2,1,0:T(8,128)} %constant.46.clone.forth) | copy-start | bytes 1572868
  64.4 9.6 %all-to-all-start.1 = ((f32[4,128,128]{2,1,0:T(8,128)}), f32[4,128,128]{2,1,0:T(8,128)S(1)}, u32[]{:S(2)}, u32[]{:S(2)}) async-start(f32[4,128,128]{2,1,0:T(8,128)} %shard_map.240), calls=%async_computation.1 | async-start | bytes 524288 | tf_op jit(solution)/shard_map/all_to_all | solution.py:360
  67.8 6.2 %copy-start.11 = (f32[1,256]{1,0:T(1,128)S(1)}, f32[1,256]{1,0:T(1,128)}, u32[]{:S(2)}) copy-start(f32[1,256]{1,0:T(1,128)} %constant.49.clone.ky2) | copy-start | bytes 3076
  67.8 6.2 %copy-start.12 = (f32[128]{0:T(128)S(1)}, f32[128]{0:T(128)}, u32[]{:S(2)}) copy-start(f32[128]{0:T(128)} %constant.45.clone.kz2) | copy-start | bytes 1540
where the time goes:
time: 96.4 us; the launch traced here: 95.8 us
  blocking collectives  46.8 us (49%)
  starting transfers between devices  21 us (22%)
  Pallas kernels  17.1 us (18%)
  waiting for transfers between devices  6.04 us (6%)
  local copies, waits for them, and re-layouts  3.67 us (4%)
    all_to_all x1, blocking collectives, shards(): got = lax.all_to_all(spectra, MODES, 0, 0, tiled=True)  28.2 us
    all_to_all x1, blocking collectives, shards(): got = lax.all_to_all(grads, MODES, 0, 0, tiled=True)  18.6 us
    pallas_call x1, Pallas kernels, shards(): call(react_kernel, [(NSPEC, CX, CY, NZ), (5, CX, CY, NZ), (NZ, 2, 2 * COL...  12.5 us
    ppermute x1, starting transfers between devices, shards(): yhi = ring(GY, n_gy, -1)(fields(every, every, 0))  8.79 us
    all_to_all x1, waiting for transfers between devices, shards(): lines = lax.all_to_all(lines, 'x', 0, 0, tiled=True)  6.03 us
    ppermute x1, starting transfers between devices, shards(): xhi = ring(GX, n_gx, -1)(fields(every, 0))  4.23 us
    all_to_all x1, starting transfers between devices, shards(): lines = lax.all_to_all(lines, 'x', 0, 0, tiled=True)  3.4 us
    ppermute x1, starting transfers between devices, shards(): xlo = ring(GX, n_gx, 1)(fields(every, CX - 1))  2.7 us
  transfers between devices with their start and end apart: 5, of which 1 were waited for; matrix products, arithmetic and copies ran while one was open for 1% of the time, Pallas kernels for 0%

commit v1 on v0

--- a/solution.py
+++ b/solution.py
@@ -53,6 +53,16 @@
 
 def dot(a, b, dims=((1,), (0,))):
     return lax.dot_general(a, b, (dims, ((), ())), precision=PRECISE, preferred_element_type=F32)
+
+
+def parts(v):
+    hi = v.astype(jnp.bfloat16)
+    return hi, (v - hi.astype(F32)).astype(jnp.bfloat16)
+
+
+def dot3(a, b, dims=((1,), (0,))):
+    one = lambda p, q: lax.dot_general(p, q, (dims, ((), ())), preferred_element_type=F32)
+    return one(a[0], b[0]) + (one(a[0], b[1]) + one(a[1], b[0]))
 
 
 def rates(z, left, right, msa, energy):
@@ -222,9 +232,10 @@
     source = (final[NSPEC] - temp0[...]) * (1.0 / DT)
     nt = ((1,), (1,))
     horizontal = flow_mid[1:3].reshape(2 * COLS, NZ)
-    spectra[:, 0, :] = dot(fz[...], horizontal, nt)
+    fz2, dz2 = (fz[0], fz[1]), (dz[0], dz[1])
+    spectra[:, 0, :] = dot3(fz2, parts(horizontal), nt)
     vertical = flow_mid[3].reshape(COLS, NZ)
-    third = dot(dz[...], vertical, nt) - dot(fz[...], source, nt)
+    third = dot3(dz2, parts(vertical), nt) - dot3(fz2, parts(source), nt)
     spectra[:, 1, :] = jnp.concatenate([third, jnp.zeros_like(third)], axis=1)
 
 
@@ -243,34 +254,35 @@
 def stream_kernel(got, fx, dx, out):
     a = swap_blocks(got[:, 0, :])
     w = swap_blocks(got[:, 1, :])
-    u = a[:, :COLS]
-    h = dot(dx[...], u) + dot(fx[...], w[:, :COLS])
-    y = dot(fx[...], a[:, COLS:])
-    both = jnp.concatenate([h, y], axis=1)
+    upper = lax.broadcasted_iota(jnp.int32, a.shape, 1) < COLS
+    fx2, dx2 = (fx[0], fx[1]), (dx[0], dx[1])
+    moved = jnp.where(upper, w, a)
+    both = dot3(fx2, parts(moved)) + jnp.where(upper, dot3(dx2, parts(a)), 0.0)
     for i in range(4):
         out[i] = both
 
 
 def solve_kernel(place, kz2, got, forth, back, kx2, ky2, fxt, dxt, out):
-    full = dot(got[0], forth[0])
-    for i in range(1, 4):
-        full = full + dot(got[i], forth[i])
+    full = None
+    for i in range(4):
+        term = dot3(parts(got[i]), (forth[0, i], forth[1, i]))
+        full = term if full is None else full + term
     k2 = kx2[...] + ky2[...] + kz2[place[0]]
     q = full / jnp.where(k2 > 0, k2, 1.0)
-    lines = dot(q, back[place[1]])
-    first = dot(fxt[...], lines)
-    second = dot(dxt[...], lines)
+    lines = parts(dot3(parts(q), (back[0, place[1]], back[1, place[1]])))
+    first = dot3((fxt[0], fxt[1]), lines)
+    second = dot3((dxt[0], dxt[1]), lines)
     out[:, 0, :] = swap_blocks(first)
     out[:, 1, :] = swap_blocks(second)
 
 
 def finish_kernel(got, mid, fz, dz, out):
-    tn = ((0,), (0,))
-    first = got[:, 0, :]
-    second = got[:, 1, :]
-    a = dot(second, fz[...], tn)[:COLS]
-    b = dot(first[:, COLS:], fz[...], tn)
-    c = dot(first[:, :COLS], dz[...], tn)
+    fz2, dz2 = (fz[0], fz[1]), (dz[0], dz[1])
+    first = parts(jnp.transpose(got[:, 0, :]))
+    second = parts(jnp.transpose(got[:, 1, :]))
+    a = dot3(second, fz2)[:COLS]
+    b = dot3(first, fz2)[COLS:]
+    c = dot3(first, dz2)[:COLS]
     out[0] = mid[0]
     out[1] = mid[1] + a.reshape(CX, CY, NZ)
     out[2] = mid[2] + b.reshape(CX, CY, NZ)
@@ -324,6 +336,12 @@
     fy, dy, ky = basis(NY)
     fx, dx, kx = basis(NX)
     f32 = lambda v: np.ascontiguousarray(v, np.float32)
+
+    def table(v):
+        v = f32(v)
+        hi = v.astype(jnp.bfloat16)
+        return np.stack([hi, (v - hi.astype(np.float32)).astype(jnp.bfloat16)])
+
     y_of = ((np.arange(8)[None, :, None] * 4 + np.arange(4)[:, None, None]) * CY + np.arange(CY)).reshape(4, COLS)
     forth = np.stack([np.concatenate([fy[:, y].T, dy[:, y].T], axis=0) for y in y_of])
     back = np.stack([np.concatenate([fy[:, y], -dy[:, y]], axis=1) for y in y_of])
@@ -352,26 +370,27 @@
         msa,
         0.5 * energy,
         newton,
-        f32(fz),
-        f32(dz),
+        table(fz),
+        table(dz),
     )
+    place = jnp.stack([lax.axis_index(MODES), lax.axis_index("x")]).astype(jnp.int32)
+    spectra, place = lax.optimization_barrier((spectra, place))
     got = lax.all_to_all(spectra, MODES, 0, 0, tiled=True)
-    lines = call(stream_kernel, [(4, NX, 2 * COLS)], [VMEM] * 3)(got, f32(fx), f32(dx))
+    lines = call(stream_kernel, [(4, NX, 2 * COLS)], [VMEM] * 3)(got, table(fx), table(dx))
     lines = lax.all_to_all(lines, "x", 0, 0, tiled=True)
-    place = jnp.stack([lax.axis_index(MODES), lax.axis_index("x")]).astype(jnp.int32)
     grads = call(solve_kernel, [(NX, 2, 2 * COLS)], [SMEM] * 2 + [VMEM] * 7)(
         place,
         f32(kz * kz),
         lines,
-        f32(forth),
-        f32(back),
+        table(forth),
+        table(back),
         f32(kx * kx)[:, None],
         f32(ky * ky)[None, :],
-        f32(fx.T),
-        f32(-dx.T),
+        table(fx.T),
+        table(-dx.T),
     )
     got = lax.all_to_all(grads, MODES, 0, 0, tiled=True)
-    flow_out = call(finish_kernel, [(5, CX, CY, NZ)], [VMEM] * 4)(got, mid, f32(fz), f32(dz))
+    flow_out = call(finish_kernel, [(5, CX, CY, NZ)], [VMEM] * 4)(got, mid, table(fz), table(dz))
     return (species_out, flow_out)
 
 

time: 96.4 us -> 95.1 us (0.987)
  blocking collectives: 46.8 us -> 57 us
  waiting for transfers between devices: 6.04 us -> 0.04 us
  starting transfers between devices: 21 us -> 17.6 us
  Pallas kernels: 17.1 us -> 15.7 us
    all_to_all x0 -> x1, blocking collectives: none -> 12.5 us  [shards(): lines = lax.all_to_all(lines, 'x', 0, 0, tiled=True)]
    all_to_all x1 -> x0, waiting for transfers between devices: 6.03 us -> none  [shards(): lines = lax.all_to_all(lines, 'x', 0, 0, tiled=True)]
    all_to_all x1 -> x0, starting transfers between devices: 3.4 us -> none  [shards(): lines = lax.all_to_all(lines, 'x', 0, 0, tiled=True)]
    all_to_all x1, blocking collectives: 28.2 us -> 25.6 us  [shards(): got = lax.all_to_all(spectra, MODES, 0, 0, tiled=True)]
  transfers between devices with their start and end apart: 5 -> 4, of which waited for: 1 -> 0; matrix products, arithmetic and copies ran while one was open for 1% -> 1% of each run, Pallas kernels for 0% -> 0%
where the time goes in v1:
time: 95.1 us; the launch traced here: 94.7 us
  blocking collectives  57 us (60%)
  starting transfers between devices  17.6 us (19%)
  Pallas kernels  15.7 us (17%)
  local copies, waits for them, and re-layouts  3.23 us (3%)
    all_to_all x1, blocking collectives, shards(): got = lax.all_to_all(spectra, MODES, 0, 0, tiled=True)  25.6 us
    all_to_all x1, blocking collectives, shards(): got = lax.all_to_all(grads, MODES, 0, 0, tiled=True)  18.9 us
    pallas_call x1, Pallas kernels, shards(): call(react_kernel, [(NSPEC, CX, CY, NZ), (5, CX, CY, NZ), (NZ, 2, 2 * COL...  12.6 us
    all_to_all x1, blocking collectives, shards(): lines = lax.all_to_all(lines, 'x', 0, 0, tiled=True)  12.5 us
    ppermute x1, starting transfers between devices, shards(): yhi = ring(GY, n_gy, -1)(fields(every, every, 0))  8.79 us
    ppermute x1, starting transfers between devices, shards(): xhi = ring(GX, n_gx, -1)(fields(every, 0))  4.23 us
    ppermute x1, starting transfers between devices, shards(): xlo = ring(GX, n_gx, 1)(fields(every, CX - 1))  2.7 us
    ppermute x1, starting transfers between devices, shards(): ylo = ring(GY, n_gy, 1)(fields(every, every, CY - 1))  1.92 us
  transfers between devices with their start and end apart: 4, of which 0 were waited for; matrix products, arithmetic and copies ran while one was open for 1% of the time, Pallas kernels for 0%

profile of v1, /device:TPU:1, one launch (start us, length us, event | category | flops | bytes accessed | tf_op | source)
XLA Modules:
  0.0 94.7 jit_solution(17192699064291903540)
XLA Ops:
  0.6 0.0 copy-start
  0.6 0.8 slice_bitcast_fusion.2
  1.4 0.8 slice_bitcast_fusion
  2.3 2.7 %collective-permute-start = (f32[14,8,128]{2,1,0:T(8,128)S(1)}, f32[14,8,128]{2,1,0:T(8,128)S(1)}, u32[]{:S(2)}, u32[]{:S(2)}) collective-permute-start(f32[14,8,128]{2,1,0:T(8,128)S(1)} %pad_maximum_fusion), channel_id=1, source_target_pairs={{0,32},{32,64},{64,96},{96,128},{128,160},{160,192},{192,224},{224... | collective-permute-start | bytes 172040 | tf_op jit(solution)/shard_map/ppermute | solution.py:329
  5.0 4.2 %collective-permute-start.1 = (f32[14,8,128]{2,1,0:T(8,128)S(1)}, f32[14,8,128]{2,1,0:T(8,128)S(1)}, u32[]{:S(2)}, u32[]{:S(2)}) collective-permute-start(f32[14,8,128]{2,1,0:T(8,128)S(1)} %pad_maximum_fusion.1), channel_id=1, source_target_pairs={{0,480},{32,0},{64,32},{96,64},{128,96},{160,128},{192,160},{224,1... | collective-permute-start | bytes 172040 | tf_op jit(solution)/shard_map/ppermute | solution.py:330
  9.2 0.0 copy-done.5
  9.2 0.0 copy-done
  9.3 1.9 %collective-permute-start.2 = (f32[14,8,128]{2,1,0:T(8,128)S(1)}, f32[14,8,128]{2,1,0:T(8,128)S(1)}, u32[]{:S(2)}, u32[]{:S(2)}) collective-permute-start(f32[14,8,128]{2,1,0:T(8,128)S(1)} %pad_maximum_fusion.2), channel_id=1, source_target_pairs={{0,1},{1,2},{2,3},{3,4},{4,5},{5,6},{6,7},{7,8},{8,9},{9,10},{10,1... | collective-permute-start | bytes 172040 | tf_op jit(solution)/shard_map/ppermute | solution.py:327
  11.2 0.0 copy-start.18
  11.3 0.0 copy-start.19
  11.3 0.0 copy-start.15
  11.3 0.0 copy-start.16
  11.3 0.0 copy-start.14
  11.3 0.0 copy-start.2
  11.3 0.0 copy-start.1
  11.3 8.8 %collective-permute-start.3 = (f32[14,8,128]{2,1,0:T(8,128)S(1)}, f32[14,8,128]{2,1,0:T(8,128)S(1)}, u32[]{:S(2)}, u32[]{:S(2)}) collective-permute-start(f32[14,8,128]{2,1,0:T(8,128)S(1)} %pad_maximum_fusion.3), channel_id=1, source_target_pairs={{0,31},{1,0},{2,1},{3,2},{4,3},{5,4},{6,5},{7,6},{8,7},{9,8},{10,9... | collective-permute-start | bytes 172040 | tf_op jit(solution)/shard_map/ppermute | solution.py:328
  20.1 0.0 copy-done.18
  20.2 0.0 copy-done.19
  20.2 0.0 copy-done.15
  20.2 0.1 copy.34.left
  20.3 0.0 copy-done.16
  20.3 0.1 copy.35.right
  20.4 0.0 copy-done.14
  20.4 0.7 copy-done.9
  21.1 0.0 copy-done.17
  21.1 0.1 fusion.msa
  21.2 0.0 copy-start.13
  21.2 0.1 pad_add_fusion.place
  21.3 0.0 collective-permute-done.xlo
  21.3 0.0 collective-permute-done.1.xhi
  21.3 0.0 collective-permute-done.2.ylo
  21.3 0.0 collective-permute-done.3.yhi
  21.4 0.0 copy-done.2
  21.4 0.0 copy-done.1
  21.4 0.6 copy-done.10
  21.9 0.0 copy-done.13
  21.9 12.6 %shard_map.239 = (f32[9,8,8,128]{3,2,1,0:T(8,128)}, f32[5,8,8,128]{3,2,1,0:T(8,128)S(1)}, f32[128,2,128]{2,1,0:T(2,128)S(1)}) custom-call(f32[9,8,8,128]{3,2,1,0:T(8,128)S(1)} %copy-done, f32[5,8,8,128]{3,2,1,0:T(8,128)S(1)} %copy-done.5, f32[14,8,128]{2,1,0:T(8,128)S(1)} %collective-permute-done.xlo, f32[14,8,128]{2,1,0:T(8,128)S(1)} %collective-permute-done.1.xhi, ...), custom_call_target="tpu_custom_call" | custom-call | tf_op jit(solution)/shard_map/pallas_call | solution.py:349
  34.5 0.0 copy-start.11
  34.5 0.0 copy-start.12
  34.5 25.6 %all_to_all.15.got = f32[128,2,128]{2,1,0:T(2,128)S(1)} all-to-all(f32[128,2,128]{2,1,0:T(2,128)S(1)} %get-tuple-element.10), channel_id=1, replica_groups=mesh['y'=8,'c'=2,'z'=8,'x'=4] {'y','c','z'}, dimensions={0} | all-to-all | bytes 262144 | tf_op jit(solution)/shard_map/all_to_all | solution.py:378
  60.1 0.5 shard_map.240
  60.6 12.5 %all_to_all.16.got = f32[4,128,128]{2,1,0:T(8,128)S(1)} all-to-all(f32[4,128,128]{2,1,0:T(8,128)S(1)} %shard_map.240), channel_id=1, replica_groups=mesh['y'=8,'c'=2,'z'=8,'x'=4] {'x'}, dimensions={0} | all-to-all | bytes 524288 | tf_op jit(solution)/shard_map/all_to_all | solution.py:380
  73.1 0.0 copy-done.6
  73.1 0.0 copy-done.7
  73.1 0.0 copy-done.8
  73.1 1.7 %shard_map.241 = f32[128,2,128]{2,1,0:T(2,128)S(1)} custom-call(s32[2]{0:T(128)S(1)} %pad_add_fusion.place, f32[128]{0:T(128)S(1)} %copy-done.12, f32[4,128,128]{2,1,0:T(8,128)S(1)} %all_to_all.16.got, bf16[2,4,128,256]{3,2,1,0:T(8,128)(2,1)S(1)} %copy-done.4, bf16[2,4,256,128]{3,2,1,0:T(8,128)(2,1)S(1)} %copy-done.3, f32[128,1]{1,0:T(8,128)S(1)} %copy-done.8, ...), custom_call_target="tpu_custom_call" | custom-call | tf_op jit(solution)/shard_map/pallas_call | solution.py:381
  74.8 18.9 %all_to_all.17.got = f32[128,2,128]{2,1,0:T(2,128)S(1)} all-to-all(f32[128,2,128]{2,1,0:T(2,128)S(1)} %shard_map.241), channel_id=1, replica_groups=mesh['y'=8,'c'=2,'z'=8,'x'=4] {'y','c','z'}, dimensions={0} | all-to-all | bytes 262144 | tf_op jit(solution)/shard_map/all_to_all | solution.py:392
  93.7 1.0 %shard_map.242 = f32[5,8,8,128]{3,2,1,0:T(8,128)} custom-call(f32[128,2,128]{2,1,0:T(2,128)S(1)} %all_to_all.17.got, f32[5,8,8,128]{3,2,1,0:T(8,128)S(1)} %get-tuple-element.11.mid, bf16[2,128,128]{2,1,0:T(8,128)(2,1)S(1)} %copy-done.2, bf16[2,128,128]{2,1,0:T(8,128)(2,1)S(1)} %copy-done.1), custom_call_target="tpu_custom_call" | custom-call | tf_op jit(solution)/shard_map/pallas_call | solution.py:393
  (21 shorter events, 0.1 us)
Async XLA Ops:
  0.6 8.6 %copy-start = (f32[9,8,8,128]{3,2,1,0:T(8,128)S(1)}, f32[9,8,8,128]{3,2,1,0:T(8,128)}, u32[]{:S(2)}) copy-start(f32[9,8,8,128]{3,2,1,0:T(8,128)} %species.1) | copy-start | bytes 884740
  1.4 7.8 %copy-start.5 = (f32[5,8,8,128]{3,2,1,0:T(8,128)S(1)}, f32[5,8,8,128]{3,2,1,0:T(8,128)}, u32[]{:S(2)}) copy-start(f32[5,8,8,128]{3,2,1,0:T(8,128)} %flow.1) | copy-start | bytes 491524
  2.3 19.1 %collective-permute-start = (f32[14,8,128]{2,1,0:T(8,128)S(1)}, f32[14,8,128]{2,1,0:T(8,128)S(1)}, u32[]{:S(2)}, u32[]{:S(2)}) collective-permute-start(f32[14,8,128]{2,1,0:T(8,128)S(1)} %pad_maximum_fusion), channel_id=1, source_target_pairs={{0,32},{32,64},{64,96},{96,128},{128,160},{160,192},{192,224},{224... | collective-permute-start | bytes 172040 | tf_op jit(solution)/shard_map/ppermute | solution.py:329
  5.0 16.4 %collective-permute-start.1 = (f32[14,8,128]{2,1,0:T(8,128)S(1)}, f32[14,8,128]{2,1,0:T(8,128)S(1)}, u32[]{:S(2)}, u32[]{:S(2)}) collective-permute-start(f32[14,8,128]{2,1,0:T(8,128)S(1)} %pad_maximum_fusion.1), channel_id=1, source_target_pairs={{0,480},{32,0},{64,32},{96,64},{128,96},{160,128},{192,160},{224,1... | collective-permute-start | bytes 172040 | tf_op jit(solution)/shard_map/ppermute | solution.py:330
  9.3 12.0 %collective-permute-start.2 = (f32[14,8,128]{2,1,0:T(8,128)S(1)}, f32[14,8,128]{2,1,0:T(8,128)S(1)}, u32[]{:S(2)}, u32[]{:S(2)}) collective-permute-start(f32[14,8,128]{2,1,0:T(8,128)S(1)} %pad_maximum_fusion.2), channel_id=1, source_target_pairs={{0,1},{1,2},{2,3},{3,4},{4,5},{5,6},{6,7},{7,8},{8,9},{9,10},{10,1... | collective-permute-start | bytes 172040 | tf_op jit(solution)/shard_map/ppermute | solution.py:327
  11.2 8.9 %copy-start.18 = (f32[19]{0:T(128)S(1)}, f32[19]{0:T(128)}, u32[]{:S(2)}) copy-start(f32[19]{0:T(128)} %param.32) | copy-start | bytes 232
  11.3 8.9 %copy-start.19 = (f32[19]{0:T(128)S(1)}, f32[19]{0:T(128)}, u32[]{:S(2)}) copy-start(f32[19]{0:T(128)} %param.33) | copy-start | bytes 232
  11.3 8.9 %copy-start.15 = (f32[19,9]{0,1:T(8,128)S(1)}, f32[19,9]{0,1:T(8,128)}, u32[]{:S(2)}) copy-start(f32[19,9]{0,1:T(8,128)} %param.28) | copy-start | bytes 2056
  11.3 9.0 %copy-start.16 = (f32[19,9]{0,1:T(8,128)S(1)}, f32[19,9]{0,1:T(8,128)}, u32[]{:S(2)}) copy-start(f32[19,9]{0,1:T(8,128)} %param.29) | copy-start | bytes 2056
  11.3 9.1 %copy-start.14 = (f32[19,9]{0,1:T(8,128)S(1)}, f32[19,9]{0,1:T(8,128)}, u32[]{:S(2)}) copy-start(f32[19,9]{0,1:T(8,128)} %param.30) | copy-start | bytes 2056
  11.3 10.1 %copy-start.2 = (bf16[2,128,128]{2,1,0:T(8,128)(2,1)S(1)}, bf16[2,128,128]{2,1,0:T(8,128)(2,1)}, u32[]{:S(2)}) copy-start(bf16[2,128,128]{2,1,0:T(8,128)(2,1)} %constant.43.clone.fz.fx) | copy-start | bytes 196612
  11.3 10.0 %copy-start.1 = (bf16[2,128,128]{2,1,0:T(8,128)(2,1)S(1)}, bf16[2,128,128]{2,1,0:T(8,128)(2,1)}, u32[]{:S(2)}) copy-start(bf16[2,128,128]{2,1,0:T(8,128)(2,1)} %constant.44.clone.dz.dx) | copy-start | bytes 196612
  11.3 10.0 %collective-permute-start.3 = (f32[14,8,128]{2,1,0:T(8,128)S(1)}, f32[14,8,128]{2,1,0:T(8,128)S(1)}, u32[]{:S(2)}, u32[]{:S(2)}) collective-permute-start(f32[14,8,128]{2,1,0:T(8,128)S(1)} %pad_maximum_fusion.3), channel_id=1, source_target_pairs={{0,31},{1,0},{2,1},{3,2},{4,3},{5,4},{6,5},{7,6},{8,7},{9,8},{10,9... | collective-permute-start | bytes 172040 | tf_op jit(solution)/shard_map/ppermute | solution.py:328
  20.4 0.7 copy-start.9
  20.4 0.7 copy-start.17
  21.2 0.7 copy-start.10
  21.2 0.7 copy-start.13
  34.5 38.6 %copy-start.6 = (bf16[2,128,128]{2,1,0:T(8,128)(2,1)S(1)}, bf16[2,128,128]{2,1,0:T(8,128)(2,1)}, u32[]{:S(2)}) copy-start(bf16[2,128,128]{2,1,0:T(8,128)(2,1)} %constant.51.clone.dxt) | copy-start | bytes 196612
  34.5 38.6 %copy-start.7 = (bf16[2,128,128]{2,1,0:T(8,128)(2,1)S(1)}, bf16[2,128,128]{2,1,0:T(8,128)(2,1)}, u32[]{:S(2)}) copy-start(bf16[2,128,128]{2,1,0:T(8,128)(2,1)} %constant.50.clone.fxt) | copy-start | bytes 196612
  34.5 38.6 %copy-start.8 = (f32[128,1]{1,0:T(8,128)S(1)}, f32[128,1]{1,0:T(8,128)}, u32[]{:S(2)}) copy-start(f32[128,1]{1,0:T(8,128)} %constant.48.clone.kx2) | copy-start | bytes 1540
  34.5 38.6 %copy-start.11 = (f32[1,256]{1,0:T(1,128)S(1)}, f32[1,256]{1,0:T(1,128)}, u32[]{:S(2)}) copy-start(f32[1,256]{1,0:T(1,128)} %constant.49.clone.ky2) | copy-start | bytes 3076
  34.5 38.6 %copy-start.12 = (f32[128]{0:T(128)S(1)}, f32[128]{0:T(128)}, u32[]{:S(2)}) copy-start(f32[128]{0:T(128)} %constant.45.clone.kz2) | copy-start | bytes 1540
  60.1 13.0 %copy-start.3 = (bf16[2,4,256,128]{3,2,1,0:T(8,128)(2,1)S(1)}, bf16[2,4,256,128]{3,2,1,0:T(8,128)(2,1)}, u32[]{:S(2)}) copy-start(bf16[2,4,256,128]{3,2,1,0:T(8,128)(2,1)} %constant.47.clone.back) | copy-start | bytes 1572868
  60.1 13.0 %copy-start.4 = (bf16[2,4,128,256]{3,2,1,0:T(8,128)(2,1)S(1)}, bf16[2,4,128,256]{3,2,1,0:T(8,128)(2,1)}, u32[]{:S(2)}) copy-start(bf16[2,4,128,256]{3,2,1,0:T(8,128)(2,1)} %constant.46.clone.forth) | copy-start | bytes 1572868

commit v2 on v1

--- a/solution.py
+++ b/solution.py
@@ -24,7 +24,6 @@
 CY = 8
 COLS = CX * CY
 CAP = COLS // 2
-CHUNK = 16
 DT = 0.25
 PRECISE = lax.Precision.HIGHEST
 F32 = jnp.float32
@@ -65,40 +64,104 @@
     return one(a[0], b[0]) + (one(a[0], b[1]) + one(a[1], b[0]))
 
 
-def rates(z, left, right, msa, energy):
-    acc = None
-    for j in range(NREAC):
-        a = left[j, 0] * z[0]
-        b = right[j, 0] * z[0]
-        for s in range(1, NSPEC):
-            a = a + left[j, s] * z[s]
-            b = b + right[j, s] * z[s]
-        r = jnp.tanh(a) * jnp.tanh(b)
-        r = r + r * jnp.tanh(energy[j] * z[NSPEC])
-        term = [msa[i, j] * r for i in range(NS)]
-        acc = term if acc is None else [p + q for p, q in zip(acc, term)]
-    return acc
-
-
-def substep(load, store, h, left, right, msa, energy, newton):
-    z0 = [load(i) for i in range(NS)]
-    acc = rates(z0, left, right, msa, energy)
-    z = tuple(z0[i] + h * acc[i] for i in range(NS))
-
-    def again(_, z):
-        acc = rates(z, left, right, msa, energy)
-        d = [z[i] - load(i) for i in range(NS)]
-        out = []
-        for i in range(NS):
-            m = newton[i, 0] * d[0]
-            for j in range(1, NS):
-                m = m + newton[i, j] * d[j]
-            out.append(z[i] + (h * acc[i] - m))
-        return tuple(out)
-
-    z = lax.fori_loop(0, 2, again, z)
-    for i in range(NS):
-        store(i, z[i])
+OFF = 3
+ROWS = 16
+LINES = 24
+FORM = 3 * LINES
+GROUPS = 4
+
+
+def one_hot(shape, f):
+    r = lax.broadcasted_iota(jnp.int32, shape, 0)
+    c = lax.broadcasted_iota(jnp.int32, shape, 1)
+    return f(r, c).astype(F32)
+
+
+def weights_kernel(left, right, stoich, heat, prefactor, energy, newton, classes, forms, update, plan):
+    down = lambda k: one_hot((FORM, NREAC), lambda r, c: r == c + k * LINES)
+    across = one_hot((NSPEC, ROWS), lambda r, c: c == r + OFF)
+    eye = one_hot((NREAC, NREAC), lambda r, c: r == c)
+    energy_col = jnp.sum(eye * energy[...][None, :], axis=1, keepdims=True)
+    temp = one_hot((NREAC, ROWS), lambda r, c: c == OFF + NSPEC)
+    w = (
+        dot(down(0), dot(left[...], across))
+        + dot(down(1), dot(right[...], across))
+        + dot(down(2), 0.5 * energy_col * temp)
+    )
+    wide = GROUPS * 3 * ROWS
+    tall = GROUPS * FORM
+    copies = dot(w, one_hot((ROWS, wide), lambda r, c: r == c % ROWS))
+    every = jnp.concatenate([copies] * GROUPS, axis=0)
+    r = lax.broadcasted_iota(jnp.int32, (tall, wide), 0)
+    c = lax.broadcasted_iota(jnp.int32, (tall, wide), 1)
+    hi, lo = parts(jnp.where(r // FORM == c // (3 * ROWS), every, 0.0))
+    forms[...] = jnp.where(c % (3 * ROWS) < 2 * ROWS, hi.astype(F32), lo.astype(F32)).astype(jnp.bfloat16)
+
+    heat_col = jnp.sum(eye * heat[...][None, :], axis=1, keepdims=True)
+    both = dot(stoich[...], one_hot((NSPEC, NS), lambda r, c: r == c))
+    both = both + heat_col * one_hot((NREAC, NS), lambda r, c: c == NSPEC)
+    msa = dot(newton[...], both, ((1,), (1,))) * (0.5 * prefactor[...][None, :])
+    v = dot(msa, one_hot((NREAC, 32), lambda r, c: r == c))
+    v = v - dot(newton[...], one_hot((NS, 32), lambda r, c: c == r + NREAC))
+    v = dot(one_hot((ROWS, NS), lambda r, c: r == c + OFF), v)
+    copies = dot(v, one_hot((32, 192), lambda r, c: r == c % 32))
+    every = jnp.concatenate([copies, copies], axis=0)
+    r = lax.broadcasted_iota(jnp.int32, (2 * ROWS, 192), 0)
+    c = lax.broadcasted_iota(jnp.int32, (2 * ROWS, 192), 1)
+    hi, lo = parts(jnp.where(r // ROWS == c // 96, every, 0.0))
+    update[...] = jnp.where(c % 96 < 64, hi.astype(F32), lo.astype(F32)).astype(jnp.bfloat16)
+
+    cls = classes[...].astype(F32)
+    pick_x = one_hot((COLS, CX), lambda r, c: r // CY == c)
+    pick_y = one_hot((COLS, CY), lambda r, c: r % CY == c)
+    class_col = jnp.sum(dot(pick_x, cls) * pick_y, axis=1, keepdims=True)
+    rows = dot(cls, pick_y, ((1,), (1,)))
+    class_row = jnp.sum(one_hot((CX, COLS), lambda r, c: c // CY == r) * rows, axis=0, keepdims=True)
+    ii = lax.broadcasted_iota(jnp.int32, (COLS, COLS), 0).astype(F32)
+    jj = lax.broadcasted_iota(jnp.int32, (COLS, COLS), 1).astype(F32)
+    rank_col = jnp.sum((class_row * COLS - jj > class_col * COLS - ii).astype(F32), axis=1, keepdims=True)
+    at = (rank_col == jj).astype(F32)
+    order = jnp.sum(at * ii, axis=0, keepdims=True)
+    sorted_class = jnp.sum(at * class_col, axis=0, keepdims=True)
+    table = jnp.concatenate([order, class_row, sorted_class, jnp.zeros((5, COLS), F32)], axis=0)
+    plan[...] = jnp.concatenate([table, jnp.zeros_like(table)], axis=1).astype(jnp.int32)
+
+
+def step_of(c):
+    return jnp.where(c == 1, DT, jnp.where(c == 2, DT / 2, jnp.where(c == 3, DT / 3, DT / 4)))
+
+
+def substep(cols, steps, forms, update):
+    per = len(cols) // GROUPS
+    wide = per * NZ
+    z0 = [jnp.concatenate(cols[g * per : (g + 1) * per], axis=1) for g in range(GROUPS)]
+    h = [
+        jnp.concatenate([jnp.full((1, NZ), 1.0, F32) * steps[g * per + i] for i in range(per)], axis=1)
+        for g in range(GROUPS)
+    ]
+    z = z0
+    for repeat in range(3):
+        stack = []
+        for g in range(GROUPS):
+            hi, lo = parts(z[g])
+            stack += [hi, lo, hi]
+        t = jnp.dot(forms, jnp.concatenate(stack, axis=0), preferred_element_type=F32)
+        pairs = []
+        for g in range(GROUPS):
+            at = g * FORM
+            p = jnp.tanh(t[at : at + LINES]) * jnp.tanh(t[at + LINES : at + 2 * LINES])
+            p = (p + p * jnp.tanh(t[at + 2 * LINES : at + FORM])) * h[g]
+            if repeat:
+                d = z[g] - z0[g]
+                x = jnp.concatenate([p[:16], p[16:] + d[:8], d[8:]], axis=0)
+            else:
+                x = jnp.concatenate([p, jnp.zeros((8, wide), F32)], axis=0)
+            hi, lo = parts(x)
+            pairs.append(jnp.concatenate([hi, lo, hi], axis=0))
+        side = [jnp.concatenate(pairs[2 * k : 2 * k + 2], axis=0) for k in range(2)]
+        change = [jnp.dot(update, s, preferred_element_type=F32) for s in side]
+        z = [z[g] + change[g // 2][(g % 2) * ROWS : (g % 2 + 1) * ROWS] for g in range(GROUPS)]
+    return [z[k // per][:, (k % per) * NZ : (k % per + 1) * NZ] for k in range(len(cols))]
 
 
 def react_kernel(
@@ -108,13 +171,10 @@
     xhi,
     ylo,
     yhi,
-    classes,
     diff,
-    left,
-    right,
-    msa,
-    energy,
-    newton,
+    plan,
+    forms,
+    update,
     fz,
     dz,
     species_out,
@@ -122,7 +182,6 @@
     spectra,
     state,
     temp0,
-    hcol,
     buf,
 ):
     ysub = lax.broadcasted_iota(jnp.int32, (CY, NZ), 0)
@@ -145,91 +204,63 @@
         )
         return field + DT * (coef * lap - adv)
 
+    zero = jnp.zeros((COLS, NZ), F32)
+    for row in list(range(OFF)) + list(range(OFF + NS, ROWS)):
+        state[:, row, :] = zero
     for f in range(NF):
         field = species[f] if f < NSPEC else flow[f - NSPEC]
         moved = transport(f, field, diff[f])
         if f < NSPEC:
-            state[:, f * NZ : (f + 1) * NZ] = moved.reshape(COLS, NZ)
+            state[:, OFF + f, :] = moved.reshape(COLS, NZ)
         elif f == NF - 1:
-            state[:, NSPEC * NZ :] = moved.reshape(COLS, NZ)
+            state[:, OFF + NSPEC, :] = moved.reshape(COLS, NZ)
             temp0[...] = moved.reshape(COLS, NZ)
         else:
             flow_mid[f - NSPEC] = moved
 
-    cls = classes[...].astype(F32)
-    col = lax.broadcasted_iota(jnp.int32, (COLS, CX), 0)
-    lane = lax.broadcasted_iota(jnp.int32, (COLS, CX), 1)
-    pick_x = (col // CY == lane).astype(F32)
-    pick_y = (col % CY == lane).astype(F32)
-    class_col = jnp.sum(dot(pick_x, cls) * pick_y, axis=1, keepdims=True)
-    rows = dot(cls, pick_y, ((1,), (1,)))
-    row_x = lax.broadcasted_iota(jnp.int32, (CX, COLS), 0)
-    row_c = lax.broadcasted_iota(jnp.int32, (CX, COLS), 1)
-    class_row = jnp.sum(jnp.where(row_c // CY == row_x, rows, 0.0), axis=0, keepdims=True)
-    hcol[...] = jnp.broadcast_to(DT / class_col, (COLS, NZ))
-    ii = lax.broadcasted_iota(jnp.int32, (COLS, COLS), 0).astype(F32)
-    jj = lax.broadcasted_iota(jnp.int32, (COLS, COLS), 1).astype(F32)
-    key_col = class_col * COLS - ii
-    key_row = class_row * COLS - jj
-    rank_row = jnp.sum((key_col > key_row).astype(F32), axis=0, keepdims=True)
-    rank_col = jnp.sum((key_row > key_col).astype(F32), axis=1, keepdims=True)
-    place = lax.broadcasted_iota(jnp.int32, (CAP, COLS), 0).astype(F32)
-    gather = (place == rank_row).astype(F32)
-    place_t = lax.broadcasted_iota(jnp.int32, (COLS, CAP), 1).astype(F32)
-    scatter = (place_t == rank_col).astype(F32)
-    counts = [jnp.sum((class_row > float(s)).astype(jnp.int32)) for s in (1, 2, 3)]
-
     def first(g, _):
-        rows16 = pl.ds(pl.multiple_of(g * CHUNK, CHUNK), CHUNK)
-
-        def load(i):
-            return state[rows16, i * NZ : (i + 1) * NZ]
-
-        def store(i, value):
-            state[rows16, i * NZ : (i + 1) * NZ] = value
-
-        substep(load, store, hcol[rows16, :], left, right, msa, energy, newton)
+        start = g * CAP
+        cols = [state[start + k] for k in range(CAP)]
+        steps = [step_of(plan[1, start + k]) for k in range(CAP)]
+        done = substep(cols, steps, forms[...], update[...])
+        for k in range(CAP):
+            state[start + k] = done[k]
         return 0
 
-    lax.fori_loop(0, COLS // CHUNK, first, 0)
-
-    buf[...] = dot(gather, state[...])
-    class_sorted = jnp.sum(gather * class_row, axis=1, keepdims=True)
-    hcol[0:CAP, :] = jnp.broadcast_to(DT / class_sorted, (CAP, NZ))
-
-    def extra(g, _):
-        start = g * CHUNK
-        rows16 = pl.ds(pl.multiple_of(start, CHUNK), CHUNK)
-        more = sum((c > start).astype(jnp.int32) for c in counts)
-
-        def again(s, _):
-            h = hcol[rows16, :]
-            active = h < DT / (s + 1.5)
-
-            def load(i):
-                return buf[rows16, i * NZ : (i + 1) * NZ]
-
-            def store(i, value):
-                buf[rows16, i * NZ : (i + 1) * NZ] = jnp.where(active, value, load(i))
-
-            substep(load, store, h, left, right, msa, energy, newton)
-            return 0
-
-        lax.fori_loop(0, more, again, 0)
+    lax.fori_loop(0, COLS // CAP, first, 0)
+
+    for k in range(CAP):
+        buf[k] = state[plan[0, k]]
+
+    def some(count, s):
+        classes = [plan[2, k] for k in range(count)]
+        cols = [buf[k] for k in range(count)]
+        done = substep(cols, [step_of(c) for c in classes], forms[...], update[...])
+        for k in range(count):
+            buf[k] = jnp.where(classes[k] > s, done[k], cols[k])
+
+    def section(s, _):
+        many = plan[2, CAP // 2] > s
+
+        @pl.when(many)
+        def _():
+            some(CAP, s)
+
+        @pl.when(jnp.logical_and(jnp.logical_not(many), plan[2, 0] > s))
+        def _():
+            some(CAP // 2, s)
+
         return 0
 
-    lax.fori_loop(0, CAP // CHUNK, extra, 0)
-
-    spread = dot(scatter, buf[...])
-    chosen = rank_col < CAP - 0.5
-    final = [
-        jnp.where(chosen, spread[:, i * NZ : (i + 1) * NZ], state[:, i * NZ : (i + 1) * NZ])
-        for i in range(NS)
-    ]
+    lax.fori_loop(1, 4, section, 0)
+
+    for k in range(CAP):
+        state[plan[0, k]] = buf[k]
     for i in range(NSPEC):
-        species_out[i] = final[i].reshape(CX, CY, NZ)
-    flow_mid[4] = final[NSPEC].reshape(CX, CY, NZ)
-    source = (final[NSPEC] - temp0[...]) * (1.0 / DT)
+        species_out[i] = state[:, OFF + i, :].reshape(CX, CY, NZ)
+    last = state[:, OFF + NSPEC, :]
+    flow_mid[4] = last.reshape(CX, CY, NZ)
+    source = (last - temp0[...]) * (1.0 / DT)
     nt = ((1,), (1,))
     horizontal = flow_mid[1:3].reshape(2 * COLS, NZ)
     fz2, dz2 = (fz[0], fz[1]), (dz[0], dz[1])
@@ -290,8 +321,9 @@
     out[4] = mid[4]
 
 
-def call(kernel, out_shapes, specs, scratch=(), flops=0, nbytes=0):
-    out = [jax.ShapeDtypeStruct(s, F32) for s in out_shapes]
+def call(kernel, out_shapes, specs, scratch=()):
+    pairs = [s if isinstance(s[0], tuple) else (s, F32) for s in out_shapes]
+    out = [jax.ShapeDtypeStruct(*s) for s in pairs]
     return pl.pallas_call(
         kernel,
         out_shape=out if len(out) > 1 else out[0],
@@ -329,8 +361,15 @@
     xlo = ring(GX, n_gx, 1)(fields(every, CX - 1))
     xhi = ring(GX, n_gx, -1)(fields(every, 0))
 
-    both = jnp.concatenate([stoich, heat[:, None]], axis=1)
-    msa = jnp.einsum("ij,rj->ir", newton, both, precision=PRECISE) * (0.5 * prefactor)[None, :]
+    forms, update, plan = call(
+        weights_kernel,
+        [
+            ((GROUPS * FORM, GROUPS * 3 * ROWS), jnp.bfloat16),
+            ((2 * ROWS, 192), jnp.bfloat16),
+            ((8, 128), jnp.int32),
+        ],
+        [VMEM] * 8,
+    )(left, right, stoich, heat, prefactor, energy, newton, classes)
 
     fz, dz, kz = basis(NZ)
     fy, dy, ky = basis(NY)
@@ -349,30 +388,13 @@
     species_out, mid, spectra = call(
         react_kernel,
         [(NSPEC, CX, CY, NZ), (5, CX, CY, NZ), (NZ, 2, 2 * COLS)],
-        [VMEM] * 7 + [SMEM] * 6 + [VMEM] * 2,
+        [VMEM] * 6 + [SMEM] * 2 + [VMEM] * 4,
         [
-            pltpu.VMEM((COLS, NS * NZ), F32),
+            pltpu.VMEM((COLS, ROWS, NZ), F32),
             pltpu.VMEM((COLS, NZ), F32),
-            pltpu.VMEM((COLS, NZ), F32),
-            pltpu.VMEM((CAP, NS * NZ), F32),
+            pltpu.VMEM((CAP, ROWS, NZ), F32),
         ],
-    )(
-        species,
-        flow,
-        xlo,
-        xhi,
-        ylo,
-        yhi,
-        classes,
-        diffusivity,
-        left,
-        right,
-        msa,
-        0.5 * energy,
-        newton,
-        table(fz),
-        table(dz),
-    )
+    )(species, flow, xlo, xhi, ylo, yhi, diffusivity, plan, forms, update, table(fz), table(dz))
     place = jnp.stack([lax.axis_index(MODES), lax.axis_index("x")]).astype(jnp.int32)
     spectra, place = lax.optimization_barrier((spectra, place))
     got = lax.all_to_all(spectra, MODES, 0, 0, tiled=True)

time: 95.1 us -> 89.1 us (0.937)
  blocking collectives: 57 us -> 53.9 us
  Pallas kernels: 15.7 us -> 13.6 us
    pallas_call x1, Pallas kernels: 12.6 us -> 8.7 us  [shards(): call(react_kernel, [(NSPEC, CX, CY, NZ), (5, CX, CY, NZ), (NZ, 2, 2 * COL...]
    all_to_all x1, blocking collectives: 12.5 us -> 9.45 us  [shards(): lines = lax.all_to_all(lines, 'x', 0, 0, tiled=True)]
    pallas_call x0 -> x1, Pallas kernels: none -> 1.75 us  [shards(): call(weights_kernel, [((GROUPS * FORM, GROUPS * 3 * ROWS), jnp.bfloat16),...]
  transfers between devices with their start and end apart: 4 -> 4, of which waited for: 0 -> 0; matrix products, arithmetic and copies ran while one was open for 1% -> 1% of each run, Pallas kernels for 0% -> 2%
where the time goes in v2:
time: 89.1 us; the launch traced here: 88.7 us
  blocking collectives  53.9 us (60%)
  starting transfers between devices  17.5 us (20%)
  Pallas kernels  13.6 us (15%)
  local copies, waits for them, and re-layouts  2.7 us (3%)
  between operations  0.91 us (1%)
    all_to_all x1, blocking collectives, shards(): got = lax.all_to_all(spectra, MODES, 0, 0, tiled=True)  25.5 us
    all_to_all x1, blocking collectives, shards(): got = lax.all_to_all(grads, MODES, 0, 0, tiled=True)  18.9 us
    all_to_all x1, blocking collectives, shards(): lines = lax.all_to_all(lines, 'x', 0, 0, tiled=True)  9.45 us
    pallas_call x1, Pallas kernels, shards(): call(react_kernel, [(NSPEC, CX, CY, NZ), (5, CX, CY, NZ), (NZ, 2, 2 * COL...  8.7 us
    ppermute x1, starting transfers between devices, shards(): yhi = ring(GY, n_gy, -1)(fields(every, every, 0))  8.65 us
    ppermute x1, starting transfers between devices, shards(): xhi = ring(GX, n_gx, -1)(fields(every, 0))  4.23 us
    ppermute x1, starting transfers between devices, shards(): xlo = ring(GX, n_gx, 1)(fields(every, CX - 1))  2.7 us
    ppermute x1, starting transfers between devices, shards(): ylo = ring(GY, n_gy, 1)(fields(every, every, CY - 1))  1.92 us
  transfers between devices with their start and end apart: 4, of which 0 were waited for; matrix products, arithmetic and copies ran while one was open for 1% of the time, Pallas kernels for 2%

profile of v2, /device:TPU:1, one launch (start us, length us, event | category | flops | bytes accessed | tf_op | source)
XLA Modules:
  0.0 88.7 jit_solution(14451772281168814018)
XLA Ops:
  0.6 0.0 copy-start
  0.6 0.8 slice_bitcast_fusion.2
  1.4 0.8 slice_bitcast_fusion
  2.3 2.7 %collective-permute-start = (f32[14,8,128]{2,1,0:T(8,128)S(1)}, f32[14,8,128]{2,1,0:T(8,128)S(1)}, u32[]{:S(2)}, u32[]{:S(2)}) collective-permute-start(f32[14,8,128]{2,1,0:T(8,128)S(1)} %pad_maximum_fusion), channel_id=1, source_target_pairs={{0,32},{32,64},{64,96},{96,128},{128,160},{160,192},{192,224},{224... | collective-permute-start | bytes 172040 | tf_op jit(solution)/shard_map/ppermute | solution.py:361
  5.0 4.2 %collective-permute-start.1 = (f32[14,8,128]{2,1,0:T(8,128)S(1)}, f32[14,8,128]{2,1,0:T(8,128)S(1)}, u32[]{:S(2)}, u32[]{:S(2)}) collective-permute-start(f32[14,8,128]{2,1,0:T(8,128)S(1)} %pad_maximum_fusion.1), channel_id=1, source_target_pairs={{0,480},{32,0},{64,32},{96,64},{128,96},{160,128},{192,160},{224,1... | collective-permute-start | bytes 172040 | tf_op jit(solution)/shard_map/ppermute | solution.py:362
  9.2 0.0 copy-done.5
  9.2 0.0 copy-done
  9.3 1.9 %collective-permute-start.2 = (f32[14,8,128]{2,1,0:T(8,128)S(1)}, f32[14,8,128]{2,1,0:T(8,128)S(1)}, u32[]{:S(2)}, u32[]{:S(2)}) collective-permute-start(f32[14,8,128]{2,1,0:T(8,128)S(1)} %pad_maximum_fusion.2), channel_id=1, source_target_pairs={{0,1},{1,2},{2,3},{3,4},{4,5},{5,6},{6,7},{7,8},{8,9},{9,10},{10,1... | collective-permute-start | bytes 172040 | tf_op jit(solution)/shard_map/ppermute | solution.py:359
  11.2 0.0 copy-start.18
  11.3 0.0 copy-start.19
  11.3 8.7 %collective-permute-start.3 = (f32[14,8,128]{2,1,0:T(8,128)S(1)}, f32[14,8,128]{2,1,0:T(8,128)S(1)}, u32[]{:S(2)}, u32[]{:S(2)}) collective-permute-start(f32[14,8,128]{2,1,0:T(8,128)S(1)} %pad_maximum_fusion.3), channel_id=1, source_target_pairs={{0,31},{1,0},{2,1},{3,2},{4,3},{5,4},{6,5},{7,6},{8,7},{9,8},{10,9... | collective-permute-start | bytes 172040 | tf_op jit(solution)/shard_map/ppermute | solution.py:360
  19.9 0.0 copy-start.10
  20.0 0.0 copy-start.17
  20.0 0.0 copy-start.9
  20.0 0.0 copy-start.14
  20.0 0.0 copy-start.15
  20.0 0.0 copy-start.16
  20.0 0.0 copy-start.12
  20.0 0.6 copy-done.17
  20.7 0.1 copy.34.left
  20.8 0.0 copy-done.18
  20.8 0.1 copy.35.right
  20.9 0.0 copy-done.19
  20.9 0.1 copy.36.stoich
  21.0 0.0 copy-done.10
  21.0 0.0 copy-done.9
  21.0 0.0 copy-done.14
  21.0 0.0 copy-done.15
  21.0 0.0 copy-done.16
  21.0 1.7 %shard_map.239 = (bf16[288,192]{1,0:T(8,128)(2,1)S(1)}, bf16[32,192]{1,0:T(8,128)(2,1)S(1)}, s32[8,128]{1,0:T(8,128)S(1)}) custom-call(f32[19,9]{1,0:T(8,128)S(1)} %copy.34.left, f32[19,9]{1,0:T(8,128)S(1)} %copy.35.right, f32[19,9]{1,0:T(8,128)S(1)} %copy.36.stoich, f32[19]{0:T(128)S(1)} %copy-done.14, f32[19]{0:T(128)S(1)} %copy-done.15, ...), custom_call_target="tpu_custom_call" | custom-call | tf_op jit(solution)/shard_map/pallas_call | solution.py:364
  22.7 0.1 pad_add_fusion.place
  22.8 0.0 collective-permute-done.xlo
  22.8 0.0 collective-permute-done.1.xhi
  22.8 0.0 collective-permute-done.2.ylo
  22.8 0.0 collective-permute-done.3.yhi
  22.8 0.0 copy-done.12
  22.8 0.0 copy-done.1
  22.9 0.0 copy-done.2
  22.9 8.7 %shard_map.240 = (f32[9,8,8,128]{3,2,1,0:T(8,128)}, f32[5,8,8,128]{3,2,1,0:T(8,128)S(1)}, f32[128,2,128]{2,1,0:T(2,128)S(1)}) custom-call(f32[9,8,8,128]{3,2,1,0:T(8,128)S(1)} %copy-done, f32[5,8,8,128]{3,2,1,0:T(8,128)S(1)} %copy-done.5, f32[14,8,128]{2,1,0:T(8,128)S(1)} %collective-permute-done.xlo, f32[14,8,128]{2,1,0:T(8,128)S(1)} %collective-permute-done.1.xhi, ...), custom_call_target="tpu_custom_call" | custom-call | tf_op jit(solution)/shard_map/pallas_call | solution.py:388
  31.6 0.0 copy-start.13
  31.6 25.5 %all_to_all.15.got = f32[128,2,128]{2,1,0:T(2,128)S(1)} all-to-all(f32[128,2,128]{2,1,0:T(2,128)S(1)} %get-tuple-element.16), channel_id=1, replica_groups=mesh['y'=8,'c'=2,'z'=8,'x'=4] {'y','c','z'}, dimensions={0} | all-to-all | bytes 262144 | tf_op jit(solution)/shard_map/all_to_all | solution.py:400
  57.1 0.5 shard_map.241
  57.6 9.4 %all_to_all.16.got = f32[4,128,128]{2,1,0:T(8,128)S(1)} all-to-all(f32[4,128,128]{2,1,0:T(8,128)S(1)} %shard_map.241), channel_id=1, replica_groups=mesh['y'=8,'c'=2,'z'=8,'x'=4] {'x'}, dimensions={0} | all-to-all | bytes 524288 | tf_op jit(solution)/shard_map/all_to_all | solution.py:402
  67.1 0.0 copy-done.6
  67.1 0.0 copy-done.7
  67.1 1.7 %shard_map.242 = f32[128,2,128]{2,1,0:T(2,128)S(1)} custom-call(s32[2]{0:T(128)S(1)} %pad_add_fusion.place, f32[128]{0:T(128)S(1)} %copy-done.13, f32[4,128,128]{2,1,0:T(8,128)S(1)} %all_to_all.16.got, bf16[2,4,128,256]{3,2,1,0:T(8,128)(2,1)S(1)} %copy-done.4, bf16[2,4,256,128]{3,2,1,0:T(8,128)(2,1)S(1)} %copy-done.3, f32[128,1]{1,0:T(8,128)S(1)} %copy-done.8, ...), custom_call_target="tpu_custom_call" | custom-call | tf_op jit(solution)/shard_map/pallas_call | solution.py:403
  68.8 18.9 %all_to_all.17.got = f32[128,2,128]{2,1,0:T(2,128)S(1)} all-to-all(f32[128,2,128]{2,1,0:T(2,128)S(1)} %shard_map.242), channel_id=1, replica_groups=mesh['y'=8,'c'=2,'z'=8,'x'=4] {'y','c','z'}, dimensions={0} | all-to-all | bytes 262144 | tf_op jit(solution)/shard_map/all_to_all | solution.py:414
  87.7 1.0 %shard_map.243 = f32[5,8,8,128]{3,2,1,0:T(8,128)} custom-call(f32[128,2,128]{2,1,0:T(2,128)S(1)} %all_to_all.17.got, f32[5,8,8,128]{3,2,1,0:T(8,128)S(1)} %get-tuple-element.17.mid, bf16[2,128,128]{2,1,0:T(8,128)(2,1)S(1)} %copy-done.2, bf16[2,128,128]{2,1,0:T(8,128)(2,1)S(1)} %copy-done.1), custom_call_target="tpu_custom_call" | custom-call | tf_op jit(solution)/shard_map/pallas_call | solution.py:415
  (20 shorter events, 0.1 us)
Async XLA Ops:
  0.6 8.6 %copy-start = (f32[9,8,8,128]{3,2,1,0:T(8,128)S(1)}, f32[9,8,8,128]{3,2,1,0:T(8,128)}, u32[]{:S(2)}) copy-start(f32[9,8,8,128]{3,2,1,0:T(8,128)} %species.1) | copy-start | bytes 884740
  1.4 7.8 %copy-start.5 = (f32[5,8,8,128]{3,2,1,0:T(8,128)S(1)}, f32[5,8,8,128]{3,2,1,0:T(8,128)}, u32[]{:S(2)}) copy-start(f32[5,8,8,128]{3,2,1,0:T(8,128)} %flow.1) | copy-start | bytes 491524
  2.3 20.5 %collective-permute-start = (f32[14,8,128]{2,1,0:T(8,128)S(1)}, f32[14,8,128]{2,1,0:T(8,128)S(1)}, u32[]{:S(2)}, u32[]{:S(2)}) collective-permute-start(f32[14,8,128]{2,1,0:T(8,128)S(1)} %pad_maximum_fusion), channel_id=1, source_target_pairs={{0,32},{32,64},{64,96},{96,128},{128,160},{160,192},{192,224},{224... | collective-permute-start | bytes 172040 | tf_op jit(solution)/shard_map/ppermute | solution.py:361
  5.0 17.8 %collective-permute-start.1 = (f32[14,8,128]{2,1,0:T(8,128)S(1)}, f32[14,8,128]{2,1,0:T(8,128)S(1)}, u32[]{:S(2)}, u32[]{:S(2)}) collective-permute-start(f32[14,8,128]{2,1,0:T(8,128)S(1)} %pad_maximum_fusion.1), channel_id=1, source_target_pairs={{0,480},{32,0},{64,32},{96,64},{128,96},{160,128},{192,160},{224,1... | collective-permute-start | bytes 172040 | tf_op jit(solution)/shard_map/ppermute | solution.py:362
  9.3 13.5 %collective-permute-start.2 = (f32[14,8,128]{2,1,0:T(8,128)S(1)}, f32[14,8,128]{2,1,0:T(8,128)S(1)}, u32[]{:S(2)}, u32[]{:S(2)}) collective-permute-start(f32[14,8,128]{2,1,0:T(8,128)S(1)} %pad_maximum_fusion.2), channel_id=1, source_target_pairs={{0,1},{1,2},{2,3},{3,4},{4,5},{5,6},{6,7},{7,8},{8,9},{9,10},{10,1... | collective-permute-start | bytes 172040 | tf_op jit(solution)/shard_map/ppermute | solution.py:359
  11.2 9.5 %copy-start.18 = (f32[19,9]{0,1:T(8,128)S(1)}, f32[19,9]{0,1:T(8,128)}, u32[]{:S(2)}) copy-start(f32[19,9]{0,1:T(8,128)} %param.29) | copy-start | bytes 2056
  11.3 9.6 %copy-start.19 = (f32[19,9]{0,1:T(8,128)S(1)}, f32[19,9]{0,1:T(8,128)}, u32[]{:S(2)}) copy-start(f32[19,9]{0,1:T(8,128)} %param.30) | copy-start | bytes 2056
  11.3 11.5 %collective-permute-start.3 = (f32[14,8,128]{2,1,0:T(8,128)S(1)}, f32[14,8,128]{2,1,0:T(8,128)S(1)}, u32[]{:S(2)}, u32[]{:S(2)}) collective-permute-start(f32[14,8,128]{2,1,0:T(8,128)S(1)} %pad_maximum_fusion.3), channel_id=1, source_target_pairs={{0,31},{1,0},{2,1},{3,2},{4,3},{5,4},{6,5},{7,6},{8,7},{9,8},{10,9... | collective-permute-start | bytes 172040 | tf_op jit(solution)/shard_map/ppermute | solution.py:360
  19.9 1.0 %copy-start.10 = (s32[8,8]{1,0:T(8,128)S(1)}, s32[8,8]{1,0:T(8,128)}, u32[]{:S(2)}) copy-start(s32[8,8]{1,0:T(8,128)} %classes.1) | copy-start | bytes 772
  20.0 0.7 copy-start.17
  20.0 1.0 %copy-start.9 = (f32[10,10]{1,0:T(8,128)S(1)}, f32[10,10]{1,0:T(8,128)}, u32[]{:S(2)}) copy-start(f32[10,10]{1,0:T(8,128)} %newton.1) | copy-start | bytes 1204
  20.0 1.0 %copy-start.14 = (f32[19]{0:T(128)S(1)}, f32[19]{0:T(128)}, u32[]{:S(2)}) copy-start(f32[19]{0:T(128)} %heat.1) | copy-start | bytes 232
  20.0 1.0 %copy-start.15 = (f32[19]{0:T(128)S(1)}, f32[19]{0:T(128)}, u32[]{:S(2)}) copy-start(f32[19]{0:T(128)} %prefactor.1) | copy-start | bytes 232
  20.0 1.0 %copy-start.16 = (f32[19]{0:T(128)S(1)}, f32[19]{0:T(128)}, u32[]{:S(2)}) copy-start(f32[19]{0:T(128)} %energy.1) | copy-start | bytes 232
  20.0 2.8 %copy-start.12 = (f32[14]{0:T(128)S(1)}, f32[14]{0:T(128)}, u32[]{:S(2)}) copy-start(f32[14]{0:T(128)} %diff.1) | copy-start | bytes 172
  20.7 2.2 %copy-start.1 = (bf16[2,128,128]{2,1,0:T(8,128)(2,1)S(1)}, bf16[2,128,128]{2,1,0:T(8,128)(2,1)}, u32[]{:S(2)}) copy-start(bf16[2,128,128]{2,1,0:T(8,128)(2,1)} %constant.42.clone.dz.dx) | copy-start | bytes 196612
  20.7 2.2 %copy-start.2 = (bf16[2,128,128]{2,1,0:T(8,128)(2,1)S(1)}, bf16[2,128,128]{2,1,0:T(8,128)(2,1)}, u32[]{:S(2)}) copy-start(bf16[2,128,128]{2,1,0:T(8,128)(2,1)} %constant.41.clone.fz.fx) | copy-start | bytes 196612
  31.6 35.5 %copy-start.6 = (bf16[2,128,128]{2,1,0:T(8,128)(2,1)S(1)}, bf16[2,128,128]{2,1,0:T(8,128)(2,1)}, u32[]{:S(2)}) copy-start(bf16[2,128,128]{2,1,0:T(8,128)(2,1)} %constant.49.clone.dxt) | copy-start | bytes 196612
  31.6 35.5 %copy-start.7 = (bf16[2,128,128]{2,1,0:T(8,128)(2,1)S(1)}, bf16[2,128,128]{2,1,0:T(8,128)(2,1)}, u32[]{:S(2)}) copy-start(bf16[2,128,128]{2,1,0:T(8,128)(2,1)} %constant.48.clone.fxt) | copy-start | bytes 196612
  31.6 35.5 %copy-start.8 = (f32[128,1]{1,0:T(8,128)S(1)}, f32[128,1]{1,0:T(8,128)}, u32[]{:S(2)}) copy-start(f32[128,1]{1,0:T(8,128)} %constant.46.clone.kx2) | copy-start | bytes 1540
  31.6 35.5 %copy-start.11 = (f32[1,256]{1,0:T(1,128)S(1)}, f32[1,256]{1,0:T(1,128)}, u32[]{:S(2)}) copy-start(f32[1,256]{1,0:T(1,128)} %constant.47.clone.ky2) | copy-start | bytes 3076
  31.6 35.5 %copy-start.13 = (f32[128]{0:T(128)S(1)}, f32[128]{0:T(128)}, u32[]{:S(2)}) copy-start(f32[128]{0:T(128)} %constant.43.clone.kz2) | copy-start | bytes 1540
  57.1 10.0 %copy-start.3 = (bf16[2,4,256,128]{3,2,1,0:T(8,128)(2,1)S(1)}, bf16[2,4,256,128]{3,2,1,0:T(8,128)(2,1)}, u32[]{:S(2)}) copy-start(bf16[2,4,256,128]{3,2,1,0:T(8,128)(2,1)} %constant.45.clone.back) | copy-start | bytes 1572868
  57.1 10.0 %copy-start.4 = (bf16[2,4,128,256]{3,2,1,0:T(8,128)(2,1)S(1)}, bf16[2,4,128,256]{3,2,1,0:T(8,128)(2,1)}, u32[]{:S(2)}) copy-start(bf16[2,4,128,256]{3,2,1,0:T(8,128)(2,1)} %constant.44.clone.forth) | copy-start | bytes 1572868

commit v3 on v2

v3 whole, which is shorter than its diff:
```python
import functools

import jax
import jax.numpy as jnp
import numpy as np
from jax import lax
from jax.experimental import pallas as pl
from jax.experimental.pallas import tpu as pltpu
from jax.sharding import Mesh
from jax.sharding import PartitionSpec as P

GX = ("y", "c")
GY = ("z", "x")
MODES = ("y", "c", "z")

NSPEC = 9
NREAC = 19
NS = NSPEC + 1
NF = 14
NX = 128
NY = 256
NZ = 128
CX = 8
CY = 8
COLS = CX * CY
CAP = COLS // 2
DT = 0.25
PRECISE = lax.Precision.HIGHEST
F32 = jnp.float32
VMEM = pl.BlockSpec(memory_space=pltpu.VMEM)
LIMIT = 32 * 1024 * 1024


def basis(n):
    j = np.arange(n)
    h = n // 2
    f = np.zeros((n, n))
    k = np.zeros(n)
    f[0] = 1.0 / np.sqrt(n)
    f[h] = (-1.0) ** j / np.sqrt(n)
    for m in range(1, h):
        f[m] = np.sqrt(2.0 / n) * np.cos(2 * np.pi * (m * j % n) / n)
        f[h + m] = np.sqrt(2.0 / n) * np.sin(2 * np.pi * (m * j % n) / n)
        k[m] = k[h + m] = 2 * np.pi * m / n
    d = np.zeros((n, n))
    for m in range(1, h):
        d[m] = k[m] * f[h + m]
        d[h + m] = -k[m] * f[m]
    return f, d, k


def dot(a, b, dims=((1,), (0,))):
    return lax.dot_general(a, b, (dims, ((), ())), precision=PRECISE, preferred_element_type=F32)


def parts(v):
    hi = v.astype(jnp.bfloat16)
    return hi, (v - hi.astype(F32)).astype(jnp.bfloat16)


def dot3(a, b, dims=((1,), (0,))):
    one = lambda p, q: lax.dot_general(p, q, (dims, ((), ())), preferred_element_type=F32)
    return one(a[0], b[0]) + (one(a[0], b[1]) + one(a[1], b[0]))


OFF = 3
ROWS = 16
FORM = 40
MAIN = 16
REST = NREAC - MAIN
GROUPS = 4
WIDE = GROUPS * 3 * ROWS


def one_hot(shape, f):
    r = lax.broadcasted_iota(jnp.int32, shape, 0)
    c = lax.broadcasted_iota(jnp.int32, shape, 1)
    return f(r, c).astype(F32)


def spread(block, height, width, copies, low):
    every = jnp.concatenate([block] * copies, axis=0)
    r = lax.broadcasted_iota(jnp.int32, every.shape, 0)
    c = lax.broadcasted_iota(jnp.int32, every.shape, 1)
    hi, lo = parts(jnp.where(r // height == c // width, every, 0.0))
    return jnp.where(c % width < low, hi.astype(F32), lo.astype(F32)).astype(jnp.bfloat16)


def form_weights(left_t, right_t):
    tn = ((1,), (1,))
    pick_l = one_hot((FORM, NREAC), lambda r, c: r == c + jnp.where(c < MAIN, 0, MAIN))
    pick_r = one_hot((FORM, NREAC), lambda r, c: r == c + jnp.where(c < MAIN, MAIN, MAIN + REST))
    w = dot(pick_l, left_t, tn) + dot(pick_r, right_t, tn)
    w = dot(w, one_hot((NSPEC, WIDE), lambda r, c: c % ROWS == r + OFF))
    return spread(w, FORM, 3 * ROWS, GROUPS, 2 * ROWS)


def update_weights(stoich_t, heat, prefactor, newton):
    both = dot(one_hot((NS, NSPEC), lambda r, c: r == c), stoich_t)
    both = both + one_hot((NS, NREAC), lambda r, c: r == NSPEC) * heat
    msa = dot(newton, both) * (0.5 * prefactor)
    v = dot(msa, one_hot((NREAC, 192), lambda r, c: c % 32 == r))
    v = v - dot(newton, one_hot((NS, 192), lambda r, c: c % 32 == r + NREAC))
    v = dot(one_hot((ROWS, NS), lambda r, c: r == c + OFF), v)
    return spread(v, ROWS, 96, 2, 64)


def column_plan(cls):
    pick_x = one_hot((COLS, CX), lambda r, c: r // CY == c)
    pick_y = one_hot((COLS, CY), lambda r, c: r % CY == c)
    class_col = jnp.sum(dot(pick_x, cls) * pick_y, axis=1, keepdims=True)
    rows = dot(cls, pick_y, ((1,), (1,)))
    class_row = jnp.sum(one_hot((CX, COLS), lambda r, c: c // CY == r) * rows, axis=0, keepdims=True)
    ii = lax.broadcasted_iota(jnp.int32, (COLS, COLS), 0).astype(F32)
    jj = lax.broadcasted_iota(jnp.int32, (COLS, COLS), 1).astype(F32)
    rank_col = jnp.sum((class_row * COLS - jj > class_col * COLS - ii).astype(F32), axis=1, keepdims=True)
    at = (rank_col == jj).astype(F32)
    order = jnp.sum(at * ii, axis=0, keepdims=True)
    sorted_class = jnp.sum(at * class_col, axis=0, keepdims=True)
    table = jnp.concatenate([order, class_row, sorted_class, jnp.zeros((5, COLS), F32)], axis=0)
    return jnp.concatenate([table, jnp.zeros_like(table)], axis=1).astype(jnp.int32)


def step_of(c):
    return jnp.where(c == 1, DT, jnp.where(c == 2, DT / 2, jnp.where(c == 3, DT / 3, DT / 4)))


def substep(cols, steps, forms, update, energy):
    per = len(cols) // GROUPS
    wide = per * NZ
    z0 = [jnp.concatenate(cols[g * per : (g + 1) * per], axis=1) for g in range(GROUPS)]
    h = [
        jnp.concatenate([jnp.full((1, NZ), 1.0, F32) * steps[g * per + i] for i in range(per)], axis=1)
        for g in range(GROUPS)
    ]
    top = lax.broadcasted_iota(jnp.int32, (8, wide), 0) < REST
    z = z0
    for repeat in range(3):
        stack = []
        for g in range(GROUPS):
            hi, lo = parts(z[g])
            stack += [hi, lo, hi]
        t = jnp.dot(forms, jnp.concatenate(stack, axis=0), preferred_element_type=F32)
        pairs = []
        for g in range(GROUPS):
            at = g * FORM
            heat = jnp.tanh(energy * z[g][OFF + NSPEC : OFF + NS])
            p = jnp.tanh(t[at : at + MAIN]) * jnp.tanh(t[at + MAIN : at + 2 * MAIN])
            p = (p + p * heat[:MAIN]) * h[g]
            q = jnp.tanh(t[at + 2 * MAIN : at + FORM])
            q = q * pltpu.roll(q, 8 - REST, 0)
            q = (q + q * heat[MAIN:]) * h[g]
            if repeat:
                d = z[g] - z0[g]
                x = jnp.concatenate([p, jnp.where(top, q, d[:8]), d[8:]], axis=0)
            else:
                zero = jnp.zeros((8, wide), F32)
                x = jnp.concatenate([p, jnp.where(top, q, zero), zero], axis=0)
            hi, lo = parts(x)
            pairs.append(jnp.concatenate([hi, lo, hi], axis=0))
        side = jnp.concatenate([jnp.concatenate(pairs[2 * k : 2 * k + 2], axis=0) for k in range(2)], axis=1)
        change = jnp.dot(update, side, preferred_element_type=F32)
        z = [
            z[g] + change[(g % 2) * ROWS : (g % 2 + 1) * ROWS, (g // 2) * wide : (g // 2 + 1) * wide]
            for g in range(GROUPS)
        ]
    return [z[k // per][:, (k % per) * NZ : (k % per + 1) * NZ] for k in range(len(cols))]


def halo_kernel(species, flow, last_x, first_x, last_y, first_y):
    for f in range(NF):
        src, at = (species, f) if f < NSPEC else (flow, f - NSPEC)
        last_x[f] = src[at, CX - 1]
        first_x[f] = src[at, 0]
        last_y[f] = src[at, :, CY - 1, :]
        first_y[f] = src[at, :, 0, :]


def react_kernel(
    species,
    flow,
    xlo,
    xhi,
    ylo,
    yhi,
    classes,
    diff,
    left_t,
    right_t,
    stoich_t,
    heat,
    prefactor,
    energy,
    newton,
    fz,
    dz,
    species_out,
    flow_mid,
    spectra,
    state,
    temp0,
    buf,
    table,
    plan,
    burnt,
    sems,
):
    table[...] = column_plan(classes[...].astype(F32))
    to_scalar = pltpu.make_async_copy(table, plan, sems.at[0])
    to_scalar.start()
    forms = form_weights(left_t[...], right_t[...])
    update = update_weights(stoich_t[...], heat[...], prefactor[...], newton[...])
    at_e = one_hot((MAIN + 8, NREAC), lambda r, c: r == c)
    energy_col = jnp.sum(at_e * (0.5 * energy[...]), axis=1, keepdims=True)

    ysub = lax.broadcasted_iota(jnp.int32, (CY, NZ), 0)
    half = [0.5 * flow[c] for c in (1, 2, 3)]

    def transport(f, field):
        coef = diff[:, f : f + 1].reshape(1, 1, 1)
        ahead_x = jnp.concatenate([field[1:], xhi[f][None]], axis=0)
        behind_x = jnp.concatenate([xlo[f][None], field[:-1]], axis=0)
        up = pltpu.roll(field, CY - 1, 1)
        down = pltpu.roll(field, 1, 1)
        ahead_y = jnp.stack([jnp.where(ysub == CY - 1, yhi[f, x : x + 1, :], up[x]) for x in range(CX)])
        behind_y = jnp.stack([jnp.where(ysub == 0, ylo[f, x : x + 1, :], down[x]) for x in range(CX)])
        ahead_z = pltpu.roll(field, NZ - 1, 2)
        behind_z = pltpu.roll(field, 1, 2)
        lap = (ahead_x + behind_x) + (ahead_y + behind_y) + (ahead_z + behind_z) - 6.0 * field
        adv = (
            half[0] * (ahead_x - behind_x)
            + half[1] * (ahead_y - behind_y)
            + half[2] * (ahead_z - behind_z)
        )
        return field + DT * (coef * lap - adv)

    zero = jnp.zeros((COLS, NZ), F32)
    for row in list(range(OFF)) + list(range(OFF + NS, ROWS)):
        state[:, row, :] = zero
    for f in range(NF):
        field = species[f] if f < NSPEC else flow[f - NSPEC]
        moved = transport(f, field)
        if f < NSPEC:
            state[:, OFF + f, :] = moved.reshape(COLS, NZ)
        elif f == NF - 1:
            state[:, OFF + NSPEC, :] = moved.reshape(COLS, NZ)
            temp0[...] = moved.reshape(COLS, NZ)
        else:
            flow_mid[f - NSPEC] = moved

    to_scalar.wait()
    steps = [step_of(plan[1, k]) for k in range(COLS)]
    done = substep([state[k] for k in range(COLS)], steps, forms, update, energy_col)
    for k in range(COLS):
        state[k] = done[k]

    for k in range(CAP):
        buf[k] = state[plan[0, k]]

    def some(count, s):
        kinds = [plan[2, k] for k in range(count)]
        cols = [buf[k] for k in range(count)]
        done = substep(cols, [step_of(c) for c in kinds], forms, update, energy_col)
        for k in range(count):
            buf[k] = jnp.where(kinds[k] > s, done[k], cols[k])

    def section(s, _):
        many = plan[2, CAP // 2] > s

        @pl.when(many)
        def _():
            some(CAP, s)

        @pl.when(jnp.logical_and(jnp.logical_not(many), plan[2, 0] > s))
        def _():
            some(CAP // 2, s)

        return 0

    lax.fori_loop(1, 4, section, 0)

    for k in range(CAP):
        state[plan[0, k]] = buf[k]
    for i in range(NSPEC):
        burnt[i] = state[:, OFF + i, :].reshape(CX, CY, NZ)
    to_out = pltpu.make_async_copy(burnt, species_out, sems.at[1])
    to_out.start()
    last = state[:, OFF + NSPEC, :]
    flow_mid[4] = last.reshape(CX, CY, NZ)
    source = (last - temp0[...]) * (1.0 / DT)
    nt = ((1,), (1,))
    horizontal = flow_mid[1:3].reshape(2 * COLS, NZ)
    fz2, dz2 = (fz[0], fz[1]), (dz[0], dz[1])
    spectra[:, 0, :] = dot3(fz2, parts(horizontal), nt)
    vertical = flow_mid[3].reshape(COLS, NZ)
    third = dot3(dz2, parts(vertical), nt) - dot3(fz2, parts(source), nt)
    spectra[:, 1, :] = jnp.concatenate([third, jnp.zeros_like(third)], axis=1)
    to_out.wait()


def swap_blocks(v):
    rows, lanes = v.shape
    r = lax.broadcasted_iota(jnp.int32, v.shape, 0)
    k = lax.broadcasted_iota(jnp.int32, v.shape, 1) // 8
    for b in (1, 2, 4):
        low_r, low_k = (r & b) == 0, (k & b) == 0
        from_above = pltpu.roll(pltpu.roll(v, b, 0), lanes - 8 * b, 1)
        from_below = pltpu.roll(pltpu.roll(v, rows - b, 0), 8 * b, 1)
        v = jnp.where(low_r == low_k, v, jnp.where(low_r, from_below, from_above))
    return v


def stream_kernel(got, fx, dx, out):
    a = swap_blocks(got[:, 0, :])
    w = swap_blocks(got[:, 1, :])
    upper = lax.broadcasted_iota(jnp.int32, a.shape, 1) < COLS
    fx2, dx2 = (fx[0], fx[1]), (dx[0], dx[1])
    moved = jnp.where(upper, w, a)
    both = dot3(fx2, parts(moved)) + jnp.where(upper, dot3(dx2, parts(a)), 0.0)
    for i in range(4):
        out[i] = both


def solve_kernel(place, got, forth, back, kx2, ky2, fxt, dxt, out):
    full = None
    for i in range(4):
        term = dot3(parts(got[i]), (forth[0, i], forth[1, i]))
        full = term if full is None else full + term
    mode = (place[:, 0:1] % (NZ // 2)).astype(F32) * (2 * np.pi / NZ)
    k2 = kx2[...] + ky2[...] + mode * mode
    mine = jnp.max(place[:, 1:2])
    q = full / jnp.where(k2 > 0, k2, 1.0)
    lines = parts(dot3(parts(q), (back[0, mine], back[1, mine])))
    first = dot3((fxt[0], fxt[1]), lines)
    second = dot3((dxt[0], dxt[1]), lines)
    out[:, 0, :] = swap_blocks(first)
    out[:, 1, :] = swap_blocks(second)


def finish_kernel(got, mid, fz, dz, out):
    fz2, dz2 = (fz[0], fz[1]), (dz[0], dz[1])
    first = parts(jnp.transpose(got[:, 0, :]))
    second = parts(jnp.transpose(got[:, 1, :]))
    a = dot3(second, fz2)[:COLS]
    b = dot3(first, fz2)[COLS:]
    c = dot3(first, dz2)[:COLS]
    out[0] = mid[0]
    out[1] = mid[1] + a.reshape(CX, CY, NZ)
    out[2] = mid[2] + b.reshape(CX, CY, NZ)
    out[3] = mid[3] - c.reshape(CX, CY, NZ)
    out[4] = mid[4]


def call(kernel, out_shapes, n_in, scratch=(), out_specs=None):
    out = [jax.ShapeDtypeStruct(s, F32) for s in out_shapes]
    one = len(out) == 1
    return pl.pallas_call(
        kernel,
        out_shape=out[0] if one else out,
        in_specs=[VMEM] * n_in,
        out_specs=VMEM if one else out_specs or [VMEM] * len(out),
        scratch_shapes=list(scratch),
        compiler_params=pltpu.CompilerParams(vmem_limit_bytes=LIMIT),
    )


def react(fields, halos, classes, diffusivity, left, right, stoich, heat, prefactor, energy, newton, fz, dz):
    row = lambda v: v[None, :]
    return call(
        react_kernel,
        [(NSPEC, CX, CY, NZ), (5, CX, CY, NZ), (NZ, 2, 2 * COLS)],
        17,
        [
            pltpu.VMEM((COLS, ROWS, NZ), F32),
            pltpu.VMEM((COLS, NZ), F32),
            pltpu.VMEM((CAP, ROWS, NZ), F32),
            pltpu.VMEM((8, NZ), jnp.int32),
            pltpu.SMEM((8, NZ), jnp.int32),
            pltpu.VMEM((NSPEC, CX, CY, NZ), F32),
            pltpu.SemaphoreType.DMA((2,)),
        ],
        [pl.BlockSpec(memory_space=pl.ANY), VMEM, VMEM],
    )(
        *fields,
        *halos,
        classes,
        row(diffusivity),
        left.T,
        right.T,
        stoich.T,
        row(heat),
        row(prefactor),
        row(energy),
        newton,
        fz,
        dz,
    )


def ring(axes, n, step):
    return functools.partial(
        lax.ppermute, axis_name=axes, perm=[(i, (i + step) % n) for i in range(n)]
    )


def shards(
    species,
    flow,
    classes,
    diffusivity,
    left,
    right,
    stoich,
    heat,
    prefactor,
    energy,
    newton,
):
    n_gx, n_gy = NX // CX, NY // CY
    edges = call(halo_kernel, [(NF, 8, NZ)] * 4, 2)(species, flow)
    ylo = ring(GY, n_gy, 1)(edges[2])
    yhi = ring(GY, n_gy, -1)(edges[3])
    xlo = ring(GX, n_gx, 1)(edges[0])
    xhi = ring(GX, n_gx, -1)(edges[1])

    fz, dz, _ = basis(NZ)
    fy, dy, ky = basis(NY)
    fx, dx, kx = basis(NX)
    f32 = lambda v: np.ascontiguousarray(v, np.float32)

    def table(v):
        v = f32(v)
        hi = v.astype(jnp.bfloat16)
        return np.stack([hi, (v - hi.astype(np.float32)).astype(jnp.bfloat16)])

    y_of = ((np.arange(8)[None, :, None] * 4 + np.arange(4)[:, None, None]) * CY + np.arange(CY)).reshape(4, COLS)
    forth = np.stack([np.concatenate([fy[:, y].T, dy[:, y].T], axis=0) for y in y_of])
    back = np.stack([np.concatenate([fy[:, y], -dy[:, y]], axis=1) for y in y_of])

    species_out, mid, spectra = react(
        (species, flow),
        (xlo, xhi, ylo, yhi),
        classes,
        diffusivity,
        left,
        right,
        stoich,
        heat,
        prefactor,
        energy,
        newton,
        table(fz),
        table(dz),
    )
    place = jnp.stack([lax.axis_index(MODES), lax.axis_index("x")]).astype(jnp.int32)[None, :]
    spectra, place = lax.optimization_barrier((spectra, place))
    got = lax.all_to_all(spectra, MODES, 0, 0, tiled=True)
    lines = call(stream_kernel, [(4, NX, 2 * COLS)], 3)(got, table(fx), table(dx))
    lines = lax.all_to_all(lines, "x", 0, 0, tiled=True)
    grads = call(solve_kernel, [(NX, 2, 2 * COLS)], 8)(
        place,
        lines,
        table(forth),
        table(back),
        f32(kx * kx)[:, None],
        f32(ky * ky)[None, :],
        table(fx.T),
        table(-dx.T),
    )
    got = lax.all_to_all(grads, MODES, 0, 0, tiled=True)
    flow_out = call(finish_kernel, [(5, CX, CY, NZ)], 4)(got, mid, table(fz), table(dz))
    return (species_out, flow_out)


def solution(mesh):
    finer = Mesh(mesh.devices.reshape(8, 2, 8, 4), GX + GY)
    return jax.shard_map(
        shards,
        mesh=finer,
        in_specs=(P(None, GX, GY, None), P(None, GX, GY, None), P(GX, GY)) + (P(),) * 8,
        out_specs=(P(None, GX, GY, None), P(None, GX, GY, None)),
        check_vma=False,
    )
```

time: 89.1 us -> 89.4 us (level)
  Pallas kernels: 13.6 us -> 10.4 us
  blocking collectives: 53.9 us -> 55.4 us
  waiting for transfers between devices: 0.01 us -> 1.03 us
  local copies, waits for them, and re-layouts: 2.7 us -> 3.66 us
    pallas_call x5, Pallas kernels: 13.6 us -> 10.4 us  [the longest x1 7.74 us: react(): call(react_kernel, [(NSPEC, CX, CY, NZ), (5, CX, CY, NZ), (NZ, 2, 2 * COL...]
    unnamed x43 -> x46, local copies, waits for them, and re-layouts: 1 us -> 3.66 us
    squeeze x2 -> x0, local copies, waits for them, and re-layouts: 1.62 us -> none  [shards(): fields = lambda *at: jnp.concatenate([species[at], flow[at]], axis=0)]
    all_to_all x1, blocking collectives: 25.5 us -> 26.6 us  [shards(): got = lax.all_to_all(spectra, MODES, 0, 0, tiled=True)]
    ppermute x4, waiting for transfers between devices: 0.01 us -> 1.03 us  [the longest x1 1.03 us: shards(): yhi = ring(GY, n_gy, -1)(edges[3])]
  transfers between devices with their start and end apart: 4 -> 4, of which waited for: 0 -> 1; matrix products, arithmetic and copies ran while one was open for 1% -> 0% of each run, Pallas kernels for 2% -> 0%
where the time goes in v3:
time: 89.4 us; the launch traced here: 89 us
  blocking collectives  55.4 us (62%)
  starting transfers between devices  17.5 us (20%)
  Pallas kernels  10.4 us (12%)
  local copies, waits for them, and re-layouts  3.66 us (4%)
  waiting for transfers between devices  1.03 us (1%)
  between operations  0.92 us (1%)
    all_to_all x1, blocking collectives, shards(): got = lax.all_to_all(spectra, MODES, 0, 0, tiled=True)  26.6 us
    all_to_all x1, blocking collectives, shards(): got = lax.all_to_all(grads, MODES, 0, 0, tiled=True)  19.1 us
    all_to_all x1, blocking collectives, shards(): lines = lax.all_to_all(lines, 'x', 0, 0, tiled=True)  9.72 us
    ppermute x1, starting transfers between devices, shards(): yhi = ring(GY, n_gy, -1)(edges[3])  8.65 us
    pallas_call x1, Pallas kernels, react(): call(react_kernel, [(NSPEC, CX, CY, NZ), (5, CX, CY, NZ), (NZ, 2, 2 * COL...  7.74 us
    ppermute x1, starting transfers between devices, shards(): xhi = ring(GX, n_gx, -1)(edges[1])  4.22 us
    unnamed x46, local copies, waits for them, and re-layouts  3.66 us
    ppermute x1, starting transfers between devices, shards(): xlo = ring(GX, n_gx, 1)(edges[0])  2.7 us
  transfers between devices with their start and end apart: 4, of which 1 were waited for; matrix products, arithmetic and copies ran while one was open for 0% of the time, Pallas kernels for 0%

profile of v3, /device:TPU:1, one launch (start us, length us, event | category | flops | bytes accessed | tf_op | source)
XLA Modules:
  0.0 89.0 jit_solution(15772284701347700163)
XLA Ops:
  0.6 0.0 copy-start
  0.6 1.0 %copy-done = f32[9,8,8,128]{3,2,1,0:T(8,128)S(1)} copy-done((f32[9,8,8,128]{3,2,1,0:T(8,128)S(1)}, f32[9,8,8,128]{3,2,1,0:T(8,128)}, u32[]{:S(2)}) %copy-start) | copy-done | bytes 294936
  1.6 0.9 %copy-done.2 = f32[5,8,8,128]{3,2,1,0:T(8,128)S(1)} copy-done((f32[5,8,8,128]{3,2,1,0:T(8,128)S(1)}, f32[5,8,8,128]{3,2,1,0:T(8,128)}, u32[]{:S(2)}) %copy-start.2) | copy-done | bytes 163864
  2.5 0.1 shard_map.230
  2.6 2.7 %collective-permute-start = (f32[14,8,128]{2,1,0:T(8,128)S(1)}, f32[14,8,128]{2,1,0:T(8,128)S(1)}, u32[]{:S(2)}, u32[]{:S(2)}) collective-permute-start(f32[14,8,128]{2,1,0:T(8,128)S(1)} %get-tuple-element.11), channel_id=1, source_target_pairs={{0,32},{32,64},{64,96},{96,128},{128,160},{160,192},{192,224},{224... | collective-permute-start | bytes 172040 | tf_op jit(solution)/shard_map/ppermute | solution.py:423
  5.3 4.2 %collective-permute-start.1 = (f32[14,8,128]{2,1,0:T(8,128)S(1)}, f32[14,8,128]{2,1,0:T(8,128)S(1)}, u32[]{:S(2)}, u32[]{:S(2)}) collective-permute-start(f32[14,8,128]{2,1,0:T(8,128)S(1)} %get-tuple-element.12), channel_id=1, source_target_pairs={{0,480},{32,0},{64,32},{96,64},{128,96},{160,128},{192,160},{224,1... | collective-permute-start | bytes 172040 | tf_op jit(solution)/shard_map/ppermute | solution.py:424
  9.5 1.9 %collective-permute-start.2 = (f32[14,8,128]{2,1,0:T(8,128)S(1)}, f32[14,8,128]{2,1,0:T(8,128)S(1)}, u32[]{:S(2)}, u32[]{:S(2)}) collective-permute-start(f32[14,8,128]{2,1,0:T(8,128)S(1)} %get-tuple-element.13), channel_id=1, source_target_pairs={{0,1},{1,2},{2,3},{3,4},{4,5},{5,6},{6,7},{7,8},{8,9},{9,10},{10,1... | collective-permute-start | bytes 172040 | tf_op jit(solution)/shard_map/ppermute | solution.py:421
  11.4 8.6 %collective-permute-start.3 = (f32[14,8,128]{2,1,0:T(8,128)S(1)}, f32[14,8,128]{2,1,0:T(8,128)S(1)}, u32[]{:S(2)}, u32[]{:S(2)}) collective-permute-start(f32[14,8,128]{2,1,0:T(8,128)S(1)} %get-tuple-element.14), channel_id=1, source_target_pairs={{0,31},{1,0},{2,1},{3,2},{4,3},{5,4},{6,5},{7,6},{8,7},{9,8},{10,9... | collective-permute-start | bytes 172040 | tf_op jit(solution)/shard_map/ppermute | solution.py:422
  20.1 0.0 copy-start.17
  20.1 0.0 copy-start.19
  20.1 0.0 copy-start.20
  20.1 0.0 copy-start.21
  20.1 0.0 copy-start.22
  20.1 0.0 copy-start.16
  20.2 0.0 copy-start.15
  20.2 0.0 copy-start.14
  20.2 0.0 copy-start.13
  20.2 0.1 add_bitcast_fusion.place
  20.3 0.0 collective-permute-done.xlo
  20.3 0.0 collective-permute-done.1.xhi
  20.3 0.0 collective-permute-done.2.ylo
  20.3 1.0 %collective-permute-done.3.yhi = f32[14,8,128]{2,1,0:T(8,128)S(1)} collective-permute-done((f32[14,8,128]{2,1,0:T(8,128)S(1)}, f32[14,8,128]{2,1,0:T(8,128)S(1)}, u32[]{:S(2)}, u32[]{:S(2)}) %collective-permute-start.3) | collective-permute-done | bytes 57376 | tf_op jit(solution)/shard_map/ppermute | solution.py:422
  21.3 0.0 copy-done.1
  21.3 0.0 copy-done.3
  21.3 0.0 copy-done.17
  21.3 0.0 copy-done.19
  21.3 0.0 copy-done.20
  21.3 0.0 copy-done.21
  21.4 0.0 copy-start.4
  21.4 0.8 copy-done.4
  22.2 0.8 copy-done.6
  23.1 7.7 %shard_map.231 = (f32[9,8,8,128]{3,2,1,0:T(8,128)}, f32[5,8,8,128]{3,2,1,0:T(8,128)S(1)}, f32[128,2,128]{2,1,0:T(2,128)S(1)}) custom-call(f32[9,8,8,128]{3,2,1,0:T(8,128)S(1)} %copy-done.1, f32[5,8,8,128]{3,2,1,0:T(8,128)S(1)} %copy-done.3, f32[14,8,128]{2,1,0:T(8,128)S(1)} %collective-permute-done.xlo, f32[14,8,128]{2,1,0:T(8,128)S(1)} %collective-permute-done.1.xhi, ...), custom_call_target="tpu_custom_call" | custom-call | tf_op jit(solution)/shard_map/pallas_call | solution.py:369
  30.8 0.0 copy-start.10
  30.8 0.0 copy-start.11
  30.8 0.0 copy-start.12
  30.9 0.0 copy-start.18
  30.9 26.6 %all_to_all.15.got = f32[128,2,128]{2,1,0:T(2,128)S(1)} all-to-all(f32[128,2,128]{2,1,0:T(2,128)S(1)} %get-tuple-element.18), channel_id=1, replica_groups=mesh['y'=8,'c'=2,'z'=8,'x'=4] {'y','c','z'}, dimensions={0} | all-to-all | bytes 262144 | tf_op jit(solution)/shard_map/all_to_all | solution.py:457
  57.5 0.5 shard_map.232
  58.0 9.7 %all_to_all.16.got = f32[4,128,128]{2,1,0:T(8,128)S(1)} all-to-all(f32[4,128,128]{2,1,0:T(8,128)S(1)} %shard_map.232), channel_id=1, replica_groups=mesh['y'=8,'c'=2,'z'=8,'x'=4] {'x'}, dimensions={0} | all-to-all | bytes 524288 | tf_op jit(solution)/shard_map/all_to_all | solution.py:459
  67.7 0.0 copy-done.18
  67.7 0.0 copy-done.8
  67.7 0.0 copy-done.9
  67.8 1.1 %shard_map.233 = f32[128,2,128]{2,1,0:T(2,128)S(1)} custom-call(s32[1,2]{1,0:T(1,128)S(1)} %add_bitcast_fusion.place, f32[4,128,128]{2,1,0:T(8,128)S(1)} %all_to_all.16.got, bf16[2,4,128,256]{3,2,1,0:T(8,128)(2,1)S(1)} %copy-done.9, bf16[2,4,256,128]{3,2,1,0:T(8,128)(2,1)S(1)} %copy-done.8, f32[128,1]{1,0:T(8,128)S(1)} %copy-done.12, ...), custom_call_target="tpu_custom_call" | custom-call | tf_op jit(solution)/shard_map/pallas_call | solution.py:460
  68.9 0.0 copy-start.5
  68.9 0.0 copy-start.7
  68.9 19.1 %all_to_all.17.got = f32[128,2,128]{2,1,0:T(2,128)S(1)} all-to-all(f32[128,2,128]{2,1,0:T(2,128)S(1)} %shard_map.233), channel_id=1, replica_groups=mesh['y'=8,'c'=2,'z'=8,'x'=4] {'y','c','z'}, dimensions={0} | all-to-all | bytes 262144 | tf_op jit(solution)/shard_map/all_to_all | solution.py:470
  88.0 0.0 copy-done.7
  88.0 1.0 %shard_map.234 = f32[5,8,8,128]{3,2,1,0:T(8,128)} custom-call(f32[128,2,128]{2,1,0:T(2,128)S(1)} %all_to_all.17.got, f32[5,8,8,128]{3,2,1,0:T(8,128)S(1)} %get-tuple-element.19.mid, bf16[2,128,128]{2,1,0:T(8,128)(2,1)S(1)} %copy-done.7, bf16[2,128,128]{2,1,0:T(8,128)(2,1)S(1)} %copy-done.5), custom_call_target="tpu_custom_call" | custom-call | tf_op jit(solution)/shard_map/pallas_call | solution.py:471
  (15 shorter events, 0.0 us)
Async XLA Ops:
  0.6 1.0 %copy-start = (f32[9,8,8,128]{3,2,1,0:T(8,128)S(1)}, f32[9,8,8,128]{3,2,1,0:T(8,128)}, u32[]{:S(2)}) copy-start(f32[9,8,8,128]{3,2,1,0:T(8,128)} %species.3) | copy-start | bytes 884740
  1.6 0.9 %copy-start.2 = (f32[5,8,8,128]{3,2,1,0:T(8,128)S(1)}, f32[5,8,8,128]{3,2,1,0:T(8,128)}, u32[]{:S(2)}) copy-start(f32[5,8,8,128]{3,2,1,0:T(8,128)} %flow.3) | copy-start | bytes 491524
  2.5 18.8 %copy-start.1 = (f32[9,8,8,128]{3,2,1,0:T(8,128)S(1)}, f32[9,8,8,128]{3,2,1,0:T(8,128)}, u32[]{:S(2)}) copy-start(f32[9,8,8,128]{3,2,1,0:T(8,128)} %species.3) | copy-start | bytes 884740
  2.5 18.8 %copy-start.3 = (f32[5,8,8,128]{3,2,1,0:T(8,128)S(1)}, f32[5,8,8,128]{3,2,1,0:T(8,128)}, u32[]{:S(2)}) copy-start(f32[5,8,8,128]{3,2,1,0:T(8,128)} %flow.3) | copy-start | bytes 491524
  2.6 17.7 %collective-permute-start = (f32[14,8,128]{2,1,0:T(8,128)S(1)}, f32[14,8,128]{2,1,0:T(8,128)S(1)}, u32[]{:S(2)}, u32[]{:S(2)}) collective-permute-start(f32[14,8,128]{2,1,0:T(8,128)S(1)} %get-tuple-element.11), channel_id=1, source_target_pairs={{0,32},{32,64},{64,96},{96,128},{128,160},{160,192},{192,224},{224... | collective-permute-start | bytes 172040 | tf_op jit(solution)/shard_map/ppermute | solution.py:423
  5.3 15.0 %collective-permute-start.1 = (f32[14,8,128]{2,1,0:T(8,128)S(1)}, f32[14,8,128]{2,1,0:T(8,128)S(1)}, u32[]{:S(2)}, u32[]{:S(2)}) collective-permute-start(f32[14,8,128]{2,1,0:T(8,128)S(1)} %get-tuple-element.12), channel_id=1, source_target_pairs={{0,480},{32,0},{64,32},{96,64},{128,96},{160,128},{192,160},{224,1... | collective-permute-start | bytes 172040 | tf_op jit(solution)/shard_map/ppermute | solution.py:424
  9.5 10.8 %collective-permute-start.2 = (f32[14,8,128]{2,1,0:T(8,128)S(1)}, f32[14,8,128]{2,1,0:T(8,128)S(1)}, u32[]{:S(2)}, u32[]{:S(2)}) collective-permute-start(f32[14,8,128]{2,1,0:T(8,128)S(1)} %get-tuple-element.13), channel_id=1, source_target_pairs={{0,1},{1,2},{2,3},{3,4},{4,5},{5,6},{6,7},{7,8},{8,9},{9,10},{10,1... | collective-permute-start | bytes 172040 | tf_op jit(solution)/shard_map/ppermute | solution.py:421
  11.4 9.9 %collective-permute-start.3 = (f32[14,8,128]{2,1,0:T(8,128)S(1)}, f32[14,8,128]{2,1,0:T(8,128)S(1)}, u32[]{:S(2)}, u32[]{:S(2)}) collective-permute-start(f32[14,8,128]{2,1,0:T(8,128)S(1)} %get-tuple-element.14), channel_id=1, source_target_pairs={{0,31},{1,0},{2,1},{3,2},{4,3},{5,4},{6,5},{7,6},{8,7},{9,8},{10,9... | collective-permute-start | bytes 172040 | tf_op jit(solution)/shard_map/ppermute | solution.py:422
  20.1 1.2 %copy-start.17 = (s32[8,8]{1,0:T(8,128)S(1)}, s32[8,8]{1,0:T(8,128)}, u32[]{:S(2)}) copy-start(s32[8,8]{1,0:T(8,128)} %classes.1) | copy-start | bytes 772
  20.1 1.2 %copy-start.19 = (f32[14]{0:T(128)S(1)}, f32[14]{0:T(128)}, u32[]{:S(2)}) copy-start(f32[14]{0:T(128)} %param.26) | copy-start | bytes 172
  20.1 1.2 %copy-start.20 = (f32[19]{0:T(128)S(1)}, f32[19]{0:T(128)}, u32[]{:S(2)}) copy-start(f32[19]{0:T(128)} %param.30) | copy-start | bytes 232
  20.1 1.2 %copy-start.21 = (f32[19]{0:T(128)S(1)}, f32[19]{0:T(128)}, u32[]{:S(2)}) copy-start(f32[19]{0:T(128)} %param.31) | copy-start | bytes 232
  20.1 1.2 %copy-start.22 = (f32[19]{0:T(128)S(1)}, f32[19]{0:T(128)}, u32[]{:S(2)}) copy-start(f32[19]{0:T(128)} %param.32) | copy-start | bytes 232
  20.1 1.2 %copy-start.16 = (f32[10,10]{1,0:T(8,128)S(1)}, f32[10,10]{1,0:T(8,128)}, u32[]{:S(2)}) copy-start(f32[10,10]{1,0:T(8,128)} %newton.1) | copy-start | bytes 1204
  20.2 1.2 %copy-start.15 = (f32[19,9]{0,1:T(8,128)S(1)}, f32[19,9]{0,1:T(8,128)}, u32[]{:S(2)}) copy-start(f32[19,9]{0,1:T(8,128)} %param.29) | copy-start | bytes 2056
  20.2 1.2 %copy-start.14 = (f32[19,9]{0,1:T(8,128)S(1)}, f32[19,9]{0,1:T(8,128)}, u32[]{:S(2)}) copy-start(f32[19,9]{0,1:T(8,128)} %param.28) | copy-start | bytes 2056
  20.2 1.2 %copy-start.13 = (f32[19,9]{0,1:T(8,128)S(1)}, f32[19,9]{0,1:T(8,128)}, u32[]{:S(2)}) copy-start(f32[19,9]{0,1:T(8,128)} %param.27) | copy-start | bytes 2056
  21.4 0.8 copy-start.4
  22.2 0.8 copy-start.6
  30.8 36.9 %copy-start.10 = (bf16[2,128,128]{2,1,0:T(8,128)(2,1)S(1)}, bf16[2,128,128]{2,1,0:T(8,128)(2,1)}, u32[]{:S(2)}) copy-start(bf16[2,128,128]{2,1,0:T(8,128)(2,1)} %constant.46.clone.dxt) | copy-start | bytes 196612
  30.8 36.9 %copy-start.11 = (bf16[2,128,128]{2,1,0:T(8,128)(2,1)S(1)}, bf16[2,128,128]{2,1,0:T(8,128)(2,1)}, u32[]{:S(2)}) copy-start(bf16[2,128,128]{2,1,0:T(8,128)(2,1)} %constant.45.clone.fxt) | copy-start | bytes 196612
  30.8 36.9 %copy-start.12 = (f32[128,1]{1,0:T(8,128)S(1)}, f32[128,1]{1,0:T(8,128)}, u32[]{:S(2)}) copy-start(f32[128,1]{1,0:T(8,128)} %constant.43.clone.kx2) | copy-start | bytes 1540
  30.9 36.9 %copy-start.18 = (f32[1,256]{1,0:T(1,128)S(1)}, f32[1,256]{1,0:T(1,128)}, u32[]{:S(2)}) copy-start(f32[1,256]{1,0:T(1,128)} %constant.44.clone.ky2) | copy-start | bytes 3076
  57.5 10.3 %copy-start.8 = (bf16[2,4,256,128]{3,2,1,0:T(8,128)(2,1)S(1)}, bf16[2,4,256,128]{3,2,1,0:T(8,128)(2,1)}, u32[]{:S(2)}) copy-start(bf16[2,4,256,128]{3,2,1,0:T(8,128)(2,1)} %constant.42.clone.back) | copy-start | bytes 1572868
  57.5 10.3 %copy-start.9 = (bf16[2,4,128,256]{3,2,1,0:T(8,128)(2,1)S(1)}, bf16[2,4,128,256]{3,2,1,0:T(8,128)(2,1)}, u32[]{:S(2)}) copy-start(bf16[2,4,128,256]{3,2,1,0:T(8,128)(2,1)} %constant.41.clone.forth) | copy-start | bytes 1572868
  68.9 19.1 %copy-start.5 = (bf16[2,128,128]{2,1,0:T(8,128)(2,1)S(1)}, bf16[2,128,128]{2,1,0:T(8,128)(2,1)}, u32[]{:S(2)}) copy-start(bf16[2,128,128]{2,1,0:T(8,128)(2,1)} %constant.40.clone.dz.dx) | copy-start | bytes 196612
  68.9 19.1 %copy-start.7 = (bf16[2,128,128]{2,1,0:T(8,128)(2,1)S(1)}, bf16[2,128,128]{2,1,0:T(8,128)(2,1)}, u32[]{:S(2)}) copy-start(bf16[2,128,128]{2,1,0:T(8,128)(2,1)} %constant.39.clone.fz.fx) | copy-start | bytes 196612

commit v4 on v3

--- a/solution.py
+++ b/solution.py
@@ -28,6 +28,7 @@
 PRECISE = lax.Precision.HIGHEST
 F32 = jnp.float32
 VMEM = pl.BlockSpec(memory_space=pltpu.VMEM)
+HBM = pl.BlockSpec(memory_space=pltpu.HBM)
 LIMIT = 32 * 1024 * 1024
 
 
@@ -167,13 +168,32 @@
     return [z[k // per][:, (k % per) * NZ : (k % per + 1) * NZ] for k in range(len(cols))]
 
 
-def halo_kernel(species, flow, last_x, first_x, last_y, first_y):
+def halo_kernel(species, flow, last_x, first_x, last_y, first_y, own_s, own_f, sems):
+    copies = [
+        pltpu.make_async_copy(species, own_s, sems.at[0]),
+        pltpu.make_async_copy(flow, own_f, sems.at[1]),
+    ]
+    for c in copies:
+        c.start()
+    for c in copies:
+        c.wait()
     for f in range(NF):
-        src, at = (species, f) if f < NSPEC else (flow, f - NSPEC)
+        src, at = (own_s, f) if f < NSPEC else (own_f, f - NSPEC)
         last_x[f] = src[at, CX - 1]
         first_x[f] = src[at, 0]
         last_y[f] = src[at, :, CY - 1, :]
         first_y[f] = src[at, :, 0, :]
+
+
+def weights_kernel(classes, left_t, right_t, stoich_t, heat, prefactor, energy, newton, diffusivity, forms, update, energy_col, diff, table):
+    table[...] = column_plan(classes[...].astype(F32))
+    forms[...] = form_weights(left_t[...], right_t[...])
+    update[...] = update_weights(stoich_t[...], heat[...], prefactor[...], newton[...])
+    at_e = one_hot((MAIN + 8, NREAC), lambda r, c: r == c)
+    col = jnp.sum(at_e * (0.5 * energy[...]), axis=1, keepdims=True)
+    energy_col[...] = jnp.broadcast_to(col, (MAIN + 8, NZ))
+    col = jnp.sum(one_hot((16, NF), lambda r, c: r == c) * diffusivity[...], axis=1, keepdims=True)
+    diff[...] = jnp.broadcast_to(col, (16, NZ))
 
 
 def react_kernel(
@@ -183,41 +203,36 @@
     xhi,
     ylo,
     yhi,
-    classes,
+    forms,
+    update,
+    energy_col,
     diff,
-    left_t,
-    right_t,
-    stoich_t,
-    heat,
-    prefactor,
-    energy,
-    newton,
-    fz,
-    dz,
+    table,
+    fz_far,
+    dz_far,
     species_out,
     flow_mid,
     spectra,
     state,
     temp0,
     buf,
-    table,
     plan,
     burnt,
+    fz,
+    dz,
     sems,
 ):
-    table[...] = column_plan(classes[...].astype(F32))
     to_scalar = pltpu.make_async_copy(table, plan, sems.at[0])
     to_scalar.start()
-    forms = form_weights(left_t[...], right_t[...])
-    update = update_weights(stoich_t[...], heat[...], prefactor[...], newton[...])
-    at_e = one_hot((MAIN + 8, NREAC), lambda r, c: r == c)
-    energy_col = jnp.sum(at_e * (0.5 * energy[...]), axis=1, keepdims=True)
+    near = [pltpu.make_async_copy(fz_far, fz, sems.at[2]), pltpu.make_async_copy(dz_far, dz, sems.at[3])]
+    for c in near:
+        c.start()
 
     ysub = lax.broadcasted_iota(jnp.int32, (CY, NZ), 0)
     half = [0.5 * flow[c] for c in (1, 2, 3)]
 
     def transport(f, field):
-        coef = diff[:, f : f + 1].reshape(1, 1, 1)
+        coef = diff[f : f + 1, :]
         ahead_x = jnp.concatenate([field[1:], xhi[f][None]], axis=0)
         behind_x = jnp.concatenate([xlo[f][None], field[:-1]], axis=0)
         up = pltpu.roll(field, CY - 1, 1)
@@ -250,7 +265,7 @@
 
     to_scalar.wait()
     steps = [step_of(plan[1, k]) for k in range(COLS)]
-    done = substep([state[k] for k in range(COLS)], steps, forms, update, energy_col)
+    done = substep([state[k] for k in range(COLS)], steps, forms[...], update[...], energy_col[:, 0:1])
     for k in range(COLS):
         state[k] = done[k]
 
@@ -260,7 +275,7 @@
     def some(count, s):
         kinds = [plan[2, k] for k in range(count)]
         cols = [buf[k] for k in range(count)]
-        done = substep(cols, [step_of(c) for c in kinds], forms, update, energy_col)
+        done = substep(cols, [step_of(c) for c in kinds], forms[...], update[...], energy_col[:, 0:1])
         for k in range(count):
             buf[k] = jnp.where(kinds[k] > s, done[k], cols[k])
 
@@ -288,6 +303,8 @@
     last = state[:, OFF + NSPEC, :]
     flow_mid[4] = last.reshape(CX, CY, NZ)
     source = (last - temp0[...]) * (1.0 / DT)
+    for c in near:
+        c.wait()
     nt = ((1,), (1,))
     horizontal = flow_mid[1:3].reshape(2 * COLS, NZ)
     fz2, dz2 = (fz[0], fz[1]), (dz[0], dz[1])
@@ -351,13 +368,18 @@
     out[4] = mid[4]
 
 
-def call(kernel, out_shapes, n_in, scratch=(), out_specs=None):
-    out = [jax.ShapeDtypeStruct(s, F32) for s in out_shapes]
+def far(v):
+    return pltpu.with_memory_space_constraint(jnp.asarray(v), pltpu.HBM)
+
+
+def call(kernel, out_shapes, in_specs, scratch=(), out_specs=None):
+    pairs = [v if isinstance(v[0], tuple) else (v, F32) for v in out_shapes]
+    out = [jax.ShapeDtypeStruct(*v) for v in pairs]
     one = len(out) == 1
     return pl.pallas_call(
         kernel,
         out_shape=out[0] if one else out,
-        in_specs=[VMEM] * n_in,
+        in_specs=[VMEM] * in_specs if isinstance(in_specs, int) else in_specs,
         out_specs=VMEM if one else out_specs or [VMEM] * len(out),
         scratch_shapes=list(scratch),
         compiler_params=pltpu.CompilerParams(vmem_limit_bytes=LIMIT),
@@ -366,35 +388,34 @@
 
 def react(fields, halos, classes, diffusivity, left, right, stoich, heat, prefactor, energy, newton, fz, dz):
     row = lambda v: v[None, :]
+    bf16 = jnp.bfloat16
+    weights = call(
+        weights_kernel,
+        [
+            ((GROUPS * FORM, WIDE), bf16),
+            ((2 * ROWS, 192), bf16),
+            ((MAIN + 8, NZ), F32),
+            ((16, NZ), F32),
+            ((8, NZ), jnp.int32),
+        ],
+        9,
+    )(classes, left.T, right.T, stoich.T, row(heat), row(prefactor), row(energy), newton, row(diffusivity))
     return call(
         react_kernel,
         [(NSPEC, CX, CY, NZ), (5, CX, CY, NZ), (NZ, 2, 2 * COLS)],
-        17,
+        [VMEM] * 11 + [HBM] * 2,
         [
             pltpu.VMEM((COLS, ROWS, NZ), F32),
             pltpu.VMEM((COLS, NZ), F32),
             pltpu.VMEM((CAP, ROWS, NZ), F32),
-            pltpu.VMEM((8, NZ), jnp.int32),
             pltpu.SMEM((8, NZ), jnp.int32),
             pltpu.VMEM((NSPEC, CX, CY, NZ), F32),
-            pltpu.SemaphoreType.DMA((2,)),
+            pltpu.VMEM((2, NZ, NZ), bf16),
+            pltpu.VMEM((2, NZ, NZ), bf16),
+            pltpu.SemaphoreType.DMA((4,)),
         ],
-        [pl.BlockSpec(memory_space=pl.ANY), VMEM, VMEM],
-    )(
-        *fields,
-        *halos,
-        classes,
-        row(diffusivity),
-        left.T,
-        right.T,
-        stoich.T,
-        row(heat),
-        row(prefactor),
-        row(energy),
-        newton,
-        fz,
-        dz,
-    )
+        [HBM, VMEM, VMEM],
+    )(*fields, *halos, *weights, far(fz), far(dz))
 
 
 def ring(axes, n, step):
@@ -417,7 +438,16 @@
     newton,
 ):
     n_gx, n_gy = NX // CX, NY // CY
-    edges = call(halo_kernel, [(NF, 8, NZ)] * 4, 2)(species, flow)
+    edges = call(
+        halo_kernel,
+        [(NF, 8, NZ)] * 4,
+        [HBM] * 2,
+        [
+            pltpu.VMEM((NSPEC, CX, CY, NZ), F32),
+            pltpu.VMEM((5, CX, CY, NZ), F32),
+            pltpu.SemaphoreType.DMA((2,)),
+        ],
+    )(far(species), far(flow))
     ylo = ring(GY, n_gy, 1)(edges[2])
     yhi = ring(GY, n_gy, -1)(edges[3])
     xlo = ring(GX, n_gx, 1)(edges[0])

time: 89.4 us -> 86.5 us (0.968)
  local copies, waits for them, and re-layouts: 3.66 us -> 0.8 us
  Pallas kernels: 10.4 us -> 11.8 us
  waiting for transfers between devices: 1.03 us -> 0.01 us
    unnamed x46 -> x38, local copies, waits for them, and re-layouts: 3.66 us -> 0.8 us
    pallas_call x1 -> x2, Pallas kernels: 0.07 us -> 2.1 us  [the longest x1 1.14 us: shards(): call(halo_kernel, [(NF, 8, NZ)] * 4, [HBM] * 2, [pltpu.VMEM((NSPEC, CX, C...]
    ppermute x1, waiting for transfers between devices: 1.03 us -> 0.01 us  [shards(): yhi = ring(GY, n_gy, -1)(edges[3])]
  transfers between devices with their start and end apart: 4 -> 4, of which waited for: 1 -> 0; matrix products, arithmetic and copies ran while one was open for 0% -> 0% of each run, Pallas kernels for 0% -> 1%
where the time goes in v4:
time: 86.5 us; the launch traced here: 86.1 us
  blocking collectives  55.1 us (64%)
  starting transfers between devices  17.5 us (20%)
  Pallas kernels  11.8 us (14%)
  between operations  0.9 us (1%)
    all_to_all x1, blocking collectives, shards(): got = lax.all_to_all(spectra, MODES, 0, 0, tiled=True)  26 us
    all_to_all x1, blocking collectives, shards(): got = lax.all_to_all(grads, MODES, 0, 0, tiled=True)  18.9 us
    all_to_all x1, blocking collectives, shards(): lines = lax.all_to_all(lines, 'x', 0, 0, tiled=True)  10.1 us
    ppermute x1, starting transfers between devices, shards(): yhi = ring(GY, n_gy, -1)(edges[3])  8.65 us
    pallas_call x1, Pallas kernels, react(): call(react_kernel, [(NSPEC, CX, CY, NZ), (5, CX, CY, NZ), (NZ, 2, 2 * COL...  7.08 us
    ppermute x1, starting transfers between devices, shards(): xhi = ring(GX, n_gx, -1)(edges[1])  4.22 us
    ppermute x1, starting transfers between devices, shards(): xlo = ring(GX, n_gx, 1)(edges[0])  2.7 us
    ppermute x1, starting transfers between devices, shards(): ylo = ring(GY, n_gy, 1)(edges[2])  1.91 us
  transfers between devices with their start and end apart: 4, of which 0 were waited for; matrix products, arithmetic and copies ran while one was open for 0% of the time, Pallas kernels for 1%

profile of v4, /device:TPU:1, one launch (start us, length us, event | category | flops | bytes accessed | tf_op | source)
XLA Modules:
  0.0 86.1 jit_solution(1999005491525221069)
XLA Ops:
  0.6 0.0 copy-start
  0.6 0.0 copy-start.1
  0.6 1.1 %shard_map.230 = (f32[14,8,128]{2,1,0:T(8,128)S(1)}, f32[14,8,128]{2,1,0:T(8,128)S(1)}, f32[14,8,128]{2,1,0:T(8,128)S(1)}, f32[14,8,128]{2,1,0:T(8,128)S(1)}) custom-call(f32[9,8,8,128]{3,2,1,0:T(8,128)} %species.3, f32[5,8,8,128]{3,2,1,0:T(8,128)} %flow.3), custom_call_target="tpu_custom_call" | custom-call | tf_op jit(solution)/shard_map/pallas_call | solution.py:441
  1.8 2.7 %collective-permute-start = (f32[14,8,128]{2,1,0:T(8,128)S(1)}, f32[14,8,128]{2,1,0:T(8,128)S(1)}, u32[]{:S(2)}, u32[]{:S(2)}) collective-permute-start(f32[14,8,128]{2,1,0:T(8,128)S(1)} %get-tuple-element.16), channel_id=1, source_target_pairs={{0,32},{32,64},{64,96},{96,128},{128,160},{160,192},{192,224},{224... | collective-permute-start | bytes 172040 | tf_op jit(solution)/shard_map/ppermute | solution.py:453
  4.5 4.2 %collective-permute-start.1 = (f32[14,8,128]{2,1,0:T(8,128)S(1)}, f32[14,8,128]{2,1,0:T(8,128)S(1)}, u32[]{:S(2)}, u32[]{:S(2)}) collective-permute-start(f32[14,8,128]{2,1,0:T(8,128)S(1)} %get-tuple-element.17), channel_id=1, source_target_pairs={{0,480},{32,0},{64,32},{96,64},{128,96},{160,128},{192,160},{224,1... | collective-permute-start | bytes 172040 | tf_op jit(solution)/shard_map/ppermute | solution.py:454
  8.7 1.9 %collective-permute-start.2 = (f32[14,8,128]{2,1,0:T(8,128)S(1)}, f32[14,8,128]{2,1,0:T(8,128)S(1)}, u32[]{:S(2)}, u32[]{:S(2)}) collective-permute-start(f32[14,8,128]{2,1,0:T(8,128)S(1)} %get-tuple-element.18), channel_id=1, source_target_pairs={{0,1},{1,2},{2,3},{3,4},{4,5},{5,6},{6,7},{7,8},{8,9},{9,10},{10,1... | collective-permute-start | bytes 172040 | tf_op jit(solution)/shard_map/ppermute | solution.py:451
  10.6 8.7 %collective-permute-start.3 = (f32[14,8,128]{2,1,0:T(8,128)S(1)}, f32[14,8,128]{2,1,0:T(8,128)S(1)}, u32[]{:S(2)}, u32[]{:S(2)}) collective-permute-start(f32[14,8,128]{2,1,0:T(8,128)S(1)} %get-tuple-element.19), channel_id=1, source_target_pairs={{0,31},{1,0},{2,1},{3,2},{4,3},{5,4},{6,5},{7,6},{8,7},{9,8},{10,9... | collective-permute-start | bytes 172040 | tf_op jit(solution)/shard_map/ppermute | solution.py:452
  19.3 0.0 copy-start.13
  19.3 0.0 copy-start.15
  19.3 0.0 copy-start.16
  19.3 0.0 copy-start.17
  19.3 0.0 copy-start.18
  19.4 0.0 copy-start.12
  19.4 0.0 copy-start.11
  19.4 0.0 copy-start.10
  19.4 0.0 copy-start.9
  19.4 0.6 copy-done.13
  20.0 0.0 copy-done.15
  20.0 0.0 copy-done.16
  20.0 0.0 copy-done.17
  20.0 0.0 copy-done.18
  20.0 0.1 copy-done.12
  20.1 0.0 copy-done.11
  20.1 0.0 copy-done.10
  20.1 0.0 copy-done.9
  20.1 1.0 %shard_map.231 = (bf16[160,192]{1,0:T(8,128)(2,1)S(1)}, bf16[32,192]{1,0:T(8,128)(2,1)S(1)}, f32[24,128]{1,0:T(8,128)S(1)}, f32[16,128]{1,0:T(8,128)S(1)}, s32[8,128]{1,0:T(8,128)S(1)}) custom-call(s32[8,8]{1,0:T(8,128)S(1)} %copy-done.13, f32[9,19]{1,0:T(8,128)S(1)} %bitcast.11, f32[9,19]{1,0:T(8,128)S(1)} %bitcast.12, f32[9,19]{1,0:T(8,128)S(1)} %bitcast.13, ...), custom_call_target="tpu_custom_call" | custom-call | tf_op jit(solution)/shard_map/pallas_call | solution.py:392
  21.1 0.1 add_bitcast_fusion.place
  21.2 0.0 collective-permute-done.xlo
  21.2 0.0 collective-permute-done.1.xhi
  21.2 0.0 collective-permute-done.2.ylo
  21.2 0.0 collective-permute-done.3.yhi
  21.2 0.0 copy-done
  21.2 0.0 copy-done.1
  21.2 0.0 copy-start.8
  21.2 0.0 copy-start.14
  21.2 7.1 %shard_map.232 = (f32[9,8,8,128]{3,2,1,0:T(8,128)}, f32[5,8,8,128]{3,2,1,0:T(8,128)S(1)}, f32[128,2,128]{2,1,0:T(2,128)S(1)}) custom-call(f32[9,8,8,128]{3,2,1,0:T(8,128)S(1)} %copy-done, f32[5,8,8,128]{3,2,1,0:T(8,128)S(1)} %copy-done.1, f32[14,8,128]{2,1,0:T(8,128)S(1)} %collective-permute-done.xlo, f32[14,8,128]{2,1,0:T(8,128)S(1)} %collective-permute-done.1.xhi, ...), custom_call_target="tpu_custom_call" | custom-call | tf_op jit(solution)/shard_map/pallas_call | solution.py:403
  28.3 0.0 copy-start.2
  28.3 0.0 copy-start.3
  28.4 0.0 copy-start.6
  28.4 0.0 copy-start.7
  28.4 26.0 %all_to_all.15.got = f32[128,2,128]{2,1,0:T(2,128)S(1)} all-to-all(f32[128,2,128]{2,1,0:T(2,128)S(1)} %get-tuple-element.28), channel_id=1, replica_groups=mesh['y'=8,'c'=2,'z'=8,'x'=4] {'y','c','z'}, dimensions={0} | all-to-all | bytes 262144 | tf_op jit(solution)/shard_map/all_to_all | solution.py:487
  54.4 0.0 copy-done.3
  54.4 0.5 shard_map.233
  54.9 10.1 %all_to_all.16.got = f32[4,128,128]{2,1,0:T(8,128)S(1)} all-to-all(f32[4,128,128]{2,1,0:T(8,128)S(1)} %shard_map.233), channel_id=1, replica_groups=mesh['y'=8,'c'=2,'z'=8,'x'=4] {'x'}, dimensions={0} | all-to-all | bytes 524288 | tf_op jit(solution)/shard_map/all_to_all | solution.py:489
  65.0 0.0 copy-done.14
  65.1 1.1 %shard_map.234 = f32[128,2,128]{2,1,0:T(2,128)S(1)} custom-call(s32[1,2]{1,0:T(1,128)S(1)} %add_bitcast_fusion.place, f32[4,128,128]{2,1,0:T(8,128)S(1)} %all_to_all.16.got, bf16[2,4,128,256]{3,2,1,0:T(8,128)(2,1)S(1)} %copy-done.5, bf16[2,4,256,128]{3,2,1,0:T(8,128)(2,1)S(1)} %copy-done.4, f32[128,1]{1,0:T(8,128)S(1)} %copy-done.8, ...), custom_call_target="tpu_custom_call" | custom-call | tf_op jit(solution)/shard_map/pallas_call | solution.py:490
  66.2 18.9 %all_to_all.17.got = f32[128,2,128]{2,1,0:T(2,128)S(1)} all-to-all(f32[128,2,128]{2,1,0:T(2,128)S(1)} %shard_map.234), channel_id=1, replica_groups=mesh['y'=8,'c'=2,'z'=8,'x'=4] {'y','c','z'}, dimensions={0} | all-to-all | bytes 262144 | tf_op jit(solution)/shard_map/all_to_all | solution.py:500
  85.1 1.0 %shard_map.235 = f32[5,8,8,128]{3,2,1,0:T(8,128)} custom-call(f32[128,2,128]{2,1,0:T(2,128)S(1)} %all_to_all.17.got, f32[5,8,8,128]{3,2,1,0:T(8,128)S(1)} %get-tuple-element.29.mid, bf16[2,128,128]{2,1,0:T(8,128)(2,1)S(1)} %copy-done.3, bf16[2,128,128]{2,1,0:T(8,128)(2,1)S(1)} %copy-done.2), custom_call_target="tpu_custom_call" | custom-call | tf_op jit(solution)/shard_map/pallas_call | solution.py:501
  (8 shorter events, 0.0 us)
Async XLA Ops:
  0.6 20.6 %copy-start = (f32[9,8,8,128]{3,2,1,0:T(8,128)S(1)}, f32[9,8,8,128]{3,2,1,0:T(8,128)}, u32[]{:S(2)}) copy-start(f32[9,8,8,128]{3,2,1,0:T(8,128)} %species.3) | copy-start | bytes 884740
  0.6 20.6 %copy-start.1 = (f32[5,8,8,128]{3,2,1,0:T(8,128)S(1)}, f32[5,8,8,128]{3,2,1,0:T(8,128)}, u32[]{:S(2)}) copy-start(f32[5,8,8,128]{3,2,1,0:T(8,128)} %flow.3) | copy-start | bytes 491524
  1.8 19.4 %collective-permute-start = (f32[14,8,128]{2,1,0:T(8,128)S(1)}, f32[14,8,128]{2,1,0:T(8,128)S(1)}, u32[]{:S(2)}, u32[]{:S(2)}) collective-permute-start(f32[14,8,128]{2,1,0:T(8,128)S(1)} %get-tuple-element.16), channel_id=1, source_target_pairs={{0,32},{32,64},{64,96},{96,128},{128,160},{160,192},{192,224},{224... | collective-permute-start | bytes 172040 | tf_op jit(solution)/shard_map/ppermute | solution.py:453
  4.5 16.7 %collective-permute-start.1 = (f32[14,8,128]{2,1,0:T(8,128)S(1)}, f32[14,8,128]{2,1,0:T(8,128)S(1)}, u32[]{:S(2)}, u32[]{:S(2)}) collective-permute-start(f32[14,8,128]{2,1,0:T(8,128)S(1)} %get-tuple-element.17), channel_id=1, source_target_pairs={{0,480},{32,0},{64,32},{96,64},{128,96},{160,128},{192,160},{224,1... | collective-permute-start | bytes 172040 | tf_op jit(solution)/shard_map/ppermute | solution.py:454
  8.7 12.5 %collective-permute-start.2 = (f32[14,8,128]{2,1,0:T(8,128)S(1)}, f32[14,8,128]{2,1,0:T(8,128)S(1)}, u32[]{:S(2)}, u32[]{:S(2)}) collective-permute-start(f32[14,8,128]{2,1,0:T(8,128)S(1)} %get-tuple-element.18), channel_id=1, source_target_pairs={{0,1},{1,2},{2,3},{3,4},{4,5},{5,6},{6,7},{7,8},{8,9},{9,10},{10,1... | collective-permute-start | bytes 172040 | tf_op jit(solution)/shard_map/ppermute | solution.py:451
  10.6 10.6 %collective-permute-start.3 = (f32[14,8,128]{2,1,0:T(8,128)S(1)}, f32[14,8,128]{2,1,0:T(8,128)S(1)}, u32[]{:S(2)}, u32[]{:S(2)}) collective-permute-start(f32[14,8,128]{2,1,0:T(8,128)S(1)} %get-tuple-element.19), channel_id=1, source_target_pairs={{0,31},{1,0},{2,1},{3,2},{4,3},{5,4},{6,5},{7,6},{8,7},{9,8},{10,9... | collective-permute-start | bytes 172040 | tf_op jit(solution)/shard_map/ppermute | solution.py:452
  19.3 0.7 copy-start.13
  19.3 0.7 copy-start.15
  19.3 0.7 copy-start.16
  19.3 0.7 copy-start.17
  19.3 0.7 copy-start.18
  19.4 0.7 copy-start.12
  19.4 0.7 copy-start.11
  19.4 0.7 copy-start.10
  19.4 0.7 copy-start.9
  21.2 43.8 %copy-start.8 = (f32[128,1]{1,0:T(8,128)S(1)}, f32[128,1]{1,0:T(8,128)}, u32[]{:S(2)}) copy-start(f32[128,1]{1,0:T(8,128)} %constant.43.clone.kx2) | copy-start | bytes 1540
  21.2 43.8 %copy-start.14 = (f32[1,256]{1,0:T(1,128)S(1)}, f32[1,256]{1,0:T(1,128)}, u32[]{:S(2)}) copy-start(f32[1,256]{1,0:T(1,128)} %constant.44.clone.ky2) | copy-start | bytes 3076
  28.3 26.1 %copy-start.2 = (bf16[2,128,128]{2,1,0:T(8,128)(2,1)S(1)}, bf16[2,128,128]{2,1,0:T(8,128)(2,1)}, u32[]{:S(2)}) copy-start(bf16[2,128,128]{2,1,0:T(8,128)(2,1)} %constant.40.clone.dz_far.dx.dz) | copy-start | bytes 196612
  28.3 26.1 %copy-start.3 = (bf16[2,128,128]{2,1,0:T(8,128)(2,1)S(1)}, bf16[2,128,128]{2,1,0:T(8,128)(2,1)}, u32[]{:S(2)}) copy-start(bf16[2,128,128]{2,1,0:T(8,128)(2,1)} %constant.39.clone.fz_far.fx.fz) | copy-start | bytes 196612
  28.4 36.7 %copy-start.6 = (bf16[2,128,128]{2,1,0:T(8,128)(2,1)S(1)}, bf16[2,128,128]{2,1,0:T(8,128)(2,1)}, u32[]{:S(2)}) copy-start(bf16[2,128,128]{2,1,0:T(8,128)(2,1)} %constant.46.clone.dxt) | copy-start | bytes 196612
  28.4 36.7 %copy-start.7 = (bf16[2,128,128]{2,1,0:T(8,128)(2,1)S(1)}, bf16[2,128,128]{2,1,0:T(8,128)(2,1)}, u32[]{:S(2)}) copy-start(bf16[2,128,128]{2,1,0:T(8,128)(2,1)} %constant.45.clone.fxt) | copy-start | bytes 196612
  54.4 10.6 %copy-start.4 = (bf16[2,4,256,128]{3,2,1,0:T(8,128)(2,1)S(1)}, bf16[2,4,256,128]{3,2,1,0:T(8,128)(2,1)}, u32[]{:S(2)}) copy-start(bf16[2,4,256,128]{3,2,1,0:T(8,128)(2,1)} %constant.42.clone.back) | copy-start | bytes 1572868
  54.4 10.6 %copy-start.5 = (bf16[2,4,128,256]{3,2,1,0:T(8,128)(2,1)S(1)}, bf16[2,4,128,256]{3,2,1,0:T(8,128)(2,1)}, u32[]{:S(2)}) copy-start(bf16[2,4,128,256]{3,2,1,0:T(8,128)(2,1)} %constant.41.clone.forth) | copy-start | bytes 1572868

commit v5 on v4

--- a/solution.py
+++ b/solution.py
@@ -92,18 +92,19 @@
     pick_l = one_hot((FORM, NREAC), lambda r, c: r == c + jnp.where(c < MAIN, 0, MAIN))
     pick_r = one_hot((FORM, NREAC), lambda r, c: r == c + jnp.where(c < MAIN, MAIN, MAIN + REST))
     w = dot(pick_l, left_t, tn) + dot(pick_r, right_t, tn)
-    w = dot(w, one_hot((NSPEC, WIDE), lambda r, c: c % ROWS == r + OFF))
-    return spread(w, FORM, 3 * ROWS, GROUPS, 2 * ROWS)
-
-
-def update_weights(stoich_t, heat, prefactor, newton):
+    wide = dot(w, one_hot((NSPEC, WIDE), lambda r, c: c % ROWS == r + OFF))
+    return w, spread(wide, FORM, 3 * ROWS, GROUPS, 2 * ROWS)
+
+
+def update_weights(w, stoich_t, heat, prefactor, newton):
     both = dot(one_hot((NS, NSPEC), lambda r, c: r == c), stoich_t)
     both = both + one_hot((NS, NREAC), lambda r, c: r == NSPEC) * heat
     msa = dot(newton, both) * (0.5 * prefactor)
     v = dot(msa, one_hot((NREAC, 192), lambda r, c: c % 32 == r))
     v = v - dot(newton, one_hot((NS, 192), lambda r, c: c % 32 == r + NREAC))
-    v = dot(one_hot((ROWS, NS), lambda r, c: r == c + OFF), v)
-    return spread(v, ROWS, 96, 2, 64)
+    by_forms = dot(w, v[:NSPEC])
+    by_rows = dot(one_hot((ROWS, NS), lambda r, c: r == c + OFF), v)
+    return spread(jnp.concatenate([by_forms, by_rows], axis=0), FORM + ROWS, 96, 2, 64)
 
 
 def column_plan(cls):
@@ -126,29 +127,34 @@
     return jnp.where(c == 1, DT, jnp.where(c == 2, DT / 2, jnp.where(c == 3, DT / 3, DT / 4)))
 
 
-def substep(cols, steps, forms, update, energy):
+def joined(cols):
+    per = len(cols) // GROUPS
+    return [jnp.concatenate(cols[g * per : (g + 1) * per], axis=1) for g in range(GROUPS)]
+
+
+def all_forms(cols, forms):
+    stack = []
+    for z in joined(cols):
+        hi, lo = parts(z)
+        stack += [hi, lo, hi]
+    t = jnp.dot(forms, jnp.concatenate(stack, axis=0), preferred_element_type=F32)
+    return [t[g * FORM : (g + 1) * FORM] for g in range(GROUPS)]
+
+
+def substep(cols, a, steps, update, energy):
     per = len(cols) // GROUPS
     wide = per * NZ
-    z0 = [jnp.concatenate(cols[g * per : (g + 1) * per], axis=1) for g in range(GROUPS)]
-    h = [
-        jnp.concatenate([jnp.full((1, NZ), 1.0, F32) * steps[g * per + i] for i in range(per)], axis=1)
-        for g in range(GROUPS)
-    ]
+    z0 = joined(cols)
+    h = joined([jnp.full((1, NZ), 1.0, F32) * v for v in steps])
     top = lax.broadcasted_iota(jnp.int32, (8, wide), 0) < REST
     z = z0
     for repeat in range(3):
-        stack = []
-        for g in range(GROUPS):
-            hi, lo = parts(z[g])
-            stack += [hi, lo, hi]
-        t = jnp.dot(forms, jnp.concatenate(stack, axis=0), preferred_element_type=F32)
         pairs = []
         for g in range(GROUPS):
-            at = g * FORM
             heat = jnp.tanh(energy * z[g][OFF + NSPEC : OFF + NS])
-            p = jnp.tanh(t[at : at + MAIN]) * jnp.tanh(t[at + MAIN : at + 2 * MAIN])
+            p = jnp.tanh(a[g][:MAIN]) * jnp.tanh(a[g][MAIN : 2 * MAIN])
             p = (p + p * heat[:MAIN]) * h[g]
-            q = jnp.tanh(t[at + 2 * MAIN : at + FORM])
+            q = jnp.tanh(a[g][2 * MAIN :])
             q = q * pltpu.roll(q, 8 - REST, 0)
             q = (q + q * heat[MAIN:]) * h[g]
             if repeat:
@@ -161,11 +167,14 @@
             pairs.append(jnp.concatenate([hi, lo, hi], axis=0))
         side = jnp.concatenate([jnp.concatenate(pairs[2 * k : 2 * k + 2], axis=0) for k in range(2)], axis=1)
         change = jnp.dot(update, side, preferred_element_type=F32)
-        z = [
-            z[g] + change[(g % 2) * ROWS : (g % 2 + 1) * ROWS, (g // 2) * wide : (g // 2 + 1) * wide]
-            for g in range(GROUPS)
+        both = FORM + ROWS
+        part = [
+            change[(g % 2) * both : (g % 2 + 1) * both, (g // 2) * wide : (g // 2 + 1) * wide] for g in range(GROUPS)
         ]
-    return [z[k // per][:, (k % per) * NZ : (k % per + 1) * NZ] for k in range(len(cols))]
+        a = [a[g] + part[g][:FORM] for g in range(GROUPS)]
+        z = [z[g] + part[g][FORM:] for g in range(GROUPS)]
+    cut = lambda v: [v[k // per][:, (k % per) * NZ : (k % per + 1) * NZ] for k in range(len(cols))]
+    return cut(z), cut(a)
 
 
 def halo_kernel(species, flow, last_x, first_x, last_y, first_y, own_s, own_f, sems):
@@ -187,8 +196,8 @@
 
 def weights_kernel(classes, left_t, right_t, stoich_t, heat, prefactor, energy, newton, diffusivity, forms, update, energy_col, diff, table):
     table[...] = column_plan(classes[...].astype(F32))
-    forms[...] = form_weights(left_t[...], right_t[...])
-    update[...] = update_weights(stoich_t[...], heat[...], prefactor[...], newton[...])
+    w, forms[...] = form_weights(left_t[...], right_t[...])
+    update[...] = update_weights(w, stoich_t[...], heat[...], prefactor[...], newton[...])
     at_e = one_hot((MAIN + 8, NREAC), lambda r, c: r == c)
     col = jnp.sum(at_e * (0.5 * energy[...]), axis=1, keepdims=True)
     energy_col[...] = jnp.broadcast_to(col, (MAIN + 8, NZ))
@@ -199,10 +208,10 @@
 def react_kernel(
     species,
     flow,
+    ylo,
+    yhi,
     xlo,
     xhi,
-    ylo,
-    yhi,
     forms,
     update,
     energy_col,
@@ -216,6 +225,8 @@
     state,
     temp0,
     buf,
+    held,
+    buf_forms,
     plan,
     burnt,
     fz,
@@ -265,19 +276,24 @@
 
     to_scalar.wait()
     steps = [step_of(plan[1, k]) for k in range(COLS)]
-    done = substep([state[k] for k in range(COLS)], steps, forms[...], update[...], energy_col[:, 0:1])
+    cols = [state[k] for k in range(COLS)]
+    done, lines = substep(cols, all_forms(cols, forms[...]), steps, update[...], energy_col[:, 0:1])
     for k in range(COLS):
         state[k] = done[k]
+        held[k] = lines[k]
 
     for k in range(CAP):
         buf[k] = state[plan[0, k]]
+        buf_forms[k] = held[plan[0, k]]
 
     def some(count, s):
         kinds = [plan[2, k] for k in range(count)]
         cols = [buf[k] for k in range(count)]
-        done = substep(cols, [step_of(c) for c in kinds], forms[...], update[...], energy_col[:, 0:1])
+        olds = [buf_forms[k] for k in range(count)]
+        done, lines = substep(cols, joined(olds), [step_of(c) for c in kinds], update[...], energy_col[:, 0:1])
         for k in range(count):
             buf[k] = jnp.where(kinds[k] > s, done[k], cols[k])
+            buf_forms[k] = jnp.where(kinds[k] > s, lines[k], olds[k])
 
     def section(s, _):
         many = plan[2, CAP // 2] > s
@@ -393,7 +409,7 @@
         weights_kernel,
         [
             ((GROUPS * FORM, WIDE), bf16),
-            ((2 * ROWS, 192), bf16),
+            ((2 * (FORM + ROWS), 192), bf16),
             ((MAIN + 8, NZ), F32),
             ((16, NZ), F32),
             ((8, NZ), jnp.int32),
@@ -408,6 +424,8 @@
             pltpu.VMEM((COLS, ROWS, NZ), F32),
             pltpu.VMEM((COLS, NZ), F32),
             pltpu.VMEM((CAP, ROWS, NZ), F32),
+            pltpu.VMEM((COLS, FORM, NZ), F32),
+            pltpu.VMEM((CAP, FORM, NZ), F32),
             pltpu.SMEM((8, NZ), jnp.int32),
             pltpu.VMEM((NSPEC, CX, CY, NZ), F32),
             pltpu.VMEM((2, NZ, NZ), bf16),
@@ -469,7 +487,7 @@
 
     species_out, mid, spectra = react(
         (species, flow),
-        (xlo, xhi, ylo, yhi),
+        (ylo, yhi, xlo, xhi),
         classes,
         diffusivity,
         left,

time: 86.5 us -> 83.9 us (0.970)
  blocking collectives: 55.1 us -> 51.3 us
  waiting for transfers between devices: 0.01 us -> 1.67 us
    ppermute x1, starting transfers between devices: 4.22 us -> 0.01 us  [shards(): xhi = ring(GX, n_gx, -1)(edges[1])]
    ppermute x1, starting transfers between devices: 8.65 us -> 11.7 us  [shards(): yhi = ring(GY, n_gy, -1)(edges[3])]
    ppermute x1, starting transfers between devices: 1.91 us -> 3.95 us  [shards(): ylo = ring(GY, n_gy, 1)(edges[2])]
    all_to_all x1, blocking collectives: 26 us -> 24.1 us  [shards(): got = lax.all_to_all(spectra, MODES, 0, 0, tiled=True)]
    ppermute x1, waiting for transfers between devices: 0.01 us -> 1.66 us  [shards(): xhi = ring(GX, n_gx, -1)(edges[1])]
    all_to_all x1, blocking collectives: 10.1 us -> 8.86 us  [shards(): lines = lax.all_to_all(lines, 'x', 0, 0, tiled=True)]
  transfers between devices with their start and end apart: 4 -> 4, of which waited for: 0 -> 1; matrix products, arithmetic and copies ran while one was open for 0% -> 0% of each run, Pallas kernels for 1% -> 1%
where the time goes in v5:
time: 83.9 us; the launch traced here: 83.6 us
  blocking collectives  51.3 us (61%)
  starting transfers between devices  17.8 us (21%)
  Pallas kernels  11.1 us (13%)
  waiting for transfers between devices  1.67 us (2%)
  between operations  0.85 us (1%)
    all_to_all x1, blocking collectives, shards(): got = lax.all_to_all(spectra, MODES, 0, 0, tiled=True)  24.1 us
    all_to_all x1, blocking collectives, shards(): got = lax.all_to_all(grads, MODES, 0, 0, tiled=True)  18.3 us
    ppermute x1, starting transfers between devices, shards(): yhi = ring(GY, n_gy, -1)(edges[3])  11.7 us
    all_to_all x1, blocking collectives, shards(): lines = lax.all_to_all(lines, 'x', 0, 0, tiled=True)  8.86 us
    pallas_call x1, Pallas kernels, react(): call(react_kernel, [(NSPEC, CX, CY, NZ), (5, CX, CY, NZ), (NZ, 2, 2 * COL...  6.36 us
    ppermute x1, starting transfers between devices, shards(): ylo = ring(GY, n_gy, 1)(edges[2])  3.95 us
    ppermute x1, starting transfers between devices, shards(): xlo = ring(GX, n_gx, 1)(edges[0])  2.15 us
  transfers between devices with their start and end apart: 4, of which 1 were waited for; matrix products, arithmetic and copies ran while one was open for 0% of the time, Pallas kernels for 1%

profile of v5, /device:TPU:1, one launch (start us, length us, event | category | flops | bytes accessed | tf_op | source)
XLA Modules:
  0.0 83.6 jit_solution(7374200332712132517)
XLA Ops:
  0.6 0.0 copy-start
  0.6 0.0 copy-start.1
  0.6 1.1 %shard_map.230 = (f32[14,8,128]{2,1,0:T(8,128)S(1)}, f32[14,8,128]{2,1,0:T(8,128)S(1)}, f32[14,8,128]{2,1,0:T(8,128)S(1)}, f32[14,8,128]{2,1,0:T(8,128)S(1)}) custom-call(f32[9,8,8,128]{3,2,1,0:T(8,128)} %species.3, f32[5,8,8,128]{3,2,1,0:T(8,128)} %flow.3), custom_call_target="tpu_custom_call" | custom-call | tf_op jit(solution)/shard_map/pallas_call | solution.py:459
  1.8 3.9 %collective-permute-start = (f32[14,8,128]{2,1,0:T(8,128)S(1)}, f32[14,8,128]{2,1,0:T(8,128)S(1)}, u32[]{:S(2)}, u32[]{:S(2)}) collective-permute-start(f32[14,8,128]{2,1,0:T(8,128)S(1)} %get-tuple-element.16), channel_id=1, source_target_pairs={{0,1},{1,2},{2,3},{3,4},{4,5},{5,6},{6,7},{7,8},{8,9},{9,10},{10,1... | collective-permute-start | bytes 172040 | tf_op jit(solution)/shard_map/ppermute | solution.py:469
  5.8 11.7 %collective-permute-start.1 = (f32[14,8,128]{2,1,0:T(8,128)S(1)}, f32[14,8,128]{2,1,0:T(8,128)S(1)}, u32[]{:S(2)}, u32[]{:S(2)}) collective-permute-start(f32[14,8,128]{2,1,0:T(8,128)S(1)} %get-tuple-element.17), channel_id=1, source_target_pairs={{0,31},{1,0},{2,1},{3,2},{4,3},{5,4},{6,5},{7,6},{8,7},{9,8},{10,9... | collective-permute-start | bytes 172040 | tf_op jit(solution)/shard_map/ppermute | solution.py:470
  17.4 2.1 %collective-permute-start.2 = (f32[14,8,128]{2,1,0:T(8,128)S(1)}, f32[14,8,128]{2,1,0:T(8,128)S(1)}, u32[]{:S(2)}, u32[]{:S(2)}) collective-permute-start(f32[14,8,128]{2,1,0:T(8,128)S(1)} %get-tuple-element.18), channel_id=1, source_target_pairs={{0,32},{32,64},{64,96},{96,128},{128,160},{160,192},{192,224},{224... | collective-permute-start | bytes 172040 | tf_op jit(solution)/shard_map/ppermute | solution.py:471
  19.6 0.0 collective-permute-start.3
  19.6 0.0 copy-start.17
  19.6 0.0 copy-start.18
  19.6 0.0 copy-start.12
  19.6 0.0 copy-start.11
  19.6 0.0 copy-start.10
  19.7 0.0 copy-start.9
  19.7 0.6 copy-done.13
  20.3 0.0 copy-done.15
  20.3 0.0 copy-done.16
  20.3 0.0 copy-done.17
  20.3 0.0 copy-done.18
  20.3 0.1 copy-done.12
  20.4 0.0 copy-done.11
  20.4 0.0 copy-done.10
  20.4 0.0 copy-done.9
  20.4 1.0 %shard_map.231 = (bf16[160,192]{1,0:T(8,128)(2,1)S(1)}, bf16[112,192]{1,0:T(8,128)(2,1)S(1)}, f32[24,128]{1,0:T(8,128)S(1)}, f32[16,128]{1,0:T(8,128)S(1)}, s32[8,128]{1,0:T(8,128)S(1)}) custom-call(s32[8,8]{1,0:T(8,128)S(1)} %copy-done.13, f32[9,19]{1,0:T(8,128)S(1)} %bitcast.11, f32[9,19]{1,0:T(8,128)S(1)} %bitcast.12, f32[9,19]{1,0:T(8,128)S(1)} %bitcast.13, ...), custom_call_target="tpu_custom_call" | custom-call | tf_op jit(solution)/shard_map/pallas_call | solution.py:408
  21.4 0.1 add_bitcast_fusion.place
  21.5 0.0 collective-permute-done.ylo
  21.5 0.0 collective-permute-done.1.yhi
  21.5 0.0 collective-permute-done.2.xlo
  21.5 1.7 %collective-permute-done.3.xhi = f32[14,8,128]{2,1,0:T(8,128)S(1)} collective-permute-done((f32[14,8,128]{2,1,0:T(8,128)S(1)}, f32[14,8,128]{2,1,0:T(8,128)S(1)}, u32[]{:S(2)}, u32[]{:S(2)}) %collective-permute-start.3) | collective-permute-done | bytes 57376 | tf_op jit(solution)/shard_map/ppermute | solution.py:472
  23.2 0.0 copy-done
  23.2 0.0 copy-done.1
  23.2 6.4 %shard_map.232 = (f32[9,8,8,128]{3,2,1,0:T(8,128)}, f32[5,8,8,128]{3,2,1,0:T(8,128)S(1)}, f32[128,2,128]{2,1,0:T(2,128)S(1)}) custom-call(f32[9,8,8,128]{3,2,1,0:T(8,128)S(1)} %copy-done, f32[5,8,8,128]{3,2,1,0:T(8,128)S(1)} %copy-done.1, f32[14,8,128]{2,1,0:T(8,128)S(1)} %collective-permute-done.ylo, f32[14,8,128]{2,1,0:T(8,128)S(1)} %collective-permute-done.1.yhi, ...), custom_call_target="tpu_custom_call" | custom-call | tf_op jit(solution)/shard_map/pallas_call | solution.py:419
  29.6 0.0 copy-start.2
  29.6 0.0 copy-start.3
  29.6 0.0 copy-start.6
  29.6 0.0 copy-start.7
  29.6 24.1 %all_to_all.15.got = f32[128,2,128]{2,1,0:T(2,128)S(1)} all-to-all(f32[128,2,128]{2,1,0:T(2,128)S(1)} %get-tuple-element.28), channel_id=1, replica_groups=mesh['y'=8,'c'=2,'z'=8,'x'=4] {'y','c','z'}, dimensions={0} | all-to-all | bytes 262144 | tf_op jit(solution)/shard_map/all_to_all | solution.py:505
  53.7 0.0 copy-done.2
  53.7 0.0 copy-done.3
  53.7 0.5 shard_map.233
  54.2 8.9 %all_to_all.16.got = f32[4,128,128]{2,1,0:T(8,128)S(1)} all-to-all(f32[4,128,128]{2,1,0:T(8,128)S(1)} %shard_map.233), channel_id=1, replica_groups=mesh['y'=8,'c'=2,'z'=8,'x'=4] {'x'}, dimensions={0} | all-to-all | bytes 524288 | tf_op jit(solution)/shard_map/all_to_all | solution.py:507
  63.1 0.0 copy-done.8
  63.1 0.0 copy-done.14
  63.1 0.0 copy-done.7
  63.1 0.0 copy-done.4
  63.1 0.0 copy-done.5
  63.1 1.1 %shard_map.234 = f32[128,2,128]{2,1,0:T(2,128)S(1)} custom-call(s32[1,2]{1,0:T(1,128)S(1)} %add_bitcast_fusion.place, f32[4,128,128]{2,1,0:T(8,128)S(1)} %all_to_all.16.got, bf16[2,4,128,256]{3,2,1,0:T(8,128)(2,1)S(1)} %copy-done.5, bf16[2,4,256,128]{3,2,1,0:T(8,128)(2,1)S(1)} %copy-done.4, f32[128,1]{1,0:T(8,128)S(1)} %copy-done.8, ...), custom_call_target="tpu_custom_call" | custom-call | tf_op jit(solution)/shard_map/pallas_call | solution.py:508
  64.3 18.3 %all_to_all.17.got = f32[128,2,128]{2,1,0:T(2,128)S(1)} all-to-all(f32[128,2,128]{2,1,0:T(2,128)S(1)} %shard_map.234), channel_id=1, replica_groups=mesh['y'=8,'c'=2,'z'=8,'x'=4] {'y','c','z'}, dimensions={0} | all-to-all | bytes 262144 | tf_op jit(solution)/shard_map/all_to_all | solution.py:518
  82.6 1.0 %shard_map.235 = f32[5,8,8,128]{3,2,1,0:T(8,128)} custom-call(f32[128,2,128]{2,1,0:T(2,128)S(1)} %all_to_all.17.got, f32[5,8,8,128]{3,2,1,0:T(8,128)S(1)} %get-tuple-element.29.mid, bf16[2,128,128]{2,1,0:T(8,128)(2,1)S(1)} %copy-done.3, bf16[2,128,128]{2,1,0:T(8,128)(2,1)S(1)} %copy-done.2), custom_call_target="tpu_custom_call" | custom-call | tf_op jit(solution)/shard_map/pallas_call | solution.py:519
  (8 shorter events, 0.0 us)
Async XLA Ops:
  0.6 22.6 %copy-start = (f32[9,8,8,128]{3,2,1,0:T(8,128)S(1)}, f32[9,8,8,128]{3,2,1,0:T(8,128)}, u32[]{:S(2)}) copy-start(f32[9,8,8,128]{3,2,1,0:T(8,128)} %species.3) | copy-start | bytes 884740
  0.6 22.5 %copy-start.1 = (f32[5,8,8,128]{3,2,1,0:T(8,128)S(1)}, f32[5,8,8,128]{3,2,1,0:T(8,128)}, u32[]{:S(2)}) copy-start(f32[5,8,8,128]{3,2,1,0:T(8,128)} %flow.3) | copy-start | bytes 491524
  1.8 19.7 %collective-permute-start = (f32[14,8,128]{2,1,0:T(8,128)S(1)}, f32[14,8,128]{2,1,0:T(8,128)S(1)}, u32[]{:S(2)}, u32[]{:S(2)}) collective-permute-start(f32[14,8,128]{2,1,0:T(8,128)S(1)} %get-tuple-element.16), channel_id=1, source_target_pairs={{0,1},{1,2},{2,3},{3,4},{4,5},{5,6},{6,7},{7,8},{8,9},{9,10},{10,1... | collective-permute-start | bytes 172040 | tf_op jit(solution)/shard_map/ppermute | solution.py:469
  5.8 15.8 %collective-permute-start.1 = (f32[14,8,128]{2,1,0:T(8,128)S(1)}, f32[14,8,128]{2,1,0:T(8,128)S(1)}, u32[]{:S(2)}, u32[]{:S(2)}) collective-permute-start(f32[14,8,128]{2,1,0:T(8,128)S(1)} %get-tuple-element.17), channel_id=1, source_target_pairs={{0,31},{1,0},{2,1},{3,2},{4,3},{5,4},{6,5},{7,6},{8,7},{9,8},{10,9... | collective-permute-start | bytes 172040 | tf_op jit(solution)/shard_map/ppermute | solution.py:470
  17.4 4.1 %collective-permute-start.2 = (f32[14,8,128]{2,1,0:T(8,128)S(1)}, f32[14,8,128]{2,1,0:T(8,128)S(1)}, u32[]{:S(2)}, u32[]{:S(2)}) collective-permute-start(f32[14,8,128]{2,1,0:T(8,128)S(1)} %get-tuple-element.18), channel_id=1, source_target_pairs={{0,32},{32,64},{64,96},{96,128},{128,160},{160,192},{192,224},{224... | collective-permute-start | bytes 172040 | tf_op jit(solution)/shard_map/ppermute | solution.py:471
  19.6 3.6 %collective-permute-start.3 = (f32[14,8,128]{2,1,0:T(8,128)S(1)}, f32[14,8,128]{2,1,0:T(8,128)S(1)}, u32[]{:S(2)}, u32[]{:S(2)}) collective-permute-start(f32[14,8,128]{2,1,0:T(8,128)S(1)} %get-tuple-element.19), channel_id=1, source_target_pairs={{0,480},{32,0},{64,32},{96,64},{128,96},{160,128},{192,160},{224,1... | collective-permute-start | bytes 172040 | tf_op jit(solution)/shard_map/ppermute | solution.py:472
  19.6 0.7 copy-start.13
  19.6 0.7 copy-start.15
  19.6 0.7 copy-start.16
  19.6 0.7 copy-start.17
  19.6 0.7 copy-start.18
  19.6 0.7 copy-start.12
  19.6 0.7 copy-start.11
  19.6 0.7 copy-start.10
  19.7 0.7 copy-start.9
  23.2 39.9 %copy-start.8 = (f32[128,1]{1,0:T(8,128)S(1)}, f32[128,1]{1,0:T(8,128)}, u32[]{:S(2)}) copy-start(f32[128,1]{1,0:T(8,128)} %constant.43.clone.kx2) | copy-start | bytes 1540
  23.2 39.9 %copy-start.14 = (f32[1,256]{1,0:T(1,128)S(1)}, f32[1,256]{1,0:T(1,128)}, u32[]{:S(2)}) copy-start(f32[1,256]{1,0:T(1,128)} %constant.44.clone.ky2) | copy-start | bytes 3076
  29.6 24.2 %copy-start.2 = (bf16[2,128,128]{2,1,0:T(8,128)(2,1)S(1)}, bf16[2,128,128]{2,1,0:T(8,128)(2,1)}, u32[]{:S(2)}) copy-start(bf16[2,128,128]{2,1,0:T(8,128)(2,1)} %constant.40.clone.dz_far.dx.dz) | copy-start | bytes 196612
  29.6 24.1 %copy-start.3 = (bf16[2,128,128]{2,1,0:T(8,128)(2,1)S(1)}, bf16[2,128,128]{2,1,0:T(8,128)(2,1)}, u32[]{:S(2)}) copy-start(bf16[2,128,128]{2,1,0:T(8,128)(2,1)} %constant.39.clone.fz_far.fx.fz) | copy-start | bytes 196612
  29.6 33.5 %copy-start.6 = (bf16[2,128,128]{2,1,0:T(8,128)(2,1)S(1)}, bf16[2,128,128]{2,1,0:T(8,128)(2,1)}, u32[]{:S(2)}) copy-start(bf16[2,128,128]{2,1,0:T(8,128)(2,1)} %constant.46.clone.dxt) | copy-start | bytes 196612
  29.6 33.5 %copy-start.7 = (bf16[2,128,128]{2,1,0:T(8,128)(2,1)S(1)}, bf16[2,128,128]{2,1,0:T(8,128)(2,1)}, u32[]{:S(2)}) copy-start(bf16[2,128,128]{2,1,0:T(8,128)(2,1)} %constant.45.clone.fxt) | copy-start | bytes 196612
  53.7 9.4 %copy-start.4 = (bf16[2,4,256,128]{3,2,1,0:T(8,128)(2,1)S(1)}, bf16[2,4,256,128]{3,2,1,0:T(8,128)(2,1)}, u32[]{:S(2)}) copy-start(bf16[2,4,256,128]{3,2,1,0:T(8,128)(2,1)} %constant.42.clone.back) | copy-start | bytes 1572868
  53.7 9.4 %copy-start.5 = (bf16[2,4,128,256]{3,2,1,0:T(8,128)(2,1)S(1)}, bf16[2,4,128,256]{3,2,1,0:T(8,128)(2,1)}, u32[]{:S(2)}) copy-start(bf16[2,4,128,256]{3,2,1,0:T(8,128)(2,1)} %constant.41.clone.forth) | copy-start | bytes 1572868

commit v6 on v5

--- a/solution.py
+++ b/solution.py
@@ -70,6 +70,7 @@
 MAIN = 16
 REST = NREAC - MAIN
 GROUPS = 4
+CHANGE = FORM + ROWS + 8
 WIDE = GROUPS * 3 * ROWS
 
 
@@ -104,7 +105,8 @@
     v = v - dot(newton, one_hot((NS, 192), lambda r, c: c % 32 == r + NREAC))
     by_forms = dot(w, v[:NSPEC])
     by_rows = dot(one_hot((ROWS, NS), lambda r, c: r == c + OFF), v)
-    return spread(jnp.concatenate([by_forms, by_rows], axis=0), FORM + ROWS, 96, 2, 64)
+    block = jnp.concatenate([by_forms, by_rows, jnp.zeros((8, 192), F32)], axis=0)
+    return spread(block[:, :96], CHANGE, 96, 1, 64)
 
 
 def column_plan(cls):
@@ -165,14 +167,11 @@
                 x = jnp.concatenate([p, jnp.where(top, q, zero), zero], axis=0)
             hi, lo = parts(x)
             pairs.append(jnp.concatenate([hi, lo, hi], axis=0))
-        side = jnp.concatenate([jnp.concatenate(pairs[2 * k : 2 * k + 2], axis=0) for k in range(2)], axis=1)
+        side = jnp.concatenate(pairs, axis=1)
         change = jnp.dot(update, side, preferred_element_type=F32)
-        both = FORM + ROWS
-        part = [
-            change[(g % 2) * both : (g % 2 + 1) * both, (g // 2) * wide : (g // 2 + 1) * wide] for g in range(GROUPS)
-        ]
+        part = [change[:, g * wide : (g + 1) * wide] for g in range(GROUPS)]
         a = [a[g] + part[g][:FORM] for g in range(GROUPS)]
-        z = [z[g] + part[g][FORM:] for g in range(GROUPS)]
+        z = [z[g] + part[g][FORM : FORM + ROWS] for g in range(GROUPS)]
     cut = lambda v: [v[k // per][:, (k % per) * NZ : (k % per + 1) * NZ] for k in range(len(cols))]
     return cut(z), cut(a)
 
@@ -354,20 +353,21 @@
         out[i] = both
 
 
-def solve_kernel(place, got, forth, back, kx2, ky2, fxt, dxt, out):
-    full = None
-    for i in range(4):
-        term = dot3(parts(got[i]), (forth[0, i], forth[1, i]))
-        full = term if full is None else full + term
+def once(a, b):
+    return jnp.dot(a, b, preferred_element_type=F32)
+
+
+def solve_kernel(place, got, forth, back, kx2, ky2, left, out):
+    hi, lo = parts(jnp.concatenate([got[i] for i in range(4)], axis=1))
+    full = once(jnp.concatenate([hi, hi, lo], axis=1), forth[...])
     mode = (place[:, 0:1] % (NZ // 2)).astype(F32) * (2 * np.pi / NZ)
     k2 = kx2[...] + ky2[...] + mode * mode
     mine = jnp.max(place[:, 1:2])
-    q = full / jnp.where(k2 > 0, k2, 1.0)
-    lines = parts(dot3(parts(q), (back[0, mine], back[1, mine])))
-    first = dot3((fxt[0], fxt[1]), lines)
-    second = dot3((dxt[0], dxt[1]), lines)
-    out[:, 0, :] = swap_blocks(first)
-    out[:, 1, :] = swap_blocks(second)
+    hi, lo = parts(full / jnp.where(k2 > 0, k2, 1.0))
+    hi, lo = parts(once(jnp.concatenate([hi, hi, lo], axis=1), back[mine]))
+    lines = once(left[...], jnp.concatenate([hi, lo, hi], axis=0))
+    out[:, 0, :] = swap_blocks(lines[:NX])
+    out[:, 1, :] = swap_blocks(lines[NX:])
 
 
 def finish_kernel(got, mid, fz, dz, out):
@@ -409,7 +409,7 @@
         weights_kernel,
         [
             ((GROUPS * FORM, WIDE), bf16),
-            ((2 * (FORM + ROWS), 192), bf16),
+            ((CHANGE, 96), bf16),
             ((MAIN + 8, NZ), F32),
             ((16, NZ), F32),
             ((8, NZ), jnp.int32),
@@ -481,6 +481,10 @@
         hi = v.astype(jnp.bfloat16)
         return np.stack([hi, (v - hi.astype(np.float32)).astype(jnp.bfloat16)])
 
+    def stacked(v, axis, first=False):
+        hi, lo = table(v)
+        return np.concatenate([hi, hi, lo] if first else [hi, lo, hi], axis=axis)
+
     y_of = ((np.arange(8)[None, :, None] * 4 + np.arange(4)[:, None, None]) * CY + np.arange(CY)).reshape(4, COLS)
     forth = np.stack([np.concatenate([fy[:, y].T, dy[:, y].T], axis=0) for y in y_of])
     back = np.stack([np.concatenate([fy[:, y], -dy[:, y]], axis=1) for y in y_of])
@@ -505,15 +509,14 @@
     got = lax.all_to_all(spectra, MODES, 0, 0, tiled=True)
     lines = call(stream_kernel, [(4, NX, 2 * COLS)], 3)(got, table(fx), table(dx))
     lines = lax.all_to_all(lines, "x", 0, 0, tiled=True)
-    grads = call(solve_kernel, [(NX, 2, 2 * COLS)], 8)(
+    grads = call(solve_kernel, [(NX, 2, 2 * COLS)], 7)(
         place,
         lines,
-        table(forth),
-        table(back),
+        stacked(forth.reshape(-1, NY), 0),
+        stacked(back, 1),
         f32(kx * kx)[:, None],
         f32(ky * ky)[None, :],
-        table(fx.T),
-        table(-dx.T),
+        stacked(np.concatenate([fx.T, -dx.T], axis=0), 1, first=True),
     )
     got = lax.all_to_all(grads, MODES, 0, 0, tiled=True)
     flow_out = call(finish_kernel, [(5, CX, CY, NZ)], 4)(got, mid, table(fz), table(dz))

time: 83.9 us -> 83.3 us (level)
  no operation moved by 1% of the time
where the time goes in v6:
time: 83.3 us; the launch traced here: 83 us
  blocking collectives  50.9 us (61%)
  starting transfers between devices  17.8 us (21%)
  Pallas kernels  10.8 us (13%)
  waiting for transfers between devices  1.68 us (2%)
  between operations  0.84 us (1%)
    all_to_all x1, blocking collectives, shards(): got = lax.all_to_all(spectra, MODES, 0, 0, tiled=True)  23.6 us
    all_to_all x1, blocking collectives, shards(): got = lax.all_to_all(grads, MODES, 0, 0, tiled=True)  18.3 us
    ppermute x1, starting transfers between devices, shards(): yhi = ring(GY, n_gy, -1)(edges[3])  11.7 us
    all_to_all x1, blocking collectives, shards(): lines = lax.all_to_all(lines, 'x', 0, 0, tiled=True)  8.99 us
    pallas_call x1, Pallas kernels, react(): call(react_kernel, [(NSPEC, CX, CY, NZ), (5, CX, CY, NZ), (NZ, 2, 2 * COL...  6.15 us
    ppermute x1, starting transfers between devices, shards(): ylo = ring(GY, n_gy, 1)(edges[2])  3.95 us
    ppermute x1, starting transfers between devices, shards(): xlo = ring(GX, n_gx, 1)(edges[0])  2.15 us
    ppermute x1, waiting for transfers between devices, shards(): xhi = ring(GX, n_gx, -1)(edges[1])  1.67 us
  transfers between devices with their start and end apart: 4, of which 1 were waited for; matrix products, arithmetic and copies ran while one was open for 0% of the time, Pallas kernels for 1%

profile of v6, /device:TPU:1, one launch (start us, length us, event | category | flops | bytes accessed | tf_op | source)
XLA Modules:
  0.0 83.0 jit_solution(1259479598459748855)
XLA Ops:
  0.6 0.0 copy-start
  0.6 0.0 copy-start.3
  0.6 1.1 %shard_map.221 = (f32[14,8,128]{2,1,0:T(8,128)S(1)}, f32[14,8,128]{2,1,0:T(8,128)S(1)}, f32[14,8,128]{2,1,0:T(8,128)S(1)}, f32[14,8,128]{2,1,0:T(8,128)S(1)}) custom-call(f32[9,8,8,128]{3,2,1,0:T(8,128)} %species.3, f32[5,8,8,128]{3,2,1,0:T(8,128)} %flow.3), custom_call_target="tpu_custom_call" | custom-call | tf_op jit(solution)/shard_map/pallas_call | solution.py:459
  1.8 3.9 %collective-permute-start = (f32[14,8,128]{2,1,0:T(8,128)S(1)}, f32[14,8,128]{2,1,0:T(8,128)S(1)}, u32[]{:S(2)}, u32[]{:S(2)}) collective-permute-start(f32[14,8,128]{2,1,0:T(8,128)S(1)} %get-tuple-element.16), channel_id=1, source_target_pairs={{0,1},{1,2},{2,3},{3,4},{4,5},{5,6},{6,7},{7,8},{8,9},{9,10},{10,1... | collective-permute-start | bytes 172040 | tf_op jit(solution)/shard_map/ppermute | solution.py:469
  5.8 11.7 %collective-permute-start.1 = (f32[14,8,128]{2,1,0:T(8,128)S(1)}, f32[14,8,128]{2,1,0:T(8,128)S(1)}, u32[]{:S(2)}, u32[]{:S(2)}) collective-permute-start(f32[14,8,128]{2,1,0:T(8,128)S(1)} %get-tuple-element.17), channel_id=1, source_target_pairs={{0,31},{1,0},{2,1},{3,2},{4,3},{5,4},{6,5},{7,6},{8,7},{9,8},{10,9... | collective-permute-start | bytes 172040 | tf_op jit(solution)/shard_map/ppermute | solution.py:470
  17.4 2.1 %collective-permute-start.2 = (f32[14,8,128]{2,1,0:T(8,128)S(1)}, f32[14,8,128]{2,1,0:T(8,128)S(1)}, u32[]{:S(2)}, u32[]{:S(2)}) collective-permute-start(f32[14,8,128]{2,1,0:T(8,128)S(1)} %get-tuple-element.18), channel_id=1, source_target_pairs={{0,32},{32,64},{64,96},{96,128},{128,160},{160,192},{192,224},{224... | collective-permute-start | bytes 172040 | tf_op jit(solution)/shard_map/ppermute | solution.py:471
  19.6 0.0 collective-permute-start.3
  19.6 0.0 copy-start.16
  19.6 0.0 copy-start.17
  19.6 0.0 copy-start.11
  19.6 0.0 copy-start.10
  19.6 0.0 copy-start.9
  19.7 0.0 copy-start.8
  19.7 0.6 copy-done.12
  20.3 0.0 copy-done.14
  20.3 0.0 copy-done.15
  20.3 0.0 copy-done.16
  20.3 0.0 copy-done.17
  20.3 0.1 copy-done.11
  20.4 0.0 copy-done.10
  20.4 0.0 copy-done.9
  20.4 0.0 copy-done.8
  20.4 1.0 %shard_map.222 = (bf16[160,192]{1,0:T(8,128)(2,1)S(1)}, bf16[64,96]{1,0:T(8,128)(2,1)S(1)}, f32[24,128]{1,0:T(8,128)S(1)}, f32[16,128]{1,0:T(8,128)S(1)}, s32[8,128]{1,0:T(8,128)S(1)}) custom-call(s32[8,8]{1,0:T(8,128)S(1)} %copy-done.12, f32[9,19]{1,0:T(8,128)S(1)} %bitcast.11, f32[9,19]{1,0:T(8,128)S(1)} %bitcast.12, f32[9,19]{1,0:T(8,128)S(1)} %bitcast.13, ...), custom_call_target="tpu_custom_call" | custom-call | tf_op jit(solution)/shard_map/pallas_call | solution.py:408
  21.4 0.1 add_bitcast_fusion.place
  21.5 0.0 collective-permute-done.ylo
  21.5 0.0 collective-permute-done.1.yhi
  21.5 0.0 collective-permute-done.2.xlo
  21.5 1.7 %collective-permute-done.3.xhi = f32[14,8,128]{2,1,0:T(8,128)S(1)} collective-permute-done((f32[14,8,128]{2,1,0:T(8,128)S(1)}, f32[14,8,128]{2,1,0:T(8,128)S(1)}, u32[]{:S(2)}, u32[]{:S(2)}) %collective-permute-start.3) | collective-permute-done | bytes 57376 | tf_op jit(solution)/shard_map/ppermute | solution.py:472
  23.2 0.0 copy-done
  23.2 0.0 copy-done.3
  23.2 0.0 copy-start.2
  23.2 6.1 %shard_map.223 = (f32[9,8,8,128]{3,2,1,0:T(8,128)}, f32[5,8,8,128]{3,2,1,0:T(8,128)S(1)}, f32[128,2,128]{2,1,0:T(2,128)S(1)}) custom-call(f32[9,8,8,128]{3,2,1,0:T(8,128)S(1)} %copy-done, f32[5,8,8,128]{3,2,1,0:T(8,128)S(1)} %copy-done.3, f32[14,8,128]{2,1,0:T(8,128)S(1)} %collective-permute-done.ylo, f32[14,8,128]{2,1,0:T(8,128)S(1)} %collective-permute-done.1.yhi, ...), custom_call_target="tpu_custom_call" | custom-call | tf_op jit(solution)/shard_map/pallas_call | solution.py:419
  29.4 0.0 copy-start.1
  29.4 23.6 %all_to_all.15.got = f32[128,2,128]{2,1,0:T(2,128)S(1)} all-to-all(f32[128,2,128]{2,1,0:T(2,128)S(1)} %get-tuple-element.28), channel_id=1, replica_groups=mesh['y'=8,'c'=2,'z'=8,'x'=4] {'y','c','z'}, dimensions={0} | all-to-all | bytes 262144 | tf_op jit(solution)/shard_map/all_to_all | solution.py:509
  53.0 0.0 copy-done.4
  53.0 0.0 copy-done.5
  53.0 0.5 shard_map.224
  53.5 0.0 copy-start.6
  53.5 0.0 copy-start.7
  53.5 0.0 copy-start.13
  53.6 9.0 %all_to_all.16.got = f32[4,128,128]{2,1,0:T(8,128)S(1)} all-to-all(f32[4,128,128]{2,1,0:T(8,128)S(1)} %shard_map.224), channel_id=1, replica_groups=mesh['y'=8,'c'=2,'z'=8,'x'=4] {'x'}, dimensions={0} | all-to-all | bytes 524288 | tf_op jit(solution)/shard_map/all_to_all | solution.py:511
  62.5 0.0 copy-done.2
  62.5 0.0 copy-done.1
  62.6 0.0 copy-done.6
  62.6 0.0 copy-done.7
  62.6 1.1 %shard_map.225 = f32[128,2,128]{2,1,0:T(2,128)S(1)} custom-call(s32[1,2]{1,0:T(1,128)S(1)} %add_bitcast_fusion.place, f32[4,128,128]{2,1,0:T(8,128)S(1)} %all_to_all.16.got, bf16[1536,256]{1,0:T(8,128)(2,1)S(1)} %copy-done.2, bf16[4,768,128]{2,1,0:T(8,128)(2,1)S(1)} %copy-done.1, f32[128,1]{1,0:T(8,128)S(1)} %copy-done.7, f32[1,256]{1,0:T(1,128)S(1)} %copy-done.13, ...), custom_call_target="tpu_custom_call" | custom-call | tf_op jit(solution)/shard_map/pallas_call | solution.py:512
  63.6 18.3 %all_to_all.17.got = f32[128,2,128]{2,1,0:T(2,128)S(1)} all-to-all(f32[128,2,128]{2,1,0:T(2,128)S(1)} %shard_map.225), channel_id=1, replica_groups=mesh['y'=8,'c'=2,'z'=8,'x'=4] {'y','c','z'}, dimensions={0} | all-to-all | bytes 262144 | tf_op jit(solution)/shard_map/all_to_all | solution.py:521
  82.0 1.0 %shard_map.226 = f32[5,8,8,128]{3,2,1,0:T(8,128)} custom-call(f32[128,2,128]{2,1,0:T(2,128)S(1)} %all_to_all.17.got, f32[5,8,8,128]{3,2,1,0:T(8,128)S(1)} %get-tuple-element.29.mid, bf16[2,128,128]{2,1,0:T(8,128)(2,1)S(1)} %copy-done.5, bf16[2,128,128]{2,1,0:T(8,128)(2,1)S(1)} %copy-done.4), custom_call_target="tpu_custom_call" | custom-call | tf_op jit(solution)/shard_map/pallas_call | solution.py:522
  (6 shorter events, 0.0 us)
Async XLA Ops:
  0.6 22.6 %copy-start = (f32[9,8,8,128]{3,2,1,0:T(8,128)S(1)}, f32[9,8,8,128]{3,2,1,0:T(8,128)}, u32[]{:S(2)}) copy-start(f32[9,8,8,128]{3,2,1,0:T(8,128)} %species.3) | copy-start | bytes 884740
  0.6 22.5 %copy-start.3 = (f32[5,8,8,128]{3,2,1,0:T(8,128)S(1)}, f32[5,8,8,128]{3,2,1,0:T(8,128)}, u32[]{:S(2)}) copy-start(f32[5,8,8,128]{3,2,1,0:T(8,128)} %flow.3) | copy-start | bytes 491524
  1.8 19.7 %collective-permute-start = (f32[14,8,128]{2,1,0:T(8,128)S(1)}, f32[14,8,128]{2,1,0:T(8,128)S(1)}, u32[]{:S(2)}, u32[]{:S(2)}) collective-permute-start(f32[14,8,128]{2,1,0:T(8,128)S(1)} %get-tuple-element.16), channel_id=1, source_target_pairs={{0,1},{1,2},{2,3},{3,4},{4,5},{5,6},{6,7},{7,8},{8,9},{9,10},{10,1... | collective-permute-start | bytes 172040 | tf_op jit(solution)/shard_map/ppermute | solution.py:469
  5.8 15.7 %collective-permute-start.1 = (f32[14,8,128]{2,1,0:T(8,128)S(1)}, f32[14,8,128]{2,1,0:T(8,128)S(1)}, u32[]{:S(2)}, u32[]{:S(2)}) collective-permute-start(f32[14,8,128]{2,1,0:T(8,128)S(1)} %get-tuple-element.17), channel_id=1, source_target_pairs={{0,31},{1,0},{2,1},{3,2},{4,3},{5,4},{6,5},{7,6},{8,7},{9,8},{10,9... | collective-permute-start | bytes 172040 | tf_op jit(solution)/shard_map/ppermute | solution.py:470
  17.4 4.1 %collective-permute-start.2 = (f32[14,8,128]{2,1,0:T(8,128)S(1)}, f32[14,8,128]{2,1,0:T(8,128)S(1)}, u32[]{:S(2)}, u32[]{:S(2)}) collective-permute-start(f32[14,8,128]{2,1,0:T(8,128)S(1)} %get-tuple-element.18), channel_id=1, source_target_pairs={{0,32},{32,64},{64,96},{96,128},{128,160},{160,192},{192,224},{224... | collective-permute-start | bytes 172040 | tf_op jit(solution)/shard_map/ppermute | solution.py:471
  19.6 3.6 %collective-permute-start.3 = (f32[14,8,128]{2,1,0:T(8,128)S(1)}, f32[14,8,128]{2,1,0:T(8,128)S(1)}, u32[]{:S(2)}, u32[]{:S(2)}) collective-permute-start(f32[14,8,128]{2,1,0:T(8,128)S(1)} %get-tuple-element.19), channel_id=1, source_target_pairs={{0,480},{32,0},{64,32},{96,64},{128,96},{160,128},{192,160},{224,1... | collective-permute-start | bytes 172040 | tf_op jit(solution)/shard_map/ppermute | solution.py:472
  19.6 0.7 copy-start.12
  19.6 0.7 copy-start.14
  19.6 0.7 copy-start.15
  19.6 0.7 copy-start.16
  19.6 0.7 copy-start.17
  19.6 0.7 copy-start.11
  19.6 0.7 copy-start.10
  19.6 0.7 copy-start.9
  19.7 0.7 copy-start.8
  23.2 29.8 %copy-start.4 = (bf16[2,128,128]{2,1,0:T(8,128)(2,1)S(1)}, bf16[2,128,128]{2,1,0:T(8,128)(2,1)}, u32[]{:S(2)}) copy-start(bf16[2,128,128]{2,1,0:T(8,128)(2,1)} %constant.38.clone.dz_far.dx.dz) | copy-start | bytes 196612
  23.2 29.8 %copy-start.5 = (bf16[2,128,128]{2,1,0:T(8,128)(2,1)S(1)}, bf16[2,128,128]{2,1,0:T(8,128)(2,1)}, u32[]{:S(2)}) copy-start(bf16[2,128,128]{2,1,0:T(8,128)(2,1)} %constant.37.clone.fz_far.fx.fz) | copy-start | bytes 196612
  23.2 39.4 %copy-start.2 = (bf16[1536,256]{1,0:T(8,128)(2,1)S(1)}, bf16[1536,256]{1,0:T(8,128)(2,1)}, u32[]{:S(2)}) copy-start(bf16[1536,256]{1,0:T(8,128)(2,1)} %constant.39.clone.forth) | copy-start | bytes 2359300
  29.4 33.2 %copy-start.1 = (bf16[4,768,128]{2,1,0:T(8,128)(2,1)S(1)}, bf16[4,768,128]{2,1,0:T(8,128)(2,1)}, u32[]{:S(2)}) copy-start(bf16[4,768,128]{2,1,0:T(8,128)(2,1)} %constant.40.clone.back) | copy-start | bytes 2359300
  53.5 9.0 %copy-start.6 = (bf16[256,384]{1,0:T(8,128)(2,1)S(1)}, bf16[256,384]{1,0:T(8,128)(2,1)}, u32[]{:S(2)}) copy-start(bf16[256,384]{1,0:T(8,128)(2,1)} %constant.43.clone.left) | copy-start | bytes 589828
  53.5 9.0 %copy-start.7 = (f32[128,1]{1,0:T(8,128)S(1)}, f32[128,1]{1,0:T(8,128)}, u32[]{:S(2)}) copy-start(f32[128,1]{1,0:T(8,128)} %constant.41.clone.kx2) | copy-start | bytes 1540
  53.5 9.0 %copy-start.13 = (f32[1,256]{1,0:T(1,128)S(1)}, f32[1,256]{1,0:T(1,128)}, u32[]{:S(2)}) copy-start(f32[1,256]{1,0:T(1,128)} %constant.42.clone.ky2) | copy-start | bytes 3076

commit v7 on v6

--- a/solution.py
+++ b/solution.py
@@ -64,6 +64,7 @@
     return one(a[0], b[0]) + (one(a[0], b[1]) + one(a[1], b[0]))
 
 
+SMALL = 9
 OFF = 3
 ROWS = 16
 FORM = 40
@@ -176,11 +177,11 @@
     return cut(z), cut(a)
 
 
-def halo_kernel(species, flow, last_x, first_x, last_y, first_y, own_s, own_f, sems):
-    copies = [
-        pltpu.make_async_copy(species, own_s, sems.at[0]),
-        pltpu.make_async_copy(flow, own_f, sems.at[1]),
-    ]
+def halo_kernel(species, flow, *refs):
+    small, (last_x, first_x, last_y, first_y) = refs[:SMALL], refs[SMALL : SMALL + 4]
+    small_out, (own_s, own_f, sems) = refs[SMALL + 4 : -3], refs[-3:]
+    pairs = [(species, own_s), (flow, own_f)] + list(zip(small, small_out))
+    copies = [pltpu.make_async_copy(a, b, sems.at[k]) for k, (a, b) in enumerate(pairs)]
     for c in copies:
         c.start()
     for c in copies:
@@ -207,10 +208,10 @@
 def react_kernel(
     species,
     flow,
+    xhi,
     ylo,
     yhi,
     xlo,
-    xhi,
     forms,
     update,
     energy_col,
@@ -402,8 +403,7 @@
     )
 
 
-def react(fields, halos, classes, diffusivity, left, right, stoich, heat, prefactor, energy, newton, fz, dz):
-    row = lambda v: v[None, :]
+def react(fields, halos, small, fz, dz):
     bf16 = jnp.bfloat16
     weights = call(
         weights_kernel,
@@ -415,7 +415,7 @@
             ((8, NZ), jnp.int32),
         ],
         9,
-    )(classes, left.T, right.T, stoich.T, row(heat), row(prefactor), row(energy), newton, row(diffusivity))
+    )(*small)
     return call(
         react_kernel,
         [(NSPEC, CX, CY, NZ), (5, CX, CY, NZ), (NZ, 2, 2 * COLS)],
@@ -456,16 +456,28 @@
     newton,
 ):
     n_gx, n_gy = NX // CX, NY // CY
+    row = lambda v: v[None, :]
+    small = (
+        classes,
+        left.T,
+        right.T,
+        stoich.T,
+        row(heat),
+        row(prefactor),
+        row(energy),
+        newton,
+        row(diffusivity),
+    )
     edges = call(
         halo_kernel,
-        [(NF, 8, NZ)] * 4,
-        [HBM] * 2,
+        [(NF, 8, NZ)] * 4 + [(v.shape, v.dtype) for v in small],
+        [HBM] * (2 + SMALL),
         [
             pltpu.VMEM((NSPEC, CX, CY, NZ), F32),
             pltpu.VMEM((5, CX, CY, NZ), F32),
-            pltpu.SemaphoreType.DMA((2,)),
+            pltpu.SemaphoreType.DMA((2 + SMALL,)),
         ],
-    )(far(species), far(flow))
+    )(far(species), far(flow), *(far(v) for v in small))
     ylo = ring(GY, n_gy, 1)(edges[2])
     yhi = ring(GY, n_gy, -1)(edges[3])
     xlo = ring(GX, n_gx, 1)(edges[0])
@@ -491,16 +503,8 @@
 
     species_out, mid, spectra = react(
         (species, flow),
-        (ylo, yhi, xlo, xhi),
-        classes,
-        diffusivity,
-        left,
-        right,
-        stoich,
-        heat,
-        prefactor,
-        energy,
-        newton,
+        (xhi, ylo, yhi, xlo),
+        edges[4:],
         table(fz),
         table(dz),
     )

time: 83.3 us -> 83.3 us (level)
  blocking collectives: 50.9 us -> 52 us
    ppermute x1, starting transfers between devices: 0.01 us -> 6.89 us  [shards(): xhi = ring(GX, n_gx, -1)(edges[1])]
    ppermute x1, starting transfers between devices: 11.7 us -> 7.49 us  [shards(): yhi = ring(GY, n_gy, -1)(edges[3])]
    ppermute x1, starting transfers between devices: 3.95 us -> 1.91 us  [shards(): ylo = ring(GY, n_gy, 1)(edges[2])]
    ppermute x1, waiting for transfers between devices: 1.67 us -> 0.01 us  [shards(): xhi = ring(GX, n_gx, -1)(edges[1])]
    ppermute x1, waiting for transfers between devices: 0.01 us -> 1.34 us  [shards(): xlo = ring(GX, n_gx, 1)(edges[0])]
    all_to_all x1, blocking collectives: 23.6 us -> 24.7 us  [shards(): got = lax.all_to_all(spectra, MODES, 0, 0, tiled=True)]
where the time goes in v7:
time: 83.3 us; the launch traced here: 83 us
  blocking collectives  52 us (62%)
  starting transfers between devices  17.8 us (21%)
  Pallas kernels  10.9 us (13%)
  waiting for transfers between devices  1.34 us (2%)
    all_to_all x1, blocking collectives, shards(): got = lax.all_to_all(spectra, MODES, 0, 0, tiled=True)  24.7 us
    all_to_all x1, blocking collectives, shards(): got = lax.all_to_all(grads, MODES, 0, 0, tiled=True)  18.3 us
    all_to_all x1, blocking collectives, shards(): lines = lax.all_to_all(lines, 'x', 0, 0, tiled=True)  8.99 us
    ppermute x1, starting transfers between devices, shards(): yhi = ring(GY, n_gy, -1)(edges[3])  7.49 us
    ppermute x1, starting transfers between devices, shards(): xhi = ring(GX, n_gx, -1)(edges[1])  6.89 us
    pallas_call x1, Pallas kernels, react(): call(react_kernel, [(NSPEC, CX, CY, NZ), (5, CX, CY, NZ), (NZ, 2, 2 * COL...  6.15 us
    ppermute x1, starting transfers between devices, shards(): ylo = ring(GY, n_gy, 1)(edges[2])  1.91 us
  transfers between devices with their start and end apart: 4, of which 1 were waited for; matrix products, arithmetic and copies ran while one was open for 0% of the time, Pallas kernels for 1%

profile of v7, /device:TPU:1, one launch (start us, length us, event | category | flops | bytes accessed | tf_op | source)
XLA Modules:
  0.0 83.0 jit_solution(18431498314359119110)
XLA Ops:
  0.6 0.0 copy-start
  0.6 0.0 copy-start.3
  0.7 1.2 %shard_map.221 = (f32[14,8,128]{2,1,0:T(8,128)S(1)}, f32[14,8,128]{2,1,0:T(8,128)S(1)}, f32[14,8,128]{2,1,0:T(8,128)S(1)}, f32[14,8,128]{2,1,0:T(8,128)S(1)}, s3...) custom-call(f32[9,8,8,128]{3,2,1,0:T(8,128)} %species.3, ...), custom_call_target="tpu_custom_call" | custom-call | tf_op jit(solution)/shard_map/pallas_call | solution.py:471
  1.9 6.9 %collective-permute-start = (f32[14,8,128]{2,1,0:T(8,128)S(1)}, f32[14,8,128]{2,1,0:T(8,128)S(1)}, u32[]{:S(2)}, u32[]{:S(2)}) collective-permute-start(f32[14,8,128]{2,1,0:T(8,128)S(1)} %get-tuple-element.25), channel_id=1, source_target_pairs={{0,480},{32,0},{64,32},{96,64},{128,96},{160,128},{192,160},{224,1... | collective-permute-start | bytes 172040 | tf_op jit(solution)/shard_map/ppermute | solution.py:484
  8.8 1.9 %collective-permute-start.1 = (f32[14,8,128]{2,1,0:T(8,128)S(1)}, f32[14,8,128]{2,1,0:T(8,128)S(1)}, u32[]{:S(2)}, u32[]{:S(2)}) collective-permute-start(f32[14,8,128]{2,1,0:T(8,128)S(1)} %get-tuple-element.26), channel_id=1, source_target_pairs={{0,1},{1,2},{2,3},{3,4},{4,5},{5,6},{6,7},{7,8},{8,9},{9,10},{10,1... | collective-permute-start | bytes 172040 | tf_op jit(solution)/shard_map/ppermute | solution.py:481
  10.7 7.5 %collective-permute-start.2 = (f32[14,8,128]{2,1,0:T(8,128)S(1)}, f32[14,8,128]{2,1,0:T(8,128)S(1)}, u32[]{:S(2)}, u32[]{:S(2)}) collective-permute-start(f32[14,8,128]{2,1,0:T(8,128)S(1)} %get-tuple-element.27), channel_id=1, source_target_pairs={{0,31},{1,0},{2,1},{3,2},{4,3},{5,4},{6,5},{7,6},{8,7},{9,8},{10,9... | collective-permute-start | bytes 172040 | tf_op jit(solution)/shard_map/ppermute | solution.py:482
  18.2 1.5 %collective-permute-start.3 = (f32[14,8,128]{2,1,0:T(8,128)S(1)}, f32[14,8,128]{2,1,0:T(8,128)S(1)}, u32[]{:S(2)}, u32[]{:S(2)}) collective-permute-start(f32[14,8,128]{2,1,0:T(8,128)S(1)} %get-tuple-element.28), channel_id=1, source_target_pairs={{0,32},{32,64},{64,96},{96,128},{128,160},{160,192},{192,224},{224... | collective-permute-start | bytes 172040 | tf_op jit(solution)/shard_map/ppermute | solution.py:483
  19.7 1.0 %shard_map.222 = (bf16[160,192]{1,0:T(8,128)(2,1)S(1)}, bf16[64,96]{1,0:T(8,128)(2,1)S(1)}, f32[24,128]{1,0:T(8,128)S(1)}, f32[16,128]{1,0:T(8,128)S(1)}, s32[8,128]{1,0:T(8,128)S(1)}) custom-call(s32[8,8]{1,0:T(8,128)S(1)} %get-tuple-element.29.classes, f32[9,19]{1,0:T(8,128)S(1)} %get-tuple-element.30.left_t, f32[9,19]{1,0:T(8,128)S(1)} %get-tuple-element.31.right_t, ...), custom_call_target="tpu_custom_call" | custom-call | tf_op jit(solution)/shard_map/pallas_call | solution.py:408
  20.7 0.1 add_bitcast_fusion.place
  20.8 0.0 collective-permute-done.xhi
  20.8 0.0 collective-permute-done.1.ylo
  20.8 0.0 collective-permute-done.2.yhi
  20.8 1.3 %collective-permute-done.3.xlo = f32[14,8,128]{2,1,0:T(8,128)S(1)} collective-permute-done((f32[14,8,128]{2,1,0:T(8,128)S(1)}, f32[14,8,128]{2,1,0:T(8,128)S(1)}, u32[]{:S(2)}, u32[]{:S(2)}) %collective-permute-start.3) | collective-permute-done | bytes 57376 | tf_op jit(solution)/shard_map/ppermute | solution.py:483
  22.1 0.0 copy-done
  22.2 0.0 copy-done.3
  22.2 0.0 copy-start.4
  22.2 0.0 copy-start.5
  22.2 0.0 copy-start.2
  22.2 6.2 %shard_map.223 = (f32[9,8,8,128]{3,2,1,0:T(8,128)}, f32[5,8,8,128]{3,2,1,0:T(8,128)S(1)}, f32[128,2,128]{2,1,0:T(2,128)S(1)}) custom-call(f32[9,8,8,128]{3,2,1,0:T(8,128)S(1)} %copy-done, f32[5,8,8,128]{3,2,1,0:T(8,128)S(1)} %copy-done.3, f32[14,8,128]{2,1,0:T(8,128)S(1)} %collective-permute-done.xhi, f32[14,8,128]{2,1,0:T(8,128)S(1)} %collective-permute-done.1.ylo, ...), custom_call_target="tpu_custom_call" | custom-call | tf_op jit(solution)/shard_map/pallas_call | solution.py:419
  28.3 0.0 copy-start.1
  28.3 24.7 %all_to_all.15.got = f32[128,2,128]{2,1,0:T(2,128)S(1)} all-to-all(f32[128,2,128]{2,1,0:T(2,128)S(1)} %get-tuple-element.46), channel_id=1, replica_groups=mesh['y'=8,'c'=2,'z'=8,'x'=4] {'y','c','z'}, dimensions={0} | all-to-all | bytes 262144 | tf_op jit(solution)/shard_map/all_to_all | solution.py:513
  53.0 0.0 copy-done.4
  53.0 0.0 copy-done.5
  53.0 0.5 shard_map.224
  53.5 0.0 copy-start.6
  53.5 0.0 copy-start.7
  53.6 0.0 copy-start.8
  53.6 9.0 %all_to_all.16.got = f32[4,128,128]{2,1,0:T(8,128)S(1)} all-to-all(f32[4,128,128]{2,1,0:T(8,128)S(1)} %shard_map.224), channel_id=1, replica_groups=mesh['y'=8,'c'=2,'z'=8,'x'=4] {'x'}, dimensions={0} | all-to-all | bytes 524288 | tf_op jit(solution)/shard_map/all_to_all | solution.py:515
  62.6 0.0 copy-done.2
  62.6 0.0 copy-done.1
  62.6 0.0 copy-done.6
  62.6 0.0 copy-done.7
  62.6 0.0 copy-done.8
  62.6 1.1 %shard_map.225 = f32[128,2,128]{2,1,0:T(2,128)S(1)} custom-call(s32[1,2]{1,0:T(1,128)S(1)} %add_bitcast_fusion.place, f32[4,128,128]{2,1,0:T(8,128)S(1)} %all_to_all.16.got, bf16[1536,256]{1,0:T(8,128)(2,1)S(1)} %copy-done.2, bf16[4,768,128]{2,1,0:T(8,128)(2,1)S(1)} %copy-done.1, f32[128,1]{1,0:T(8,128)S(1)} %copy-done.7, f32[1,256]{1,0:T(1,128)S(1)} %copy-done.8, ...), custom_call_target="tpu_custom_call" | custom-call | tf_op jit(solution)/shard_map/pallas_call | solution.py:516
  63.6 18.3 %all_to_all.17.got = f32[128,2,128]{2,1,0:T(2,128)S(1)} all-to-all(f32[128,2,128]{2,1,0:T(2,128)S(1)} %shard_map.225), channel_id=1, replica_groups=mesh['y'=8,'c'=2,'z'=8,'x'=4] {'y','c','z'}, dimensions={0} | all-to-all | bytes 262144 | tf_op jit(solution)/shard_map/all_to_all | solution.py:525
  82.0 1.0 %shard_map.226 = f32[5,8,8,128]{3,2,1,0:T(8,128)} custom-call(f32[128,2,128]{2,1,0:T(2,128)S(1)} %all_to_all.17.got, f32[5,8,8,128]{3,2,1,0:T(8,128)S(1)} %get-tuple-element.47.mid, bf16[2,128,128]{2,1,0:T(8,128)(2,1)S(1)} %copy-done.5, bf16[2,128,128]{2,1,0:T(8,128)(2,1)S(1)} %copy-done.4), custom_call_target="tpu_custom_call" | custom-call | tf_op jit(solution)/shard_map/pallas_call | solution.py:526
Async XLA Ops:
  0.6 21.5 %copy-start = (f32[9,8,8,128]{3,2,1,0:T(8,128)S(1)}, f32[9,8,8,128]{3,2,1,0:T(8,128)}, u32[]{:S(2)}) copy-start(f32[9,8,8,128]{3,2,1,0:T(8,128)} %species.3) | copy-start | bytes 884740
  0.6 21.5 %copy-start.3 = (f32[5,8,8,128]{3,2,1,0:T(8,128)S(1)}, f32[5,8,8,128]{3,2,1,0:T(8,128)}, u32[]{:S(2)}) copy-start(f32[5,8,8,128]{3,2,1,0:T(8,128)} %flow.3) | copy-start | bytes 491524
  1.9 18.9 %collective-permute-start = (f32[14,8,128]{2,1,0:T(8,128)S(1)}, f32[14,8,128]{2,1,0:T(8,128)S(1)}, u32[]{:S(2)}, u32[]{:S(2)}) collective-permute-start(f32[14,8,128]{2,1,0:T(8,128)S(1)} %get-tuple-element.25), channel_id=1, source_target_pairs={{0,480},{32,0},{64,32},{96,64},{128,96},{160,128},{192,160},{224,1... | collective-permute-start | bytes 172040 | tf_op jit(solution)/shard_map/ppermute | solution.py:484
  8.8 12.0 %collective-permute-start.1 = (f32[14,8,128]{2,1,0:T(8,128)S(1)}, f32[14,8,128]{2,1,0:T(8,128)S(1)}, u32[]{:S(2)}, u32[]{:S(2)}) collective-permute-start(f32[14,8,128]{2,1,0:T(8,128)S(1)} %get-tuple-element.26), channel_id=1, source_target_pairs={{0,1},{1,2},{2,3},{3,4},{4,5},{5,6},{6,7},{7,8},{8,9},{9,10},{10,1... | collective-permute-start | bytes 172040 | tf_op jit(solution)/shard_map/ppermute | solution.py:481
  10.7 10.1 %collective-permute-start.2 = (f32[14,8,128]{2,1,0:T(8,128)S(1)}, f32[14,8,128]{2,1,0:T(8,128)S(1)}, u32[]{:S(2)}, u32[]{:S(2)}) collective-permute-start(f32[14,8,128]{2,1,0:T(8,128)S(1)} %get-tuple-element.27), channel_id=1, source_target_pairs={{0,31},{1,0},{2,1},{3,2},{4,3},{5,4},{6,5},{7,6},{8,7},{9,8},{10,9... | collective-permute-start | bytes 172040 | tf_op jit(solution)/shard_map/ppermute | solution.py:482
  18.2 3.9 %collective-permute-start.3 = (f32[14,8,128]{2,1,0:T(8,128)S(1)}, f32[14,8,128]{2,1,0:T(8,128)S(1)}, u32[]{:S(2)}, u32[]{:S(2)}) collective-permute-start(f32[14,8,128]{2,1,0:T(8,128)S(1)} %get-tuple-element.28), channel_id=1, source_target_pairs={{0,32},{32,64},{64,96},{96,128},{128,160},{160,192},{192,224},{224... | collective-permute-start | bytes 172040 | tf_op jit(solution)/shard_map/ppermute | solution.py:483
  22.2 30.9 %copy-start.4 = (bf16[2,128,128]{2,1,0:T(8,128)(2,1)S(1)}, bf16[2,128,128]{2,1,0:T(8,128)(2,1)}, u32[]{:S(2)}) copy-start(bf16[2,128,128]{2,1,0:T(8,128)(2,1)} %constant.38.clone.dz_far.dx.dz) | copy-start | bytes 196612
  22.2 30.9 %copy-start.5 = (bf16[2,128,128]{2,1,0:T(8,128)(2,1)S(1)}, bf16[2,128,128]{2,1,0:T(8,128)(2,1)}, u32[]{:S(2)}) copy-start(bf16[2,128,128]{2,1,0:T(8,128)(2,1)} %constant.37.clone.fz_far.fx.fz) | copy-start | bytes 196612
  22.2 40.4 %copy-start.2 = (bf16[1536,256]{1,0:T(8,128)(2,1)S(1)}, bf16[1536,256]{1,0:T(8,128)(2,1)}, u32[]{:S(2)}) copy-start(bf16[1536,256]{1,0:T(8,128)(2,1)} %constant.39.clone.forth) | copy-start | bytes 2359300
  28.3 34.2 %copy-start.1 = (bf16[4,768,128]{2,1,0:T(8,128)(2,1)S(1)}, bf16[4,768,128]{2,1,0:T(8,128)(2,1)}, u32[]{:S(2)}) copy-start(bf16[4,768,128]{2,1,0:T(8,128)(2,1)} %constant.40.clone.back) | copy-start | bytes 2359300
  53.5 9.0 %copy-start.6 = (bf16[256,384]{1,0:T(8,128)(2,1)S(1)}, bf16[256,384]{1,0:T(8,128)(2,1)}, u32[]{:S(2)}) copy-start(bf16[256,384]{1,0:T(8,128)(2,1)} %constant.43.clone.left) | copy-start | bytes 589828
  53.5 9.0 %copy-start.7 = (f32[128,1]{1,0:T(8,128)S(1)}, f32[128,1]{1,0:T(8,128)}, u32[]{:S(2)}) copy-start(f32[128,1]{1,0:T(8,128)} %constant.41.clone.kx2) | copy-start | bytes 1540
  53.6 9.0 %copy-start.8 = (f32[1,256]{1,0:T(1,128)S(1)}, f32[1,256]{1,0:T(1,128)}, u32[]{:S(2)}) copy-start(f32[1,256]{1,0:T(1,128)} %constant.42.clone.ky2) | copy-start | bytes 3076

commit v8 on v7

--- a/solution.py
+++ b/solution.py
@@ -208,9 +208,9 @@
 def react_kernel(
     species,
     flow,
-    xhi,
     ylo,
     yhi,
+    xhi,
     xlo,
     forms,
     update,
@@ -470,13 +470,9 @@
     )
     edges = call(
         halo_kernel,
-        [(NF, 8, NZ)] * 4 + [(v.shape, v.dtype) for v in small],
+        [(NF, 8, NZ)] * 4 + [(v.shape, v.dtype) for v in small] + [species.shape, flow.shape],
         [HBM] * (2 + SMALL),
-        [
-            pltpu.VMEM((NSPEC, CX, CY, NZ), F32),
-            pltpu.VMEM((5, CX, CY, NZ), F32),
-            pltpu.SemaphoreType.DMA((2 + SMALL,)),
-        ],
+        [pltpu.SemaphoreType.DMA((2 + SMALL,))],
     )(far(species), far(flow), *(far(v) for v in small))
     ylo = ring(GY, n_gy, 1)(edges[2])
     yhi = ring(GY, n_gy, -1)(edges[3])
@@ -502,9 +498,9 @@
     back = np.stack([np.concatenate([fy[:, y], -dy[:, y]], axis=1) for y in y_of])
 
     species_out, mid, spectra = react(
-        (species, flow),
-        (xhi, ylo, yhi, xlo),
-        edges[4:],
+        edges[-2:],
+        (ylo, yhi, xhi, xlo),
+        edges[4:-2],
         table(fz),
         table(dz),
     )

time: 83.3 us -> 83.2 us (level)
    ppermute x1, starting transfers between devices: 6.89 us -> 0.97 us  [shards(): xhi = ring(GX, n_gx, -1)(edges[1])]
    ppermute x1, starting transfers between devices: 7.49 us -> 11.7 us  [shards(): yhi = ring(GY, n_gy, -1)(edges[3])]
    ppermute x1, starting transfers between devices: 1.91 us -> 3.95 us  [shards(): ylo = ring(GY, n_gy, 1)(edges[2])]
    ppermute x1, waiting for transfers between devices: 1.34 us -> 0.32 us  [shards(): xlo = ring(GX, n_gx, 1)(edges[0])]
  transfers between devices with their start and end apart: 4 -> 4, of which waited for: 1 -> 2; matrix products, arithmetic and copies ran while one was open for 0% -> 0% of each run, Pallas kernels for 1% -> 1%
where the time goes in v8:
time: 83.2 us; the launch traced here: 82.9 us
  blocking collectives  52.3 us (63%)
  starting transfers between devices  17.8 us (21%)
  Pallas kernels  10.9 us (13%)
  waiting for transfers between devices  1.06 us (1%)
    all_to_all x1, blocking collectives, shards(): got = lax.all_to_all(spectra, MODES, 0, 0, tiled=True)  24.9 us
    all_to_all x1, blocking collectives, shards(): got = lax.all_to_all(grads, MODES, 0, 0, tiled=True)  18.3 us
    ppermute x1, starting transfers between devices, shards(): yhi = ring(GY, n_gy, -1)(edges[3])  11.7 us
    all_to_all x1, blocking collectives, shards(): lines = lax.all_to_all(lines, 'x', 0, 0, tiled=True)  8.99 us
    pallas_call x1, Pallas kernels, react(): call(react_kernel, [(NSPEC, CX, CY, NZ), (5, CX, CY, NZ), (NZ, 2, 2 * COL...  6.14 us
    ppermute x1, starting transfers between devices, shards(): ylo = ring(GY, n_gy, 1)(edges[2])  3.95 us
  transfers between devices with their start and end apart: 4, of which 2 were waited for; matrix products, arithmetic and copies ran while one was open for 0% of the time, Pallas kernels for 1%

profile of v8, /device:TPU:1, one launch (start us, length us, event | category | flops | bytes accessed | tf_op | source)
XLA Modules:
  0.0 82.9 jit_solution(9071689493266741203)
XLA Ops:
  0.6 1.2 %shard_map.221 = (f32[14,8,128]{2,1,0:T(8,128)S(1)}, f32[14,8,128]{2,1,0:T(8,128)S(1)}, f32[14,8,128]{2,1,0:T(8,128)S(1)}, f32[14,8,128]{2,1,0:T(8,128)S(1)}, s3...) custom-call(f32[9,8,8,128]{3,2,1,0:T(8,128)} %species.1, ...), custom_call_target="tpu_custom_call" | custom-call | tf_op jit(solution)/shard_map/pallas_call | solution.py:471
  1.8 3.9 %collective-permute-start = (f32[14,8,128]{2,1,0:T(8,128)S(1)}, f32[14,8,128]{2,1,0:T(8,128)S(1)}, u32[]{:S(2)}, u32[]{:S(2)}) collective-permute-start(f32[14,8,128]{2,1,0:T(8,128)S(1)} %get-tuple-element.29), channel_id=1, source_target_pairs={{0,1},{1,2},{2,3},{3,4},{4,5},{5,6},{6,7},{7,8},{8,9},{9,10},{10,1... | collective-permute-start | bytes 172040 | tf_op jit(solution)/shard_map/ppermute | solution.py:477
  5.8 11.7 %collective-permute-start.1 = (f32[14,8,128]{2,1,0:T(8,128)S(1)}, f32[14,8,128]{2,1,0:T(8,128)S(1)}, u32[]{:S(2)}, u32[]{:S(2)}) collective-permute-start(f32[14,8,128]{2,1,0:T(8,128)S(1)} %get-tuple-element.30), channel_id=1, source_target_pairs={{0,31},{1,0},{2,1},{3,2},{4,3},{5,4},{6,5},{7,6},{8,7},{9,8},{10,9... | collective-permute-start | bytes 172040 | tf_op jit(solution)/shard_map/ppermute | solution.py:478
  17.5 1.0 %collective-permute-start.2 = (f32[14,8,128]{2,1,0:T(8,128)S(1)}, f32[14,8,128]{2,1,0:T(8,128)S(1)}, u32[]{:S(2)}, u32[]{:S(2)}) collective-permute-start(f32[14,8,128]{2,1,0:T(8,128)S(1)} %get-tuple-element.31), channel_id=1, source_target_pairs={{0,480},{32,0},{64,32},{96,64},{128,96},{160,128},{192,160},{224,1... | collective-permute-start | bytes 172040 | tf_op jit(solution)/shard_map/ppermute | solution.py:480
  18.4 1.2 %collective-permute-start.3 = (f32[14,8,128]{2,1,0:T(8,128)S(1)}, f32[14,8,128]{2,1,0:T(8,128)S(1)}, u32[]{:S(2)}, u32[]{:S(2)}) collective-permute-start(f32[14,8,128]{2,1,0:T(8,128)S(1)} %get-tuple-element.32), channel_id=1, source_target_pairs={{0,32},{32,64},{64,96},{96,128},{128,160},{160,192},{192,224},{224... | collective-permute-start | bytes 172040 | tf_op jit(solution)/shard_map/ppermute | solution.py:479
  19.6 1.0 %shard_map.222 = (bf16[160,192]{1,0:T(8,128)(2,1)S(1)}, bf16[64,96]{1,0:T(8,128)(2,1)S(1)}, f32[24,128]{1,0:T(8,128)S(1)}, f32[16,128]{1,0:T(8,128)S(1)}, s32[8,128]{1,0:T(8,128)S(1)}) custom-call(s32[8,8]{1,0:T(8,128)S(1)} %get-tuple-element.33.classes, f32[9,19]{1,0:T(8,128)S(1)} %get-tuple-element.34.left_t, f32[9,19]{1,0:T(8,128)S(1)} %get-tuple-element.35.right_t, ...), custom_call_target="tpu_custom_call" | custom-call | tf_op jit(solution)/shard_map/pallas_call | solution.py:408
  20.7 0.1 add_bitcast_fusion.place
  20.7 0.0 collective-permute-done.ylo
  20.7 0.0 collective-permute-done.1.yhi
  20.7 0.7 collective-permute-done.2.xhi
  21.5 0.3 collective-permute-done.3.xlo
  21.8 0.0 copy-start.2
  21.8 0.0 copy-start.3
  21.8 0.0 copy-start.1
  21.8 6.1 %shard_map.223 = (f32[9,8,8,128]{3,2,1,0:T(8,128)}, f32[5,8,8,128]{3,2,1,0:T(8,128)S(1)}, f32[128,2,128]{2,1,0:T(2,128)S(1)}) custom-call(f32[9,8,8,128]{3,2,1,0:T(8,128)S(1)} %get-tuple-element.27.species, f32[5,8,8,128]{3,2,1,0:T(8,128)S(1)} %get-tuple-element.28.flow, f32[14,8,128]{2,1,0:T(8,128)S(1)} %collective-permute-done.ylo, ...), custom_call_target="tpu_custom_call" | custom-call | tf_op jit(solution)/shard_map/pallas_call | solution.py:419
  28.0 0.0 copy-start
  28.0 24.9 %all_to_all.15.got = f32[128,2,128]{2,1,0:T(2,128)S(1)} all-to-all(f32[128,2,128]{2,1,0:T(2,128)S(1)} %get-tuple-element.50), channel_id=1, replica_groups=mesh['y'=8,'c'=2,'z'=8,'x'=4] {'y','c','z'}, dimensions={0} | all-to-all | bytes 262144 | tf_op jit(solution)/shard_map/all_to_all | solution.py:509
  52.9 0.0 copy-done.2
  52.9 0.0 copy-done.3
  52.9 0.5 shard_map.224
  53.4 0.0 copy-start.4
  53.4 0.0 copy-start.5
  53.5 0.0 copy-start.6
  53.5 9.0 %all_to_all.16.got = f32[4,128,128]{2,1,0:T(8,128)S(1)} all-to-all(f32[4,128,128]{2,1,0:T(8,128)S(1)} %shard_map.224), channel_id=1, replica_groups=mesh['y'=8,'c'=2,'z'=8,'x'=4] {'x'}, dimensions={0} | all-to-all | bytes 524288 | tf_op jit(solution)/shard_map/all_to_all | solution.py:511
  62.5 0.0 copy-done.1
  62.5 0.0 copy-done
  62.5 0.0 copy-done.4
  62.5 0.0 copy-done.5
  62.5 0.0 copy-done.6
  62.5 1.1 %shard_map.225 = f32[128,2,128]{2,1,0:T(2,128)S(1)} custom-call(s32[1,2]{1,0:T(1,128)S(1)} %add_bitcast_fusion.place, f32[4,128,128]{2,1,0:T(8,128)S(1)} %all_to_all.16.got, bf16[1536,256]{1,0:T(8,128)(2,1)S(1)} %copy-done, bf16[4,768,128]{2,1,0:T(8,128)(2,1)S(1)} %copy-done.1, f32[128,1]{1,0:T(8,128)S(1)} %copy-done.5, f32[1,256]{1,0:T(1,128)S(1)} %copy-done.6, ...), custom_call_target="tpu_custom_call" | custom-call | tf_op jit(solution)/shard_map/pallas_call | solution.py:512
  63.5 18.3 %all_to_all.17.got = f32[128,2,128]{2,1,0:T(2,128)S(1)} all-to-all(f32[128,2,128]{2,1,0:T(2,128)S(1)} %shard_map.225), channel_id=1, replica_groups=mesh['y'=8,'c'=2,'z'=8,'x'=4] {'y','c','z'}, dimensions={0} | all-to-all | bytes 262144 | tf_op jit(solution)/shard_map/all_to_all | solution.py:521
  81.9 1.0 %shard_map.226 = f32[5,8,8,128]{3,2,1,0:T(8,128)} custom-call(f32[128,2,128]{2,1,0:T(2,128)S(1)} %all_to_all.17.got, f32[5,8,8,128]{3,2,1,0:T(8,128)S(1)} %get-tuple-element.51.mid, bf16[2,128,128]{2,1,0:T(8,128)(2,1)S(1)} %copy-done.2, bf16[2,128,128]{2,1,0:T(8,128)(2,1)S(1)} %copy-done.3), custom_call_target="tpu_custom_call" | custom-call | tf_op jit(solution)/shard_map/pallas_call | solution.py:522
Async XLA Ops:
  1.8 18.9 %collective-permute-start = (f32[14,8,128]{2,1,0:T(8,128)S(1)}, f32[14,8,128]{2,1,0:T(8,128)S(1)}, u32[]{:S(2)}, u32[]{:S(2)}) collective-permute-start(f32[14,8,128]{2,1,0:T(8,128)S(1)} %get-tuple-element.29), channel_id=1, source_target_pairs={{0,1},{1,2},{2,3},{3,4},{4,5},{5,6},{6,7},{7,8},{8,9},{9,10},{10,1... | collective-permute-start | bytes 172040 | tf_op jit(solution)/shard_map/ppermute | solution.py:477
  5.8 14.9 %collective-permute-start.1 = (f32[14,8,128]{2,1,0:T(8,128)S(1)}, f32[14,8,128]{2,1,0:T(8,128)S(1)}, u32[]{:S(2)}, u32[]{:S(2)}) collective-permute-start(f32[14,8,128]{2,1,0:T(8,128)S(1)} %get-tuple-element.30), channel_id=1, source_target_pairs={{0,31},{1,0},{2,1},{3,2},{4,3},{5,4},{6,5},{7,6},{8,7},{9,8},{10,9... | collective-permute-start | bytes 172040 | tf_op jit(solution)/shard_map/ppermute | solution.py:478
  17.5 4.0 %collective-permute-start.2 = (f32[14,8,128]{2,1,0:T(8,128)S(1)}, f32[14,8,128]{2,1,0:T(8,128)S(1)}, u32[]{:S(2)}, u32[]{:S(2)}) collective-permute-start(f32[14,8,128]{2,1,0:T(8,128)S(1)} %get-tuple-element.31), channel_id=1, source_target_pairs={{0,480},{32,0},{64,32},{96,64},{128,96},{160,128},{192,160},{224,1... | collective-permute-start | bytes 172040 | tf_op jit(solution)/shard_map/ppermute | solution.py:480
  18.4 3.4 %collective-permute-start.3 = (f32[14,8,128]{2,1,0:T(8,128)S(1)}, f32[14,8,128]{2,1,0:T(8,128)S(1)}, u32[]{:S(2)}, u32[]{:S(2)}) collective-permute-start(f32[14,8,128]{2,1,0:T(8,128)S(1)} %get-tuple-element.32), channel_id=1, source_target_pairs={{0,32},{32,64},{64,96},{96,128},{128,160},{160,192},{192,224},{224... | collective-permute-start | bytes 172040 | tf_op jit(solution)/shard_map/ppermute | solution.py:479
  21.8 31.1 %copy-start.2 = (bf16[2,128,128]{2,1,0:T(8,128)(2,1)S(1)}, bf16[2,128,128]{2,1,0:T(8,128)(2,1)}, u32[]{:S(2)}) copy-start(bf16[2,128,128]{2,1,0:T(8,128)(2,1)} %constant.37.clone.fz_far.fx.fz) | copy-start | bytes 196612
  21.8 31.1 %copy-start.3 = (bf16[2,128,128]{2,1,0:T(8,128)(2,1)S(1)}, bf16[2,128,128]{2,1,0:T(8,128)(2,1)}, u32[]{:S(2)}) copy-start(bf16[2,128,128]{2,1,0:T(8,128)(2,1)} %constant.38.clone.dz_far.dx.dz) | copy-start | bytes 196612
  21.8 40.7 %copy-start.1 = (bf16[4,768,128]{2,1,0:T(8,128)(2,1)S(1)}, bf16[4,768,128]{2,1,0:T(8,128)(2,1)}, u32[]{:S(2)}) copy-start(bf16[4,768,128]{2,1,0:T(8,128)(2,1)} %constant.40.clone.back) | copy-start | bytes 2359300
  28.0 34.5 %copy-start = (bf16[1536,256]{1,0:T(8,128)(2,1)S(1)}, bf16[1536,256]{1,0:T(8,128)(2,1)}, u32[]{:S(2)}) copy-start(bf16[1536,256]{1,0:T(8,128)(2,1)} %constant.39.clone.forth) | copy-start | bytes 2359300
  53.4 9.0 %copy-start.4 = (bf16[256,384]{1,0:T(8,128)(2,1)S(1)}, bf16[256,384]{1,0:T(8,128)(2,1)}, u32[]{:S(2)}) copy-start(bf16[256,384]{1,0:T(8,128)(2,1)} %constant.43.clone.left) | copy-start | bytes 589828
  53.4 9.0 %copy-start.5 = (f32[128,1]{1,0:T(8,128)S(1)}, f32[128,1]{1,0:T(8,128)}, u32[]{:S(2)}) copy-start(f32[128,1]{1,0:T(8,128)} %constant.41.clone.kx2) | copy-start | bytes 1540
  53.5 9.0 %copy-start.6 = (f32[1,256]{1,0:T(1,128)S(1)}, f32[1,256]{1,0:T(1,128)}, u32[]{:S(2)}) copy-start(f32[1,256]{1,0:T(1,128)} %constant.42.clone.ky2) | copy-start | bytes 3076

commit v9 on v8

--- a/solution.py
+++ b/solution.py
@@ -177,8 +177,12 @@
     return cut(z), cut(a)
 
 
-def halo_kernel(species, flow, *refs):
-    small, (last_x, first_x, last_y, first_y) = refs[:SMALL], refs[SMALL : SMALL + 4]
+def is_even(place, k):
+    return jnp.broadcast_to(place[:, k : k + 1], (8, NZ)) == 0
+
+
+def halo_kernel(species, flow, odd, *refs):
+    small, (outer_x, inner_x, outer_y, inner_y) = refs[:SMALL], refs[SMALL : SMALL + 4]
     small_out, (own_s, own_f, sems) = refs[SMALL + 4 : -3], refs[-3:]
     pairs = [(species, own_s), (flow, own_f)] + list(zip(small, small_out))
     copies = [pltpu.make_async_copy(a, b, sems.at[k]) for k, (a, b) in enumerate(pairs)]
@@ -188,10 +192,12 @@
         c.wait()
     for f in range(NF):
         src, at = (own_s, f) if f < NSPEC else (own_f, f - NSPEC)
-        last_x[f] = src[at, CX - 1]
-        first_x[f] = src[at, 0]
-        last_y[f] = src[at, :, CY - 1, :]
-        first_y[f] = src[at, :, 0, :]
+        last_x, first_x = src[at, CX - 1], src[at, 0]
+        last_y, first_y = src[at, :, CY - 1, :], src[at, :, 0, :]
+        outer_x[f] = jnp.where(is_even(odd, 0), first_x, last_x)
+        inner_x[f] = jnp.where(is_even(odd, 0), last_x, first_x)
+        outer_y[f] = jnp.where(is_even(odd, 1), first_y, last_y)
+        inner_y[f] = jnp.where(is_even(odd, 1), last_y, first_y)
 
 
 def weights_kernel(classes, left_t, right_t, stoich_t, heat, prefactor, energy, newton, diffusivity, forms, update, energy_col, diff, table):
@@ -208,10 +214,11 @@
 def react_kernel(
     species,
     flow,
-    ylo,
-    yhi,
-    xhi,
-    xlo,
+    outer_y,
+    outer_x,
+    inner_y,
+    inner_x,
+    odd,
     forms,
     update,
     energy_col,
@@ -244,12 +251,16 @@
 
     def transport(f, field):
         coef = diff[f : f + 1, :]
-        ahead_x = jnp.concatenate([field[1:], xhi[f][None]], axis=0)
-        behind_x = jnp.concatenate([xlo[f][None], field[:-1]], axis=0)
+        xlo = jnp.where(is_even(odd, 0), outer_x[f], inner_x[f])
+        xhi = jnp.where(is_even(odd, 0), inner_x[f], outer_x[f])
+        ylo = jnp.where(is_even(odd, 1), outer_y[f], inner_y[f])
+        yhi = jnp.where(is_even(odd, 1), inner_y[f], outer_y[f])
+        ahead_x = jnp.concatenate([field[1:], xhi[None]], axis=0)
+        behind_x = jnp.concatenate([xlo[None], field[:-1]], axis=0)
         up = pltpu.roll(field, CY - 1, 1)
         down = pltpu.roll(field, 1, 1)
-        ahead_y = jnp.stack([jnp.where(ysub == CY - 1, yhi[f, x : x + 1, :], up[x]) for x in range(CX)])
-        behind_y = jnp.stack([jnp.where(ysub == 0, ylo[f, x : x + 1, :], down[x]) for x in range(CX)])
+        ahead_y = jnp.stack([jnp.where(ysub == CY - 1, yhi[x : x + 1, :], up[x]) for x in range(CX)])
+        behind_y = jnp.stack([jnp.where(ysub == 0, ylo[x : x + 1, :], down[x]) for x in range(CX)])
         ahead_z = pltpu.roll(field, NZ - 1, 2)
         behind_z = pltpu.roll(field, 1, 2)
         lap = (ahead_x + behind_x) + (ahead_y + behind_y) + (ahead_z + behind_z) - 6.0 * field
@@ -419,7 +430,7 @@
     return call(
         react_kernel,
         [(NSPEC, CX, CY, NZ), (5, CX, CY, NZ), (NZ, 2, 2 * COLS)],
-        [VMEM] * 11 + [HBM] * 2,
+        [VMEM] * 12 + [HBM] * 2,
         [
             pltpu.VMEM((COLS, ROWS, NZ), F32),
             pltpu.VMEM((COLS, NZ), F32),
@@ -436,10 +447,9 @@
     )(*fields, *halos, *weights, far(fz), far(dz))
 
 
-def ring(axes, n, step):
-    return functools.partial(
-        lax.ppermute, axis_name=axes, perm=[(i, (i + step) % n) for i in range(n)]
-    )
+def swap(axes, n, first):
+    pairs = [(k % n, (k + 1) % n) for k in range(first, n + first, 2)]
+    return functools.partial(lax.ppermute, axis_name=axes, perm=pairs + [(b, a) for a, b in pairs])
 
 
 def shards(
@@ -456,6 +466,7 @@
     newton,
 ):
     n_gx, n_gy = NX // CX, NY // CY
+    odd = (jnp.stack([lax.axis_index(GX), lax.axis_index(GY)]) % 2).astype(jnp.int32)[None, :]
     row = lambda v: v[None, :]
     small = (
         classes,
@@ -471,13 +482,16 @@
     edges = call(
         halo_kernel,
         [(NF, 8, NZ)] * 4 + [(v.shape, v.dtype) for v in small] + [species.shape, flow.shape],
-        [HBM] * (2 + SMALL),
+        [HBM] * 2 + [VMEM] + [HBM] * SMALL,
         [pltpu.SemaphoreType.DMA((2 + SMALL,))],
-    )(far(species), far(flow), *(far(v) for v in small))
-    ylo = ring(GY, n_gy, 1)(edges[2])
-    yhi = ring(GY, n_gy, -1)(edges[3])
-    xlo = ring(GX, n_gx, 1)(edges[0])
-    xhi = ring(GX, n_gx, -1)(edges[1])
+    )(far(species), far(flow), odd, *(far(v) for v in small))
+    halos = (
+        swap(GY, n_gy, 1)(edges[2]),
+        swap(GX, n_gx, 1)(edges[0]),
+        swap(GY, n_gy, 0)(edges[3]),
+        swap(GX, n_gx, 0)(edges[1]),
+        odd,
+    )
 
     fz, dz, _ = basis(NZ)
     fy, dy, ky = basis(NY)
@@ -499,7 +513,7 @@
 
     species_out, mid, spectra = react(
         edges[-2:],
-        (ylo, yhi, xhi, xlo),
+        halos,
         edges[4:-2],
         table(fz),
         table(dz),

time: 83.2 us -> 83.6 us (level)
  starting transfers between devices: 17.8 us -> 23 us
  blocking collectives: 52.3 us -> 47.4 us
  waiting for transfers between devices: 1.06 us -> 0.01 us
  Pallas kernels: 10.9 us -> 11.9 us
    all_to_all x1, blocking collectives: 24.9 us -> 19.5 us  [shards(): got = lax.all_to_all(spectra, MODES, 0, 0, tiled=True)]
    ppermute x4, starting transfers between devices: 17.8 us -> 23 us  [the longest x1 13.7 us: shards(): swap(GY, n_gy, 1)(edges[2])]
    ppermute x4, waiting for transfers between devices: 1.06 us -> 0.01 us  [the longest x1 0.01 us: shards(): swap(GY, n_gy, 1)(edges[2])]
    pallas_call x1, Pallas kernels: 6.14 us -> 7.01 us  [react(): call(react_kernel, [(NSPEC, CX, CY, NZ), (5, CX, CY, NZ), (NZ, 2, 2 * COL...]
  transfers between devices with their start and end apart: 4 -> 4, of which waited for: 2 -> 0; matrix products, arithmetic and copies ran while one was open for 0% -> 0% of each run, Pallas kernels for 1% -> 1%
where the time goes in v9:
time: 83.6 us; the launch traced here: 83.3 us
  blocking collectives  47.4 us (57%)
  starting transfers between devices  23 us (28%)
  Pallas kernels  11.9 us (14%)
    all_to_all x1, blocking collectives, shards(): got = lax.all_to_all(spectra, MODES, 0, 0, tiled=True)  19.5 us
    all_to_all x1, blocking collectives, shards(): got = lax.all_to_all(grads, MODES, 0, 0, tiled=True)  18.9 us
    ppermute x1, starting transfers between devices, shards(): swap(GY, n_gy, 1)(edges[2])  13.7 us
    all_to_all x1, blocking collectives, shards(): lines = lax.all_to_all(lines, 'x', 0, 0, tiled=True)  8.94 us
    pallas_call x1, Pallas kernels, react(): call(react_kernel, [(NSPEC, CX, CY, NZ), (5, CX, CY, NZ), (NZ, 2, 2 * COL...  7.01 us
    ppermute x1, starting transfers between devices, shards(): swap(GX, n_gx, 1)(edges[0])  4.05 us
    ppermute x1, starting transfers between devices, shards(): swap(GX, n_gx, 0)(edges[1])  3.36 us
    ppermute x1, starting transfers between devices, shards(): swap(GY, n_gy, 0)(edges[3])  1.92 us
  transfers between devices with their start and end apart: 4, of which 0 were waited for; matrix products, arithmetic and copies ran while one was open for 0% of the time, Pallas kernels for 1%

profile of v9, /device:TPU:1, one launch (start us, length us, event | category | flops | bytes accessed | tf_op | source)
XLA Modules:
  0.0 83.3 jit_solution(3775812041584074376)
XLA Ops:
  0.6 0.1 and_select_fusion.odd
  0.7 1.3 %shard_map.221 = (f32[14,8,128]{2,1,0:T(8,128)S(1)}, f32[14,8,128]{2,1,0:T(8,128)S(1)}, f32[14,8,128]{2,1,0:T(8,128)S(1)}, f32[14,8,128]{2,1,0:T(8,128)S(1)}, s3...) custom-call(f32[9,8,8,128]{3,2,1,0:T(8,128)} %species.1, ...), custom_call_target="tpu_custom_call" | custom-call | tf_op jit(solution)/shard_map/pallas_call | solution.py:482
  2.0 13.7 %collective-permute-start = (f32[14,8,128]{2,1,0:T(8,128)S(1)}, f32[14,8,128]{2,1,0:T(8,128)S(1)}, u32[]{:S(2)}, u32[]{:S(2)}) collective-permute-start(f32[14,8,128]{2,1,0:T(8,128)S(1)} %get-tuple-element.29), channel_id=1, source_target_pairs={{1,2},{3,4},{5,6},{7,8},{9,10},{11,12},{13,14},{15,16},{17,18},{19... | collective-permute-start | bytes 172040 | tf_op jit(solution)/shard_map/ppermute | solution.py:489
  15.7 4.0 %collective-permute-start.1 = (f32[14,8,128]{2,1,0:T(8,128)S(1)}, f32[14,8,128]{2,1,0:T(8,128)S(1)}, u32[]{:S(2)}, u32[]{:S(2)}) collective-permute-start(f32[14,8,128]{2,1,0:T(8,128)S(1)} %get-tuple-element.30), channel_id=1, source_target_pairs={{32,64},{96,128},{160,192},{224,256},{288,320},{352,384},{416,448}... | collective-permute-start | bytes 172040 | tf_op jit(solution)/shard_map/ppermute | solution.py:490
  19.8 1.9 %collective-permute-start.2 = (f32[14,8,128]{2,1,0:T(8,128)S(1)}, f32[14,8,128]{2,1,0:T(8,128)S(1)}, u32[]{:S(2)}, u32[]{:S(2)}) collective-permute-start(f32[14,8,128]{2,1,0:T(8,128)S(1)} %get-tuple-element.31), channel_id=1, source_target_pairs={{0,1},{2,3},{4,5},{6,7},{8,9},{10,11},{12,13},{14,15},{16,17},{18,... | collective-permute-start | bytes 172040 | tf_op jit(solution)/shard_map/ppermute | solution.py:491
  21.7 3.4 %collective-permute-start.3 = (f32[14,8,128]{2,1,0:T(8,128)S(1)}, f32[14,8,128]{2,1,0:T(8,128)S(1)}, u32[]{:S(2)}, u32[]{:S(2)}) collective-permute-start(f32[14,8,128]{2,1,0:T(8,128)S(1)} %get-tuple-element.32), channel_id=1, source_target_pairs={{0,32},{64,96},{128,160},{192,224},{256,288},{320,352},{384,416},{... | collective-permute-start | bytes 172040 | tf_op jit(solution)/shard_map/ppermute | solution.py:492
  25.1 1.0 %shard_map.222 = (bf16[160,192]{1,0:T(8,128)(2,1)S(1)}, bf16[64,96]{1,0:T(8,128)(2,1)S(1)}, f32[24,128]{1,0:T(8,128)S(1)}, f32[16,128]{1,0:T(8,128)S(1)}, s32[8,128]{1,0:T(8,128)S(1)}) custom-call(s32[8,8]{1,0:T(8,128)S(1)} %get-tuple-element.33.classes, f32[9,19]{1,0:T(8,128)S(1)} %get-tuple-element.34.left_t, f32[9,19]{1,0:T(8,128)S(1)} %get-tuple-element.35.right_t, ...), custom_call_target="tpu_custom_call" | custom-call | tf_op jit(solution)/shard_map/pallas_call | solution.py:419
  26.1 0.1 add_bitcast_fusion.place
  26.2 0.0 collective-permute-done.outer_y
  26.2 0.0 collective-permute-done.1.outer_x
  26.2 0.0 collective-permute-done.2.inner_y
  26.2 0.0 collective-permute-done.3.inner_x
  26.2 0.0 copy-start.2
  26.2 0.0 copy-start.3
  26.2 0.0 copy-start.1
  26.2 7.0 %shard_map.223 = (f32[9,8,8,128]{3,2,1,0:T(8,128)}, f32[5,8,8,128]{3,2,1,0:T(8,128)S(1)}, f32[128,2,128]{2,1,0:T(2,128)S(1)}) custom-call(f32[9,8,8,128]{3,2,1,0:T(8,128)S(1)} %get-tuple-element.27.species, f32[5,8,8,128]{3,2,1,0:T(8,128)S(1)} %get-tuple-element.28.flow, f32[14,8,128]{2,1,0:T(8,128)S(1)} %collective-permute-done.outer_y, ...), custom_call_target="tpu_custom_call" | custom-call | tf_op jit(solution)/shard_map/pallas_call | solution.py:430
  33.3 0.0 copy-start
  33.3 19.5 %all_to_all.15.got = f32[128,2,128]{2,1,0:T(2,128)S(1)} all-to-all(f32[128,2,128]{2,1,0:T(2,128)S(1)} %get-tuple-element.50), channel_id=1, replica_groups=mesh['y'=8,'c'=2,'z'=8,'x'=4] {'y','c','z'}, dimensions={0} | all-to-all | bytes 262144 | tf_op jit(solution)/shard_map/all_to_all | solution.py:523
  52.8 0.0 copy-done.2
  52.8 0.0 copy-done.3
  52.8 0.5 shard_map.224
  53.3 0.0 copy-start.4
  53.3 0.0 copy-start.5
  53.3 0.0 copy-start.6
  53.3 8.9 %all_to_all.16.got = f32[4,128,128]{2,1,0:T(8,128)S(1)} all-to-all(f32[4,128,128]{2,1,0:T(8,128)S(1)} %shard_map.224), channel_id=1, replica_groups=mesh['y'=8,'c'=2,'z'=8,'x'=4] {'x'}, dimensions={0} | all-to-all | bytes 524288 | tf_op jit(solution)/shard_map/all_to_all | solution.py:525
  62.3 0.0 copy-done.1
  62.3 0.0 copy-done
  62.3 0.0 copy-done.4
  62.3 0.0 copy-done.5
  62.3 0.0 copy-done.6
  62.3 1.1 %shard_map.225 = f32[128,2,128]{2,1,0:T(2,128)S(1)} custom-call(s32[1,2]{1,0:T(1,128)S(1)} %add_bitcast_fusion.place, f32[4,128,128]{2,1,0:T(8,128)S(1)} %all_to_all.16.got, bf16[1536,256]{1,0:T(8,128)(2,1)S(1)} %copy-done.1, bf16[4,768,128]{2,1,0:T(8,128)(2,1)S(1)} %copy-done, f32[128,1]{1,0:T(8,128)S(1)} %copy-done.5, f32[1,256]{1,0:T(1,128)S(1)} %copy-done.6, ...), custom_call_target="tpu_custom_call" | custom-call | tf_op jit(solution)/shard_map/pallas_call | solution.py:526
  63.4 18.9 %all_to_all.17.got = f32[128,2,128]{2,1,0:T(2,128)S(1)} all-to-all(f32[128,2,128]{2,1,0:T(2,128)S(1)} %shard_map.225), channel_id=1, replica_groups=mesh['y'=8,'c'=2,'z'=8,'x'=4] {'y','c','z'}, dimensions={0} | all-to-all | bytes 262144 | tf_op jit(solution)/shard_map/all_to_all | solution.py:535
  82.3 1.0 %shard_map.226 = f32[5,8,8,128]{3,2,1,0:T(8,128)} custom-call(f32[128,2,128]{2,1,0:T(2,128)S(1)} %all_to_all.17.got, f32[5,8,8,128]{3,2,1,0:T(8,128)S(1)} %get-tuple-element.51.mid, bf16[2,128,128]{2,1,0:T(8,128)(2,1)S(1)} %copy-done.3, bf16[2,128,128]{2,1,0:T(8,128)(2,1)S(1)} %copy-done.2), custom_call_target="tpu_custom_call" | custom-call | tf_op jit(solution)/shard_map/pallas_call | solution.py:536
Async XLA Ops:
  2.0 24.2 %collective-permute-start = (f32[14,8,128]{2,1,0:T(8,128)S(1)}, f32[14,8,128]{2,1,0:T(8,128)S(1)}, u32[]{:S(2)}, u32[]{:S(2)}) collective-permute-start(f32[14,8,128]{2,1,0:T(8,128)S(1)} %get-tuple-element.29), channel_id=1, source_target_pairs={{1,2},{3,4},{5,6},{7,8},{9,10},{11,12},{13,14},{15,16},{17,18},{19... | collective-permute-start | bytes 172040 | tf_op jit(solution)/shard_map/ppermute | solution.py:489
  15.7 10.5 %collective-permute-start.1 = (f32[14,8,128]{2,1,0:T(8,128)S(1)}, f32[14,8,128]{2,1,0:T(8,128)S(1)}, u32[]{:S(2)}, u32[]{:S(2)}) collective-permute-start(f32[14,8,128]{2,1,0:T(8,128)S(1)} %get-tuple-element.30), channel_id=1, source_target_pairs={{32,64},{96,128},{160,192},{224,256},{288,320},{352,384},{416,448}... | collective-permute-start | bytes 172040 | tf_op jit(solution)/shard_map/ppermute | solution.py:490
  19.8 6.4 %collective-permute-start.2 = (f32[14,8,128]{2,1,0:T(8,128)S(1)}, f32[14,8,128]{2,1,0:T(8,128)S(1)}, u32[]{:S(2)}, u32[]{:S(2)}) collective-permute-start(f32[14,8,128]{2,1,0:T(8,128)S(1)} %get-tuple-element.31), channel_id=1, source_target_pairs={{0,1},{2,3},{4,5},{6,7},{8,9},{10,11},{12,13},{14,15},{16,17},{18,... | collective-permute-start | bytes 172040 | tf_op jit(solution)/shard_map/ppermute | solution.py:491
  21.7 4.5 %collective-permute-start.3 = (f32[14,8,128]{2,1,0:T(8,128)S(1)}, f32[14,8,128]{2,1,0:T(8,128)S(1)}, u32[]{:S(2)}, u32[]{:S(2)}) collective-permute-start(f32[14,8,128]{2,1,0:T(8,128)S(1)} %get-tuple-element.32), channel_id=1, source_target_pairs={{0,32},{64,96},{128,160},{192,224},{256,288},{320,352},{384,416},{... | collective-permute-start | bytes 172040 | tf_op jit(solution)/shard_map/ppermute | solution.py:492
  26.2 26.6 %copy-start.2 = (bf16[2,128,128]{2,1,0:T(8,128)(2,1)S(1)}, bf16[2,128,128]{2,1,0:T(8,128)(2,1)}, u32[]{:S(2)}) copy-start(bf16[2,128,128]{2,1,0:T(8,128)(2,1)} %constant.55.clone.dz_far.dx.dz) | copy-start | bytes 196612
  26.2 26.6 %copy-start.3 = (bf16[2,128,128]{2,1,0:T(8,128)(2,1)S(1)}, bf16[2,128,128]{2,1,0:T(8,128)(2,1)}, u32[]{:S(2)}) copy-start(bf16[2,128,128]{2,1,0:T(8,128)(2,1)} %constant.54.clone.fz_far.fx.fz) | copy-start | bytes 196612
  26.2 36.0 %copy-start.1 = (bf16[1536,256]{1,0:T(8,128)(2,1)S(1)}, bf16[1536,256]{1,0:T(8,128)(2,1)}, u32[]{:S(2)}) copy-start(bf16[1536,256]{1,0:T(8,128)(2,1)} %constant.56.clone.forth) | copy-start | bytes 2359300
  33.3 29.0 %copy-start = (bf16[4,768,128]{2,1,0:T(8,128)(2,1)S(1)}, bf16[4,768,128]{2,1,0:T(8,128)(2,1)}, u32[]{:S(2)}) copy-start(bf16[4,768,128]{2,1,0:T(8,128)(2,1)} %constant.57.clone.back) | copy-start | bytes 2359300
  53.3 9.0 %copy-start.4 = (bf16[256,384]{1,0:T(8,128)(2,1)S(1)}, bf16[256,384]{1,0:T(8,128)(2,1)}, u32[]{:S(2)}) copy-start(bf16[256,384]{1,0:T(8,128)(2,1)} %constant.60.clone.left) | copy-start | bytes 589828
  53.3 9.0 %copy-start.5 = (f32[128,1]{1,0:T(8,128)S(1)}, f32[128,1]{1,0:T(8,128)}, u32[]{:S(2)}) copy-start(f32[128,1]{1,0:T(8,128)} %constant.58.clone.kx2) | copy-start | bytes 1540
  53.3 9.0 %copy-start.6 = (f32[1,256]{1,0:T(1,128)S(1)}, f32[1,256]{1,0:T(1,128)}, u32[]{:S(2)}) copy-start(f32[1,256]{1,0:T(1,128)} %constant.59.clone.ky2) | copy-start | bytes 3076

commit v10 on v9

--- a/solution.py
+++ b/solution.py
@@ -177,12 +177,12 @@
     return cut(z), cut(a)
 
 
-def is_even(place, k):
-    return jnp.broadcast_to(place[:, k : k + 1], (8, NZ)) == 0
+def is_even(odd):
+    return jnp.broadcast_to(odd[...], (8, NZ)) == 0
 
 
 def halo_kernel(species, flow, odd, *refs):
-    small, (outer_x, inner_x, outer_y, inner_y) = refs[:SMALL], refs[SMALL : SMALL + 4]
+    small, (end_x, start_x, outer_y, inner_y) = refs[:SMALL], refs[SMALL : SMALL + 4]
     small_out, (own_s, own_f, sems) = refs[SMALL + 4 : -3], refs[-3:]
     pairs = [(species, own_s), (flow, own_f)] + list(zip(small, small_out))
     copies = [pltpu.make_async_copy(a, b, sems.at[k]) for k, (a, b) in enumerate(pairs)]
@@ -192,12 +192,11 @@
         c.wait()
     for f in range(NF):
         src, at = (own_s, f) if f < NSPEC else (own_f, f - NSPEC)
-        last_x, first_x = src[at, CX - 1], src[at, 0]
         last_y, first_y = src[at, :, CY - 1, :], src[at, :, 0, :]
-        outer_x[f] = jnp.where(is_even(odd, 0), first_x, last_x)
-        inner_x[f] = jnp.where(is_even(odd, 0), last_x, first_x)
-        outer_y[f] = jnp.where(is_even(odd, 1), first_y, last_y)
-        inner_y[f] = jnp.where(is_even(odd, 1), last_y, first_y)
+        end_x[f] = src[at, CX - 1]
+        start_x[f] = src[at, 0]
+        outer_y[f] = jnp.where(is_even(odd), first_y, last_y)
+        inner_y[f] = jnp.where(is_even(odd), last_y, first_y)
 
 
 def weights_kernel(classes, left_t, right_t, stoich_t, heat, prefactor, energy, newton, diffusivity, forms, update, energy_col, diff, table):
@@ -215,9 +214,9 @@
     species,
     flow,
     outer_y,
-    outer_x,
     inner_y,
-    inner_x,
+    xhi,
+    xlo,
     odd,
     forms,
     update,
@@ -251,12 +250,10 @@
 
     def transport(f, field):
         coef = diff[f : f + 1, :]
-        xlo = jnp.where(is_even(odd, 0), outer_x[f], inner_x[f])
-        xhi = jnp.where(is_even(odd, 0), inner_x[f], outer_x[f])
-        ylo = jnp.where(is_even(odd, 1), outer_y[f], inner_y[f])
-        yhi = jnp.where(is_even(odd, 1), inner_y[f], outer_y[f])
-        ahead_x = jnp.concatenate([field[1:], xhi[None]], axis=0)
-        behind_x = jnp.concatenate([xlo[None], field[:-1]], axis=0)
+        ylo = jnp.where(is_even(odd), outer_y[f], inner_y[f])
+        yhi = jnp.where(is_even(odd), inner_y[f], outer_y[f])
+        ahead_x = jnp.concatenate([field[1:], xhi[f][None]], axis=0)
+        behind_x = jnp.concatenate([xlo[f][None], field[:-1]], axis=0)
         up = pltpu.roll(field, CY - 1, 1)
         down = pltpu.roll(field, 1, 1)
         ahead_y = jnp.stack([jnp.where(ysub == CY - 1, yhi[x : x + 1, :], up[x]) for x in range(CX)])
@@ -452,6 +449,12 @@
     return functools.partial(lax.ppermute, axis_name=axes, perm=pairs + [(b, a) for a, b in pairs])
 
 
+def shift(axes, n, step):
+    return functools.partial(
+        lax.ppermute, axis_name=axes, perm=[(i, (i + step) % n) for i in range(n)]
+    )
+
+
 def shards(
     species,
     flow,
@@ -466,7 +469,7 @@
     newton,
 ):
     n_gx, n_gy = NX // CX, NY // CY
-    odd = (jnp.stack([lax.axis_index(GX), lax.axis_index(GY)]) % 2).astype(jnp.int32)[None, :]
+    odd = (lax.axis_index(GY) % 2).astype(jnp.int32).reshape(1, 1)
     row = lambda v: v[None, :]
     small = (
         classes,
@@ -487,9 +490,9 @@
     )(far(species), far(flow), odd, *(far(v) for v in small))
     halos = (
         swap(GY, n_gy, 1)(edges[2]),
-        swap(GX, n_gx, 1)(edges[0]),
         swap(GY, n_gy, 0)(edges[3]),
-        swap(GX, n_gx, 0)(edges[1]),
+        shift(GX, n_gx, -1)(edges[1]),
+        shift(GX, n_gx, 1)(edges[0]),
         odd,
     )
 

time: 83.6 us -> 81.8 us (0.978)
  starting transfers between devices: 23 us -> 17.8 us
  blocking collectives: 47.4 us -> 50.9 us
  Pallas kernels: 11.9 us -> 10.8 us
  waiting for transfers between devices: 0.01 us -> 1.06 us
    ppermute x2, starting transfers between devices: 7.4 us -> 2.17 us  [the longest x1 1.21 us: shards(): shift(GX, n_gx, 1)(edges[0])]
    all_to_all x1, blocking collectives: 19.5 us -> 23.2 us  [shards(): got = lax.all_to_all(spectra, MODES, 0, 0, tiled=True)]
    pallas_call x1, Pallas kernels: 7.01 us -> 5.95 us  [react(): call(react_kernel, [(NSPEC, CX, CY, NZ), (5, CX, CY, NZ), (NZ, 2, 2 * COL...]
    ppermute x2, waiting for transfers between devices: 0.01 us -> 1.06 us  [the longest x1 1.04 us: shards(): shift(GX, n_gx, -1)(edges[1])]
  transfers between devices with their start and end apart: 4 -> 4, of which waited for: 0 -> 1; matrix products, arithmetic and copies ran while one was open for 0% -> 0% of each run, Pallas kernels for 1% -> 1%
where the time goes in v10:
time: 81.8 us; the launch traced here: 81.5 us
  blocking collectives  50.9 us (62%)
  starting transfers between devices  17.8 us (22%)
  Pallas kernels  10.8 us (13%)
  waiting for transfers between devices  1.06 us (1%)
    all_to_all x1, blocking collectives, shards(): got = lax.all_to_all(spectra, MODES, 0, 0, tiled=True)  23.2 us
    all_to_all x1, blocking collectives, shards(): got = lax.all_to_all(grads, MODES, 0, 0, tiled=True)  18.9 us
    ppermute x1, starting transfers between devices, shards(): swap(GY, n_gy, 1)(edges[2])  13.7 us
    all_to_all x1, blocking collectives, shards(): lines = lax.all_to_all(lines, 'x', 0, 0, tiled=True)  8.83 us
    pallas_call x1, Pallas kernels, react(): call(react_kernel, [(NSPEC, CX, CY, NZ), (5, CX, CY, NZ), (NZ, 2, 2 * COL...  5.95 us
    ppermute x1, starting transfers between devices, shards(): swap(GY, n_gy, 0)(edges[3])  1.92 us
  transfers between devices with their start and end apart: 4, of which 1 were waited for; matrix products, arithmetic and copies ran while one was open for 0% of the time, Pallas kernels for 1%

profile of v10, /device:TPU:1, one launch (start us, length us, event | category | flops | bytes accessed | tf_op | source)
XLA Modules:
  0.0 81.5 jit_solution(8576013718525359140)
XLA Ops:
  0.6 1.3 %shard_map.221 = (f32[14,8,128]{2,1,0:T(8,128)S(1)}, f32[14,8,128]{2,1,0:T(8,128)S(1)}, f32[14,8,128]{2,1,0:T(8,128)S(1)}, f32[14,8,128]{2,1,0:T(8,128)S(1)}, s3...) custom-call(f32[9,8,8,128]{3,2,1,0:T(8,128)} %species.1, ...), custom_call_target="tpu_custom_call" | custom-call | tf_op jit(solution)/shard_map/pallas_call | solution.py:485
  1.9 13.7 %collective-permute-start = (f32[14,8,128]{2,1,0:T(8,128)S(1)}, f32[14,8,128]{2,1,0:T(8,128)S(1)}, u32[]{:S(2)}, u32[]{:S(2)}) collective-permute-start(f32[14,8,128]{2,1,0:T(8,128)S(1)} %get-tuple-element.29), channel_id=1, source_target_pairs={{1,2},{3,4},{5,6},{7,8},{9,10},{11,12},{13,14},{15,16},{17,18},{19... | collective-permute-start | bytes 172040 | tf_op jit(solution)/shard_map/ppermute | solution.py:492
  15.6 1.9 %collective-permute-start.1 = (f32[14,8,128]{2,1,0:T(8,128)S(1)}, f32[14,8,128]{2,1,0:T(8,128)S(1)}, u32[]{:S(2)}, u32[]{:S(2)}) collective-permute-start(f32[14,8,128]{2,1,0:T(8,128)S(1)} %get-tuple-element.30), channel_id=1, source_target_pairs={{0,1},{2,3},{4,5},{6,7},{8,9},{10,11},{12,13},{14,15},{16,17},{18,... | collective-permute-start | bytes 172040 | tf_op jit(solution)/shard_map/ppermute | solution.py:493
  17.6 1.0 %collective-permute-start.2 = (f32[14,8,128]{2,1,0:T(8,128)S(1)}, f32[14,8,128]{2,1,0:T(8,128)S(1)}, u32[]{:S(2)}, u32[]{:S(2)}) collective-permute-start(f32[14,8,128]{2,1,0:T(8,128)S(1)} %get-tuple-element.31), channel_id=1, source_target_pairs={{0,480},{32,0},{64,32},{96,64},{128,96},{160,128},{192,160},{224,1... | collective-permute-start | bytes 172040 | tf_op jit(solution)/shard_map/ppermute | solution.py:494
  18.5 1.2 %collective-permute-start.3 = (f32[14,8,128]{2,1,0:T(8,128)S(1)}, f32[14,8,128]{2,1,0:T(8,128)S(1)}, u32[]{:S(2)}, u32[]{:S(2)}) collective-permute-start(f32[14,8,128]{2,1,0:T(8,128)S(1)} %get-tuple-element.32), channel_id=1, source_target_pairs={{0,32},{32,64},{64,96},{96,128},{128,160},{160,192},{192,224},{224... | collective-permute-start | bytes 172040 | tf_op jit(solution)/shard_map/ppermute | solution.py:495
  19.7 1.0 %shard_map.222 = (bf16[160,192]{1,0:T(8,128)(2,1)S(1)}, bf16[64,96]{1,0:T(8,128)(2,1)S(1)}, f32[24,128]{1,0:T(8,128)S(1)}, f32[16,128]{1,0:T(8,128)S(1)}, s32[8,128]{1,0:T(8,128)S(1)}) custom-call(s32[8,8]{1,0:T(8,128)S(1)} %get-tuple-element.33.classes, f32[9,19]{1,0:T(8,128)S(1)} %get-tuple-element.34.left_t, f32[9,19]{1,0:T(8,128)S(1)} %get-tuple-element.35.right_t, ...), custom_call_target="tpu_custom_call" | custom-call | tf_op jit(solution)/shard_map/pallas_call | solution.py:416
  20.8 0.1 add_bitcast_fusion.place
  20.8 0.0 collective-permute-done.outer_y
  20.8 0.0 collective-permute-done.1.inner_y
  20.8 1.0 %collective-permute-done.2.xhi = f32[14,8,128]{2,1,0:T(8,128)S(1)} collective-permute-done((f32[14,8,128]{2,1,0:T(8,128)S(1)}, f32[14,8,128]{2,1,0:T(8,128)S(1)}, u32[]{:S(2)}, u32[]{:S(2)}) %collective-permute-start.2) | collective-permute-done | bytes 57376 | tf_op jit(solution)/shard_map/ppermute | solution.py:494
  21.9 0.0 collective-permute-done.3.xlo
  21.9 0.0 copy-start.2
  21.9 0.0 copy-start.3
  21.9 0.0 copy-start.1
  21.9 5.9 %shard_map.223 = (f32[9,8,8,128]{3,2,1,0:T(8,128)}, f32[5,8,8,128]{3,2,1,0:T(8,128)S(1)}, f32[128,2,128]{2,1,0:T(2,128)S(1)}) custom-call(f32[9,8,8,128]{3,2,1,0:T(8,128)S(1)} %get-tuple-element.27.species, f32[5,8,8,128]{3,2,1,0:T(8,128)S(1)} %get-tuple-element.28.flow, f32[14,8,128]{2,1,0:T(8,128)S(1)} %collective-permute-done.outer_y, ...), custom_call_target="tpu_custom_call" | custom-call | tf_op jit(solution)/shard_map/pallas_call | solution.py:427
  27.9 0.0 copy-start
  27.9 23.2 %all_to_all.15.got = f32[128,2,128]{2,1,0:T(2,128)S(1)} all-to-all(f32[128,2,128]{2,1,0:T(2,128)S(1)} %get-tuple-element.50), channel_id=1, replica_groups=mesh['y'=8,'c'=2,'z'=8,'x'=4] {'y','c','z'}, dimensions={0} | all-to-all | bytes 262144 | tf_op jit(solution)/shard_map/all_to_all | solution.py:526
  51.1 0.0 copy-done.2
  51.1 0.0 copy-done.3
  51.1 0.5 shard_map.224
  51.6 0.0 copy-start.4
  51.6 0.0 copy-start.5
  51.6 0.0 copy-start.6
  51.6 8.8 %all_to_all.16.got = f32[4,128,128]{2,1,0:T(8,128)S(1)} all-to-all(f32[4,128,128]{2,1,0:T(8,128)S(1)} %shard_map.224), channel_id=1, replica_groups=mesh['y'=8,'c'=2,'z'=8,'x'=4] {'x'}, dimensions={0} | all-to-all | bytes 524288 | tf_op jit(solution)/shard_map/all_to_all | solution.py:528
  60.4 0.0 copy-done.1
  60.4 0.0 copy-done
  60.4 0.0 copy-done.4
  60.5 0.0 copy-done.5
  60.5 0.0 copy-done.6
  60.5 1.1 %shard_map.225 = f32[128,2,128]{2,1,0:T(2,128)S(1)} custom-call(s32[1,2]{1,0:T(1,128)S(1)} %add_bitcast_fusion.place, f32[4,128,128]{2,1,0:T(8,128)S(1)} %all_to_all.16.got, bf16[1536,256]{1,0:T(8,128)(2,1)S(1)} %copy-done.1, bf16[4,768,128]{2,1,0:T(8,128)(2,1)S(1)} %copy-done, f32[128,1]{1,0:T(8,128)S(1)} %copy-done.5, f32[1,256]{1,0:T(1,128)S(1)} %copy-done.6, ...), custom_call_target="tpu_custom_call" | custom-call | tf_op jit(solution)/shard_map/pallas_call | solution.py:529
  61.5 18.9 %all_to_all.17.got = f32[128,2,128]{2,1,0:T(2,128)S(1)} all-to-all(f32[128,2,128]{2,1,0:T(2,128)S(1)} %shard_map.225), channel_id=1, replica_groups=mesh['y'=8,'c'=2,'z'=8,'x'=4] {'y','c','z'}, dimensions={0} | all-to-all | bytes 262144 | tf_op jit(solution)/shard_map/all_to_all | solution.py:538
  80.5 1.0 %shard_map.226 = f32[5,8,8,128]{3,2,1,0:T(8,128)} custom-call(f32[128,2,128]{2,1,0:T(2,128)S(1)} %all_to_all.17.got, f32[5,8,8,128]{3,2,1,0:T(8,128)S(1)} %get-tuple-element.51.mid, bf16[2,128,128]{2,1,0:T(8,128)(2,1)S(1)} %copy-done.3, bf16[2,128,128]{2,1,0:T(8,128)(2,1)S(1)} %copy-done.2), custom_call_target="tpu_custom_call" | custom-call | tf_op jit(solution)/shard_map/pallas_call | solution.py:539
Async XLA Ops:
  1.9 18.9 %collective-permute-start = (f32[14,8,128]{2,1,0:T(8,128)S(1)}, f32[14,8,128]{2,1,0:T(8,128)S(1)}, u32[]{:S(2)}, u32[]{:S(2)}) collective-permute-start(f32[14,8,128]{2,1,0:T(8,128)S(1)} %get-tuple-element.29), channel_id=1, source_target_pairs={{1,2},{3,4},{5,6},{7,8},{9,10},{11,12},{13,14},{15,16},{17,18},{19... | collective-permute-start | bytes 172040 | tf_op jit(solution)/shard_map/ppermute | solution.py:492
  15.6 5.2 %collective-permute-start.1 = (f32[14,8,128]{2,1,0:T(8,128)S(1)}, f32[14,8,128]{2,1,0:T(8,128)S(1)}, u32[]{:S(2)}, u32[]{:S(2)}) collective-permute-start(f32[14,8,128]{2,1,0:T(8,128)S(1)} %get-tuple-element.30), channel_id=1, source_target_pairs={{0,1},{2,3},{4,5},{6,7},{8,9},{10,11},{12,13},{14,15},{16,17},{18,... | collective-permute-start | bytes 172040 | tf_op jit(solution)/shard_map/ppermute | solution.py:493
  17.6 4.3 %collective-permute-start.2 = (f32[14,8,128]{2,1,0:T(8,128)S(1)}, f32[14,8,128]{2,1,0:T(8,128)S(1)}, u32[]{:S(2)}, u32[]{:S(2)}) collective-permute-start(f32[14,8,128]{2,1,0:T(8,128)S(1)} %get-tuple-element.31), channel_id=1, source_target_pairs={{0,480},{32,0},{64,32},{96,64},{128,96},{160,128},{192,160},{224,1... | collective-permute-start | bytes 172040 | tf_op jit(solution)/shard_map/ppermute | solution.py:494
  18.5 3.4 %collective-permute-start.3 = (f32[14,8,128]{2,1,0:T(8,128)S(1)}, f32[14,8,128]{2,1,0:T(8,128)S(1)}, u32[]{:S(2)}, u32[]{:S(2)}) collective-permute-start(f32[14,8,128]{2,1,0:T(8,128)S(1)} %get-tuple-element.32), channel_id=1, source_target_pairs={{0,32},{32,64},{64,96},{96,128},{128,160},{160,192},{192,224},{224... | collective-permute-start | bytes 172040 | tf_op jit(solution)/shard_map/ppermute | solution.py:495
  21.9 29.2 %copy-start.2 = (bf16[2,128,128]{2,1,0:T(8,128)(2,1)S(1)}, bf16[2,128,128]{2,1,0:T(8,128)(2,1)}, u32[]{:S(2)}) copy-start(bf16[2,128,128]{2,1,0:T(8,128)(2,1)} %constant.53.clone.dz_far.dx.dz) | copy-start | bytes 196612
  21.9 29.2 %copy-start.3 = (bf16[2,128,128]{2,1,0:T(8,128)(2,1)S(1)}, bf16[2,128,128]{2,1,0:T(8,128)(2,1)}, u32[]{:S(2)}) copy-start(bf16[2,128,128]{2,1,0:T(8,128)(2,1)} %constant.52.clone.fz_far.fx.fz) | copy-start | bytes 196612
  21.9 38.5 %copy-start.1 = (bf16[1536,256]{1,0:T(8,128)(2,1)S(1)}, bf16[1536,256]{1,0:T(8,128)(2,1)}, u32[]{:S(2)}) copy-start(bf16[1536,256]{1,0:T(8,128)(2,1)} %constant.54.clone.forth) | copy-start | bytes 2359300
  27.9 32.6 %copy-start = (bf16[4,768,128]{2,1,0:T(8,128)(2,1)S(1)}, bf16[4,768,128]{2,1,0:T(8,128)(2,1)}, u32[]{:S(2)}) copy-start(bf16[4,768,128]{2,1,0:T(8,128)(2,1)} %constant.55.clone.back) | copy-start | bytes 2359300
  51.6 8.9 %copy-start.4 = (bf16[256,384]{1,0:T(8,128)(2,1)S(1)}, bf16[256,384]{1,0:T(8,128)(2,1)}, u32[]{:S(2)}) copy-start(bf16[256,384]{1,0:T(8,128)(2,1)} %constant.58.clone.left) | copy-start | bytes 589828
  51.6 8.9 %copy-start.5 = (f32[128,1]{1,0:T(8,128)S(1)}, f32[128,1]{1,0:T(8,128)}, u32[]{:S(2)}) copy-start(f32[128,1]{1,0:T(8,128)} %constant.56.clone.kx2) | copy-start | bytes 1540
  51.6 8.9 %copy-start.6 = (f32[1,256]{1,0:T(1,128)S(1)}, f32[1,256]{1,0:T(1,128)}, u32[]{:S(2)}) copy-start(f32[1,256]{1,0:T(1,128)} %constant.57.clone.ky2) | copy-start | bytes 3076

commit v11 on v10

--- a/solution.py
+++ b/solution.py
@@ -215,8 +215,8 @@
     flow,
     outer_y,
     inner_y,
+    xlo,
     xhi,
-    xlo,
     odd,
     forms,
     update,
@@ -491,8 +491,8 @@
     halos = (
         swap(GY, n_gy, 1)(edges[2]),
         swap(GY, n_gy, 0)(edges[3]),
+        shift(GX, n_gx, 1)(edges[0]),
         shift(GX, n_gx, -1)(edges[1]),
-        shift(GX, n_gx, 1)(edges[0]),
         odd,
     )
 

time: 81.8 us -> 82.6 us (level)
  waiting for transfers between devices: 1.06 us -> 2.5 us
    all_to_all x1, blocking collectives: 23.2 us -> 21.7 us  [shards(): got = lax.all_to_all(spectra, MODES, 0, 0, tiled=True)]
    ppermute x1, waiting for transfers between devices: 1.04 us -> 2.35 us  [shards(): shift(GX, n_gx, -1)(edges[1])]
    ppermute x1, starting transfers between devices: 0.97 us -> 0.01 us  [shards(): shift(GX, n_gx, -1)(edges[1])]
    ppermute x1, starting transfers between devices: 1.21 us -> 2.15 us  [shards(): shift(GX, n_gx, 1)(edges[0])]
    all_to_all x1, blocking collectives: 8.83 us -> 9.68 us  [shards(): lines = lax.all_to_all(lines, 'x', 0, 0, tiled=True)]
  transfers between devices with their start and end apart: 4 -> 4, of which waited for: 1 -> 2; matrix products, arithmetic and copies ran while one was open for 0% -> 0% of each run, Pallas kernels for 1% -> 1%
where the time goes in v11:
time: 82.6 us; the launch traced here: 82.3 us
  blocking collectives  50.4 us (61%)
  starting transfers between devices  17.8 us (22%)
  Pallas kernels  10.8 us (13%)
  waiting for transfers between devices  2.5 us (3%)
    all_to_all x1, blocking collectives, shards(): got = lax.all_to_all(spectra, MODES, 0, 0, tiled=True)  21.7 us
    all_to_all x1, blocking collectives, shards(): got = lax.all_to_all(grads, MODES, 0, 0, tiled=True)  18.9 us
    ppermute x1, starting transfers between devices, shards(): swap(GY, n_gy, 1)(edges[2])  13.7 us
    all_to_all x1, blocking collectives, shards(): lines = lax.all_to_all(lines, 'x', 0, 0, tiled=True)  9.68 us
    pallas_call x1, Pallas kernels, react(): call(react_kernel, [(NSPEC, CX, CY, NZ), (5, CX, CY, NZ), (NZ, 2, 2 * COL...  5.95 us
    ppermute x1, waiting for transfers between devices, shards(): shift(GX, n_gx, -1)(edges[1])  2.35 us
    ppermute x1, starting transfers between devices, shards(): shift(GX, n_gx, 1)(edges[0])  2.15 us
    ppermute x1, starting transfers between devices, shards(): swap(GY, n_gy, 0)(edges[3])  1.92 us
  transfers between devices with their start and end apart: 4, of which 2 were waited for; matrix products, arithmetic and copies ran while one was open for 0% of the time, Pallas kernels for 1%

profile of v11, /device:TPU:1, one launch (start us, length us, event | category | flops | bytes accessed | tf_op | source)
XLA Modules:
  0.0 82.3 jit_solution(17457084639970354363)
XLA Ops:
  0.6 1.3 %shard_map.221 = (f32[14,8,128]{2,1,0:T(8,128)S(1)}, f32[14,8,128]{2,1,0:T(8,128)S(1)}, f32[14,8,128]{2,1,0:T(8,128)S(1)}, f32[14,8,128]{2,1,0:T(8,128)S(1)}, s3...) custom-call(f32[9,8,8,128]{3,2,1,0:T(8,128)} %species.1, ...), custom_call_target="tpu_custom_call" | custom-call | tf_op jit(solution)/shard_map/pallas_call | solution.py:485
  1.9 13.7 %collective-permute-start = (f32[14,8,128]{2,1,0:T(8,128)S(1)}, f32[14,8,128]{2,1,0:T(8,128)S(1)}, u32[]{:S(2)}, u32[]{:S(2)}) collective-permute-start(f32[14,8,128]{2,1,0:T(8,128)S(1)} %get-tuple-element.29), channel_id=1, source_target_pairs={{1,2},{3,4},{5,6},{7,8},{9,10},{11,12},{13,14},{15,16},{17,18},{19... | collective-permute-start | bytes 172040 | tf_op jit(solution)/shard_map/ppermute | solution.py:492
  15.6 1.9 %collective-permute-start.1 = (f32[14,8,128]{2,1,0:T(8,128)S(1)}, f32[14,8,128]{2,1,0:T(8,128)S(1)}, u32[]{:S(2)}, u32[]{:S(2)}) collective-permute-start(f32[14,8,128]{2,1,0:T(8,128)S(1)} %get-tuple-element.30), channel_id=1, source_target_pairs={{0,1},{2,3},{4,5},{6,7},{8,9},{10,11},{12,13},{14,15},{16,17},{18,... | collective-permute-start | bytes 172040 | tf_op jit(solution)/shard_map/ppermute | solution.py:493
  17.6 2.1 %collective-permute-start.2 = (f32[14,8,128]{2,1,0:T(8,128)S(1)}, f32[14,8,128]{2,1,0:T(8,128)S(1)}, u32[]{:S(2)}, u32[]{:S(2)}) collective-permute-start(f32[14,8,128]{2,1,0:T(8,128)S(1)} %get-tuple-element.31), channel_id=1, source_target_pairs={{0,32},{32,64},{64,96},{96,128},{128,160},{160,192},{192,224},{224... | collective-permute-start | bytes 172040 | tf_op jit(solution)/shard_map/ppermute | solution.py:494
  19.7 0.0 collective-permute-start.3
  19.7 1.0 %shard_map.222 = (bf16[160,192]{1,0:T(8,128)(2,1)S(1)}, bf16[64,96]{1,0:T(8,128)(2,1)S(1)}, f32[24,128]{1,0:T(8,128)S(1)}, f32[16,128]{1,0:T(8,128)S(1)}, s32[8,128]{1,0:T(8,128)S(1)}) custom-call(s32[8,8]{1,0:T(8,128)S(1)} %get-tuple-element.33.classes, f32[9,19]{1,0:T(8,128)S(1)} %get-tuple-element.34.left_t, f32[9,19]{1,0:T(8,128)S(1)} %get-tuple-element.35.right_t, ...), custom_call_target="tpu_custom_call" | custom-call | tf_op jit(solution)/shard_map/pallas_call | solution.py:416
  20.7 0.1 add_bitcast_fusion.place
  20.8 0.0 collective-permute-done.outer_y
  20.8 0.0 collective-permute-done.1.inner_y
  20.8 0.2 collective-permute-done.2.xlo
  21.0 2.3 %collective-permute-done.3.xhi = f32[14,8,128]{2,1,0:T(8,128)S(1)} collective-permute-done((f32[14,8,128]{2,1,0:T(8,128)S(1)}, f32[14,8,128]{2,1,0:T(8,128)S(1)}, u32[]{:S(2)}, u32[]{:S(2)}) %collective-permute-start.3) | collective-permute-done | bytes 57376 | tf_op jit(solution)/shard_map/ppermute | solution.py:495
  23.3 0.0 copy-start.2
  23.3 0.0 copy-start.3
  23.3 0.0 copy-start.1
  23.3 5.9 %shard_map.223 = (f32[9,8,8,128]{3,2,1,0:T(8,128)}, f32[5,8,8,128]{3,2,1,0:T(8,128)S(1)}, f32[128,2,128]{2,1,0:T(2,128)S(1)}) custom-call(f32[9,8,8,128]{3,2,1,0:T(8,128)S(1)} %get-tuple-element.27.species, f32[5,8,8,128]{3,2,1,0:T(8,128)S(1)} %get-tuple-element.28.flow, f32[14,8,128]{2,1,0:T(8,128)S(1)} %collective-permute-done.outer_y, ...), custom_call_target="tpu_custom_call" | custom-call | tf_op jit(solution)/shard_map/pallas_call | solution.py:427
  29.3 0.0 copy-start
  29.3 21.7 %all_to_all.15.got = f32[128,2,128]{2,1,0:T(2,128)S(1)} all-to-all(f32[128,2,128]{2,1,0:T(2,128)S(1)} %get-tuple-element.50), channel_id=1, replica_groups=mesh['y'=8,'c'=2,'z'=8,'x'=4] {'y','c','z'}, dimensions={0} | all-to-all | bytes 262144 | tf_op jit(solution)/shard_map/all_to_all | solution.py:526
  51.0 0.0 copy-done.2
  51.0 0.0 copy-done.3
  51.0 0.5 shard_map.224
  51.6 0.0 copy-start.4
  51.6 0.0 copy-start.5
  51.6 0.0 copy-start.6
  51.6 9.7 %all_to_all.16.got = f32[4,128,128]{2,1,0:T(8,128)S(1)} all-to-all(f32[4,128,128]{2,1,0:T(8,128)S(1)} %shard_map.224), channel_id=1, replica_groups=mesh['y'=8,'c'=2,'z'=8,'x'=4] {'x'}, dimensions={0} | all-to-all | bytes 524288 | tf_op jit(solution)/shard_map/all_to_all | solution.py:528
  61.3 0.0 copy-done.1
  61.3 0.0 copy-done
  61.3 0.0 copy-done.4
  61.3 0.0 copy-done.5
  61.3 0.0 copy-done.6
  61.3 1.1 %shard_map.225 = f32[128,2,128]{2,1,0:T(2,128)S(1)} custom-call(s32[1,2]{1,0:T(1,128)S(1)} %add_bitcast_fusion.place, f32[4,128,128]{2,1,0:T(8,128)S(1)} %all_to_all.16.got, bf16[1536,256]{1,0:T(8,128)(2,1)S(1)} %copy-done.1, bf16[4,768,128]{2,1,0:T(8,128)(2,1)S(1)} %copy-done, f32[128,1]{1,0:T(8,128)S(1)} %copy-done.5, f32[1,256]{1,0:T(1,128)S(1)} %copy-done.6, ...), custom_call_target="tpu_custom_call" | custom-call | tf_op jit(solution)/shard_map/pallas_call | solution.py:529
  62.4 18.9 %all_to_all.17.got = f32[128,2,128]{2,1,0:T(2,128)S(1)} all-to-all(f32[128,2,128]{2,1,0:T(2,128)S(1)} %shard_map.225), channel_id=1, replica_groups=mesh['y'=8,'c'=2,'z'=8,'x'=4] {'y','c','z'}, dimensions={0} | all-to-all | bytes 262144 | tf_op jit(solution)/shard_map/all_to_all | solution.py:538
  81.3 1.0 %shard_map.226 = f32[5,8,8,128]{3,2,1,0:T(8,128)} custom-call(f32[128,2,128]{2,1,0:T(2,128)S(1)} %all_to_all.17.got, f32[5,8,8,128]{3,2,1,0:T(8,128)S(1)} %get-tuple-element.51.mid, bf16[2,128,128]{2,1,0:T(8,128)(2,1)S(1)} %copy-done.3, bf16[2,128,128]{2,1,0:T(8,128)(2,1)S(1)} %copy-done.2), custom_call_target="tpu_custom_call" | custom-call | tf_op jit(solution)/shard_map/pallas_call | solution.py:539
Async XLA Ops:
  1.9 18.9 %collective-permute-start = (f32[14,8,128]{2,1,0:T(8,128)S(1)}, f32[14,8,128]{2,1,0:T(8,128)S(1)}, u32[]{:S(2)}, u32[]{:S(2)}) collective-permute-start(f32[14,8,128]{2,1,0:T(8,128)S(1)} %get-tuple-element.29), channel_id=1, source_target_pairs={{1,2},{3,4},{5,6},{7,8},{9,10},{11,12},{13,14},{15,16},{17,18},{19... | collective-permute-start | bytes 172040 | tf_op jit(solution)/shard_map/ppermute | solution.py:492
  15.6 5.2 %collective-permute-start.1 = (f32[14,8,128]{2,1,0:T(8,128)S(1)}, f32[14,8,128]{2,1,0:T(8,128)S(1)}, u32[]{:S(2)}, u32[]{:S(2)}) collective-permute-start(f32[14,8,128]{2,1,0:T(8,128)S(1)} %get-tuple-element.30), channel_id=1, source_target_pairs={{0,1},{2,3},{4,5},{6,7},{8,9},{10,11},{12,13},{14,15},{16,17},{18,... | collective-permute-start | bytes 172040 | tf_op jit(solution)/shard_map/ppermute | solution.py:493
  17.6 3.4 %collective-permute-start.2 = (f32[14,8,128]{2,1,0:T(8,128)S(1)}, f32[14,8,128]{2,1,0:T(8,128)S(1)}, u32[]{:S(2)}, u32[]{:S(2)}) collective-permute-start(f32[14,8,128]{2,1,0:T(8,128)S(1)} %get-tuple-element.31), channel_id=1, source_target_pairs={{0,32},{32,64},{64,96},{96,128},{128,160},{160,192},{192,224},{224... | collective-permute-start | bytes 172040 | tf_op jit(solution)/shard_map/ppermute | solution.py:494
  19.7 3.6 %collective-permute-start.3 = (f32[14,8,128]{2,1,0:T(8,128)S(1)}, f32[14,8,128]{2,1,0:T(8,128)S(1)}, u32[]{:S(2)}, u32[]{:S(2)}) collective-permute-start(f32[14,8,128]{2,1,0:T(8,128)S(1)} %get-tuple-element.32), channel_id=1, source_target_pairs={{0,480},{32,0},{64,32},{96,64},{128,96},{160,128},{192,160},{224,1... | collective-permute-start | bytes 172040 | tf_op jit(solution)/shard_map/ppermute | solution.py:495
  23.3 27.7 %copy-start.2 = (bf16[2,128,128]{2,1,0:T(8,128)(2,1)S(1)}, bf16[2,128,128]{2,1,0:T(8,128)(2,1)}, u32[]{:S(2)}) copy-start(bf16[2,128,128]{2,1,0:T(8,128)(2,1)} %constant.53.clone.dz_far.dx.dz) | copy-start | bytes 196612
  23.3 27.7 %copy-start.3 = (bf16[2,128,128]{2,1,0:T(8,128)(2,1)S(1)}, bf16[2,128,128]{2,1,0:T(8,128)(2,1)}, u32[]{:S(2)}) copy-start(bf16[2,128,128]{2,1,0:T(8,128)(2,1)} %constant.52.clone.fz_far.fx.fz) | copy-start | bytes 196612
  23.3 38.0 %copy-start.1 = (bf16[1536,256]{1,0:T(8,128)(2,1)S(1)}, bf16[1536,256]{1,0:T(8,128)(2,1)}, u32[]{:S(2)}) copy-start(bf16[1536,256]{1,0:T(8,128)(2,1)} %constant.54.clone.forth) | copy-start | bytes 2359300
  29.3 32.0 %copy-start = (bf16[4,768,128]{2,1,0:T(8,128)(2,1)S(1)}, bf16[4,768,128]{2,1,0:T(8,128)(2,1)}, u32[]{:S(2)}) copy-start(bf16[4,768,128]{2,1,0:T(8,128)(2,1)} %constant.55.clone.back) | copy-start | bytes 2359300
  51.6 9.7 %copy-start.4 = (bf16[256,384]{1,0:T(8,128)(2,1)S(1)}, bf16[256,384]{1,0:T(8,128)(2,1)}, u32[]{:S(2)}) copy-start(bf16[256,384]{1,0:T(8,128)(2,1)} %constant.58.clone.left) | copy-start | bytes 589828
  51.6 9.7 %copy-start.5 = (f32[128,1]{1,0:T(8,128)S(1)}, f32[128,1]{1,0:T(8,128)}, u32[]{:S(2)}) copy-start(f32[128,1]{1,0:T(8,128)} %constant.56.clone.kx2) | copy-start | bytes 1540
  51.6 9.7 %copy-start.6 = (f32[1,256]{1,0:T(1,128)S(1)}, f32[1,256]{1,0:T(1,128)}, u32[]{:S(2)}) copy-start(f32[1,256]{1,0:T(1,128)} %constant.57.clone.ky2) | copy-start | bytes 3076
